TPU v7x, 32 devices: a whole 2x2x4 slice. The times are simulated.
32 devices in a mesh: dom: 8 (over z, x), chan: 4 (over y, core).
Axes of the slice: x: 2, y: 2, z: 4, core: 2. Of those that a mesh axis runs over, the one named last changes fastest.
Arguments:
- latent: bfloat16 [512, 16384], P('chan', 'dom'), may hold values from -6 to 6
- edge_weight: bfloat16 [1024, 128, 128], P('dom'), may hold values from -0.125 to 0.125
- send_blocks: int32 [64, 2], P('dom'), may hold values from 0 to 15, as said below
- send_counts: int32 [64], P('dom'), may hold values from 1 to 2, as said below
- edge_src: int32 [1024], P('dom'), may hold values from 0 to 31, as said below
- edge_obs: int32 [1024], P('dom'), may hold values from 0 to 7, as said below
- w_in: bfloat16 [512, 2048], P('chan'), may hold values from -0.25 to 0.25
- bias: float32 [2048], replicated, may hold values from -3 to 3
- w_out: bfloat16 [2048, 128], replicated, may hold values from -0.125 to 0.125
- g_out: bfloat16 [8192, 128], P('dom'), may hold values from -6 to 6
Outputs:
- obs_out: bfloat16 [8192, 128], P('dom')
- d_latent: bfloat16 [512, 16384], P('chan', 'dom')
Inputs may be any that keep to these rules, and one draw needn't show every extreme that they name: `send_counts`: for every sending partition, some receiving partition gets all 2 slots live. `send_blocks`: A mesh block of the sending partition for each slot; entries of slots that are not live are arbitrary. `edge_src`: values below 16 name a mesh block of the partition itself; 16 + p * 2 + s names slot s from partition p to this partition, and only live slots are named. `edge_obs`: every observation block of a partition has at least one edge block.
All inputs are finite; a program needn't handle non-finite values.
Results may differ from a plain program's by a relative error of at most 0.0065.
Values may be sent and summed in bfloat16 or wider, within the bound.
No kernel may reach another device: no remote copies, remote signals or barrier semaphores. Data moves between devices by JAX's collectives and lax.ppermute only.
A program may use at most 64 MiB of HBM per device.

v0:
```python
import jax
import jax.numpy as jnp
from jax import lax
from jax.sharding import PartitionSpec as P


def on_device(
    latent, edge_weight, send_blocks, send_counts, edge_src, edge_obs, w_in, bias, w_out, g_out
):
    highest = lax.Precision.HIGHEST
    dom_count = lax.axis_size("dom")
    chan_count = lax.axis_size("chan")
    feat_width, node_cols = latent.shape
    block_size = edge_weight.shape[1]
    edge_count = edge_weight.shape[0]
    local_count = node_cols // block_size
    capacity = send_blocks.shape[1]
    obs_blocks = g_out.shape[0] // block_size
    obs_rows = obs_blocks * block_size
    hidden_width = w_in.shape[1]
    share_width = hidden_width // chan_count
    blocks = latent.reshape(feat_width, local_count, block_size).transpose(1, 0, 2)
    slot_live = jnp.arange(capacity)[None, :] < send_counts[:, None]
    outgoing = blocks[send_blocks]
    outgoing = jnp.where(slot_live[:, :, None, None], outgoing, jnp.zeros_like(outgoing))
    arrived = lax.all_to_all(outgoing, "dom", split_axis=0, concat_axis=0, tiled=True)
    source_pool = jnp.concatenate(
        [blocks, arrived.reshape(dom_count * capacity, feat_width, block_size)], axis=0
    )
    picked = source_pool[edge_src]
    partial_value = jnp.einsum(
        "edn,eon->edo", picked, edge_weight, preferred_element_type=jnp.float32
    )
    onehot_obs = (edge_obs[:, None] == jnp.arange(obs_blocks)[None, :]).astype(jnp.float32)
    summed = jnp.dot(
        onehot_obs.T, partial_value.reshape(edge_count, feat_width * block_size), precision=highest
    )
    aggregate = summed.reshape(obs_blocks, feat_width, block_size).astype(jnp.bfloat16)
    share_start = lax.axis_index("chan") * share_width
    w_cols = lax.all_to_all(w_in, "chan", split_axis=1, concat_axis=0, tiled=True)
    rows_w = w_cols
    pre_grid = jnp.einsum(
        "dc,bdo->cbo",
        rows_w,
        lax.all_gather(aggregate, "chan", axis=1, tiled=True),
        preferred_element_type=jnp.float32,
    )
    pre_act = (
        pre_grid.reshape(share_width, obs_rows)
        + lax.dynamic_slice_in_dim(bias, share_start, share_width, 0)[:, None]
    )
    hidden = jax.nn.silu(pre_act).astype(jnp.bfloat16)
    out_share = lax.dynamic_slice_in_dim(w_out, share_start, share_width, 0)
    mixed_term = lax.dot_general(
        hidden, out_share, (((0,), (0,)), ((), ())), preferred_element_type=jnp.float32
    )
    obs_out = lax.psum(mixed_term, "chan").astype(jnp.bfloat16)
    back_hidden = lax.dot_general(
        out_share, g_out, (((1,), (1,)), ((), ())), preferred_element_type=jnp.float32
    )
    sigma_pre = jax.nn.sigmoid(pre_act)
    grad_share = (back_hidden * sigma_pre * (1.0 + pre_act * (1.0 - sigma_pre))).astype(
        jnp.bfloat16
    )
    rows_w = w_cols
    grad_feat = lax.psum_scatter(
        jnp.dot(rows_w, grad_share, preferred_element_type=jnp.float32),
        "chan",
        scatter_dimension=0,
        tiled=True,
    )
    grad_agg = (
        grad_feat.reshape(feat_width, obs_blocks, block_size)
        .transpose(1, 0, 2)
        .astype(jnp.bfloat16)
    )
    grad_rows = grad_agg[edge_obs]
    grad_picked = jnp.einsum(
        "edo,eon->edn", grad_rows, edge_weight, preferred_element_type=jnp.float32
    )
    pool_count = local_count + dom_count * capacity
    onehot_src = (edge_src[:, None] == jnp.arange(pool_count)[None, :]).astype(jnp.float32)
    pool_grad = jnp.dot(
        onehot_src.T, grad_picked.reshape(edge_count, feat_width * block_size), precision=highest
    )
    local_grad = pool_grad[:local_count]
    slot_grad = (
        pool_grad[local_count:]
        .reshape(dom_count, capacity, feat_width, block_size)
        .astype(jnp.bfloat16)
    )
    returned = lax.all_to_all(slot_grad, "dom", split_axis=0, concat_axis=0, tiled=True)
    returned = jnp.where(slot_live[:, :, None, None], returned, jnp.zeros_like(returned))
    onehot_send = (
        send_blocks.reshape(dom_count * capacity)[:, None] == jnp.arange(local_count)[None, :]
    ).astype(jnp.float32)
    back_blocks = jnp.dot(
        onehot_send.T,
        returned.reshape(dom_count * capacity, feat_width * block_size).astype(jnp.float32),
        precision=highest,
    )
    grad_nodes = local_grad + back_blocks
    d_latent = (
        grad_nodes.reshape(local_count, feat_width, block_size)
        .transpose(1, 0, 2)
        .reshape(feat_width, node_cols)
        .astype(jnp.bfloat16)
    )
    return (obs_out, d_latent)


def solution(mesh):
    return jax.shard_map(
        on_device,
        mesh=mesh,
        in_specs=(
            P("chan", "dom"),
            P("dom", None, None),
            P("dom", None),
            P("dom"),
            P("dom"),
            P("dom"),
            P("chan", None),
            P(),
            P(),
            P("dom", None),
        ),
        out_specs=(P("dom", None), P("chan", "dom")),
        check_vma=False,
    )
```

profile of v0, /device:TPU:0, one launch (start us, length us, event | category | flops | bytes accessed | tf_op | source)
XLA Modules:
  0.0 180.3 jit_solution(810662629588188137)
XLA Ops:
  7.2 1.4 copy.33
  8.6 0.3 copy.34
  8.9 0.7 compare_select_fusion
  9.7 0.7 iota_compare_fusion.4
  10.4 0.6 gather_fusion
  11.1 0.9 broadcast_select_fusion.1
  12.0 7.3 %all-to-all-start = ((bf16[8,2,128,128]{3,2,1,0:T(8,128)(2,1)}), bf16[8,2,128,128]{3,2,1,0:T(8,128)(2,1)S(1)}, u32[]{:S(2)}, u32[]{:S(2)}) async-start(bf16[8,2,128,128]{3,2,1,0:T(8,128)(2,1)} %broadcast_select_fusion.1), calls=%async_computation | async-start | bytes 1048576 | tf_op jit(solution)/shard_map/all_to_all | solution.py:26
  19.3 14.4 %all-to-all-done = bf16[8,2,128,128]{3,2,1,0:T(8,128)(2,1)S(1)} async-done(((bf16[8,2,128,128]{3,2,1,0:T(8,128)(2,1)}), bf16[8,2,128,128]{3,2,1,0:T(8,128)(2,1)S(1)}, u32[]{:S(2)}, u32[]{:S(2)}) %all-to-all-start) | async-done | bytes 524320 | tf_op jit(solution)/shard_map/all_to_all | solution.py:26
  33.8 3.0 %gather_fusion.1 = bf16[128,128,128]{2,1,0:T(8,128)(2,1)} fusion(bf16[32,128,128]{2,1,0:T(8,128)(2,1)S(1)} %pad_maximum_fusion, s32[1024]{0:T(1024)S(1)} %pad_clamp_fusion.1), kind=kCustom, calls=%fused_computation.1 | custom fusion | bytes 8389120 | tf_op jit(solution)/shard_map/gather | solution.py:30
  36.9 6.5 %fusion.26 = f32[128,128,128]{2,1,0:T(8,128)S(1)} fusion(bf16[128,128,128]{2,1,0:T(8,128)(2,1)} %gather_fusion.1, bf16[128,128,128]{2,1,0:T(8,128)(2,1)} %param.11), kind=kOutput, calls=%fused_computation.49 | convolution fusion | flops 536870912 | bytes 16777216 | tf_op jit(solution)/shard_map/edn,eon->edo/dot_general | solution.py:31
  43.4 9.8 %copy.63 = f32[16,8,128,128]{3,1,2,0:T(8,128)} copy(f32[16,8,128,128]{3,2,1,0:T(8,128)S(1)} %bitcast.62) | data formatting | bytes 16777216
  53.1 9.0 %copy.36 = f32[16384,128]{1,0:T(8,128)} copy(f32[16384,128]{0,1:T(8,128)} %bitcast.63) | data formatting | bytes 16777216 | tf_op jit(solution)/shard_map/dot_general | solution.py:35
  62.1 7.9 %convolution_convert_fusion = bf16[8,128,128]{2,0,1:T(8,128)(2,1)} fusion(f32[128,128,128]{2,1,0:T(8,128)} %bitcast.64, s32[128]{0:T(128)S(1)} %copy-done.3), kind=kOutput, calls=%fused_computation.14 | convolution fusion | flops 201458688 | bytes 8651264 | tf_op jit(solution)/shard_map/dot_general | solution.py:35
  70.0 0.8 copy.65
  70.9 3.5 %all-to-all-start.1 = ((bf16[128,4,512]{2,0,1:T(8,128)(2,1)}), bf16[128,4,512]{2,0,1:T(8,128)(2,1)S(1)}, u32[]{:S(2)}, u32[]{:S(2)}) async-start(bf16[128,4,512]{2,0,1:T(8,128)(2,1)} %bitcast.60), calls=%async_computation.1 | async-start | bytes 1048576 | tf_op jit(solution)/shard_map/all_to_all | solution.py:40
  74.4 0.8 dynamic_slice.6
  75.2 12.8 %all-to-all-done.1 = bf16[128,4,512]{2,0,1:T(8,128)(2,1)S(1)} async-done(((bf16[128,4,512]{2,0,1:T(8,128)(2,1)}), bf16[128,4,512]{2,0,1:T(8,128)(2,1)S(1)}, u32[]{:S(2)}, u32[]{:S(2)}) %all-to-all-start.1) | async-done | bytes 524320 | tf_op jit(solution)/shard_map/all_to_all | solution.py:40
  88.0 2.3 %all-gather.2.cloned.1.call-done = bf16[8,512,128]{2,0,1:T(8,128)(2,1)} async-done(((bf16[8,128,128]{2,0,1:T(8,128)(2,1)}), bf16[8,512,128]{2,0,1:T(8,128)(2,1)}) %all-gather.2.cloned.1.call-update) | async-done | bytes 1048592 | tf_op jit(solution)/shard_map/all_gather | solution.py:45
  90.3 2.0 %fusion.5 = f32[8,128,512]{2,1,0:T(8,128)S(1)} fusion(bf16[512,512,1]{1,0,2:T(8,128)(2,1)S(1)} %bitcast.70, bf16[8,512,128]{2,0,1:T(8,128)(2,1)} %all-gather.2.cloned.1.call-done), kind=kOutput, calls=%fused_computation.17 | convolution fusion | flops 536870912 | bytes 3670016 | tf_op jit(solution)/shard_map/dc,bdo->cbo/dot_general | solution.py:42
  92.2 1.8 %copy.39 = f32[512,1024]{1,0:T(8,128)} copy(f32[512,1024]{0,1:T(8,128)S(1)} %bitcast.66) | data formatting | bytes 4194304 | tf_op jit(solution)/shard_map/reshape | solution.py:49
  94.1 4.2 %convolution_bitcast_fusion = f32[512,1024]{0,1:T(8,128)} fusion(bf16[512,512]{1,0:T(8,128)(2,1)S(1)} %bitcast.71, f32[512,1024]{1,0:T(8,128)} %copy.39, bf16[1024,128]{1,0:T(8,128)(2,1)S(1)} %copy-done.5, f32[512]{0:T(512)S(1)} %dynamic_slice.6, bf16[2048,128]{1,0:T(8,128)(2,1)S(1)} %copy-done, s32[]{:T(128)S(6)} %select_n.23), kind=kOutput, calls=%fused_computation.12 | convolution fusion | flops 676331520 | bytes 5113860 | tf_op jit(solution)/shard_map/dot_general | solution.py:67
  98.5 29.5 %reduce-scatter.2.cloned.1.call-done = f32[128,1024]{0,1:T(8,128)} async-done(((f32[512,1024]{0,1:T(8,128)}), f32[128,1024]{0,1:T(8,128)}) %reduce-scatter.2.cloned.1.call-update) | async-done | bytes 524304 | tf_op jit(solution)/shard_map/reduce_scatter | solution.py:66
  128.0 1.1 convert_element_type.45
  129.3 3.0 %gather_fusion.2 = bf16[128,128,128]{2,1,0:T(8,128)(2,1)} fusion(bf16[8,128,128]{2,1,0:T(8,128)(2,1)S(1)} %bitcast.61, s32[1024]{0:T(1024)S(1)} %pad_clamp_fusion), kind=kCustom, calls=%fused_computation.2 | custom fusion | bytes 8389120 | tf_op jit(solution)/shard_map/gather | solution.py:77
  132.3 4.7 %fusion.27 = f32[128,128,128]{2,1,0:T(8,128)S(1)} fusion(bf16[128,128,128]{2,1,0:T(8,128)(2,1)} %gather_fusion.2, bf16[128,128,128]{2,1,0:T(8,128)(2,1)} %param.11), kind=kOutput, calls=%fused_computation.50 | convolution fusion | flops 536870912 | bytes 16777216 | tf_op jit(solution)/shard_map/edo,eon->edn/dot_general | solution.py:78
  137.0 7.9 %fusion.1 = f32[32,16384]{1,0:T(8,128)S(1)} fusion(f32[16,8,128,128]{3,2,1,0:T(8,128)S(1)} %bitcast.65, s32[128]{0:T(128)S(1)} %copy-done.4), kind=kOutput, calls=%fused_computation.5 | convolution fusion | flops 805310464 | bytes 10486272 | tf_op jit(solution)/shard_map/dot_general | solution.py:83
  145.0 0.9 copy.47
  145.9 5.5 %all-to-all-start.2 = ((bf16[8,2,128,128]{3,2,1,0:T(8,128)(2,1)}), bf16[8,2,128,128]{3,2,1,0:T(8,128)(2,1)S(1)}, u32[]{:S(2)}, u32[]{:S(2)}) async-start(bf16[8,2,128,128]{3,2,1,0:T(8,128)(2,1)} %bitcast.73), calls=%async_computation.3 | async-start | bytes 1048576 | tf_op jit(solution)/shard_map/all_to_all | solution.py:92
  151.4 3.2 %fusion.9 = f32[1024,128]{1,0:T(8,128)} fusion(f32[512,1024]{1,0:T(8,128)} %copy.39, f32[512]{0:T(512)S(1)} %dynamic_slice.6, bf16[2048,128]{1,0:T(8,128)(2,1)S(1)} %copy-done, s32[]{:T(128)S(6)} %select_n.23), kind=kOutput, calls=%fused_computation.21 | convolution fusion | flops 137363456 | bytes 2754564 | tf_op jit(solution)/shard_map/dot_general | solution.py:54
  154.6 17.2 %all-reduce.1 = bf16[1024,128]{1,0:T(8,128)(2,1)} all-reduce(f32[1024,128]{1,0:T(8,128)} %fusion.9), channel_id=1, replica_groups=mesh['dom'=8,'chan'=4] {'chan'}, use_global_device_ids=true, to_apply=%region_0.1 | all-reduce | flops 131072 | bytes 786432 | tf_op jit(solution)/shard_map/psum | solution.py:57
  172.0 0.5 fusion.4
  172.6 0.9 copy.64
  (31 shorter events, 1.0 us)
Async XLA Ops:
  7.2 86.9 %copy-start = (bf16[2048,128]{1,0:T(8,128)(2,1)S(1)}, bf16[2048,128]{1,0:T(8,128)(2,1)}, u32[]{:S(2)}) copy-start(bf16[2048,128]{1,0:T(8,128)(2,1)} %param.18) | copy-start | bytes 1572868
  7.2 12.1 %copy-start.4 = (s32[128]{0:T(128)S(1)}, s32[128]{0:T(128)}, u32[]{:S(2)}) copy-start(s32[128]{0:T(128)} %param.14) | copy-start | bytes 1540
  12.0 21.7 %all-to-all-start = ((bf16[8,2,128,128]{3,2,1,0:T(8,128)(2,1)}), bf16[8,2,128,128]{3,2,1,0:T(8,128)(2,1)S(1)}, u32[]{:S(2)}, u32[]{:S(2)}) async-start(bf16[8,2,128,128]{3,2,1,0:T(8,128)(2,1)} %broadcast_select_fusion.1), calls=%async_computation | async-start | bytes 1048576 | tf_op jit(solution)/shard_map/all_to_all | solution.py:26
  19.3 71.0 %all-gather.2.cloned.1.call-start = ((), (), s32[]{:S(2)}) async-start(), calls=%async_computation.4 | async-start | bytes 1310720 | tf_op jit(solution)/shard_map/all_gather | solution.py:45
  53.1 9.0 %copy-start.3 = (s32[128]{0:T(128)S(1)}, s32[128]{0:T(128)}, u32[]{:S(2)}) copy-start(s32[128]{0:T(128)} %param.15) | copy-start | bytes 1540
  62.1 7.9 %copy-start.1 = (bf16[128,2048]{1,0:T(8,128)(2,1)S(1)}, bf16[128,2048]{1,0:T(8,128)(2,1)}, u32[]{:S(2)}) copy-start(bf16[128,2048]{1,0:T(8,128)(2,1)} %param.16) | copy-start | bytes 1572868
  70.9 17.1 %all-to-all-start.1 = ((bf16[128,4,512]{2,0,1:T(8,128)(2,1)}), bf16[128,4,512]{2,0,1:T(8,128)(2,1)S(1)}, u32[]{:S(2)}, u32[]{:S(2)}) async-start(bf16[128,4,512]{2,0,1:T(8,128)(2,1)} %bitcast.60), calls=%async_computation.1 | async-start | bytes 1048576 | tf_op jit(solution)/shard_map/all_to_all | solution.py:40
  74.4 19.7 %copy-start.5 = (bf16[1024,128]{1,0:T(8,128)(2,1)S(1)}, bf16[1024,128]{1,0:T(8,128)(2,1)}, u32[]{:S(2)}) copy-start(bf16[1024,128]{1,0:T(8,128)(2,1)} %param.19) | copy-start | bytes 786436
  74.4 53.6 %reduce-scatter.2.cloned.1.call-start = ((), (), s32[]{:S(2)}) async-start(), calls=%async_computation.5 | async-start | bytes 2621440 | tf_op jit(solution)/shard_map/reduce_scatter | solution.py:66
  94.1 4.2 %copy-start.2 = (s32[8,2]{0,1:T(2,128)S(1)}, s32[8,2]{0,1:T(2,128)}, u32[]{:S(2)}) copy-start(s32[8,2]{0,1:T(2,128)} %param.12) | copy-start | bytes 196
  145.9 26.0 %all-to-all-start.2 = ((bf16[8,2,128,128]{3,2,1,0:T(8,128)(2,1)}), bf16[8,2,128,128]{3,2,1,0:T(8,128)(2,1)S(1)}, u32[]{:S(2)}, u32[]{:S(2)}) async-start(bf16[8,2,128,128]{3,2,1,0:T(8,128)(2,1)} %bitcast.73), calls=%async_computation.3 | async-start | bytes 1048576 | tf_op jit(solution)/shard_map/all_to_all | solution.py:92
Sparse Core Ops, SparseCore 0:
  70.2 20.0 all-gather.1
  98.4 29.5 reduce-scatter.1
where the time goes:
time: 181 us; the launch traced here: 180 us
  waiting for transfers between devices  59 us (33%)
  matrix products  36.9 us (20%)
  local copies, waits for them, and re-layouts  33.1 us (18%)
  blocking collectives  17.2 us (10%)
  starting transfers between devices  16.3 us (9%)
  between operations  14.2 us (8%)
  other arithmetic  3.61 us (2%)
    reduce_scatter x1, waiting for transfers between devices, on_device(): lax.psum_scatter(jnp.dot(rows_w, grad_share, preferred_element_type=jnp.f...  29.5 us
    psum x1, blocking collectives, on_device(): obs_out = lax.psum(mixed_term, 'chan').astype(jnp.bfloat16)  17.2 us
    all_to_all x1, waiting for transfers between devices, on_device(): lax.all_to_all(outgoing, 'dom', split_axis=0, concat_axis=0, tiled=True)  14.4 us
    all_to_all x1, waiting for transfers between devices, on_device(): lax.all_to_all(w_in, 'chan', split_axis=1, concat_axis=0, tiled=True)  12.8 us
    unnamed x18, local copies, waits for them, and re-layouts  12.3 us
    dot_general x1, local copies, waits for them, and re-layouts, on_device(): jnp.dot(onehot_obs.T, partial_value.reshape(edge_count, feat_width * bloc...  8.97 us
    dot_general x1, matrix products, on_device(): jnp.dot(onehot_obs.T, partial_value.reshape(edge_count, feat_width * bloc...  7.91 us
    dot_general x1, matrix products, on_device(): jnp.dot(onehot_src.T, grad_picked.reshape(edge_count, feat_width * block_...  7.88 us
  transfers between devices with their start and end apart: 5, of which 4 were waited for; matrix products, arithmetic and copies ran while one was open for 3% of the time, Pallas kernels for 0%

commit v1 on v0

v1 whole, which is shorter than its diff:
```python
import functools

import jax
import jax.numpy as jnp
from jax import lax
from jax.experimental import pallas as pl
from jax.experimental.pallas import tpu as pltpu
from jax.sharding import PartitionSpec as P

F32 = jnp.float32
BF16 = jnp.bfloat16
UNROLL = 8
NT = (((1,), (1,)), ((), ()))
NN = (((1,), (0,)), ((), ()))


def target(index, shift, count):
    if count & (count - 1) == 0:
        return index ^ shift
    return (index + shift) % count


def source(index, shift, count):
    if count & (count - 1) == 0:
        return index ^ shift
    return (index + count - shift) % count


def send(value, axis, shift, count):
    return lax.ppermute(value, axis, [(i, target(i, shift, count)) for i in range(count)])


def send_back(value, axis, shift, count):
    return lax.ppermute(value, axis, [(target(i, shift, count), i) for i in range(count)])


def vmem(count):
    return [pl.BlockSpec(memory_space=pltpu.VMEM)] * count


def smem(count):
    return [pl.BlockSpec(memory_space=pltpu.SMEM)] * count


def params():
    return pltpu.CompilerParams(vmem_limit_bytes=48 * 1024 * 1024)


def pack_kernel(dom, cap, blk, nodes, blocks_ref, counts_ref, latent_ref, *outs):
    me = lax.axis_index("dom")
    for d in range(dom):
        q = target(me, d, dom)
        for s in range(cap):
            block = jnp.clip(blocks_ref[q, s], 0, nodes - 1)
            start = pl.multiple_of(block * blk, blk)
            live = s < counts_ref[q]

            @pl.when(live)
            def _():
                outs[d][s] = latent_ref[:, pl.ds(start, blk)]

            @pl.when(jnp.logical_not(live))
            def _():
                outs[d][s] = jnp.zeros_like(outs[d][s])


def edge_loop(first, last, body):
    def step(t, carry):
        for u in range(UNROLL):
            i = first + t * UNROLL + u
            body(i, i < last)
        return carry

    lax.fori_loop(0, (last - first + UNROLL - 1) // UNROLL, step, 0)


def local_forward_kernel(
    edges, blk, nodes, obs, src_ref, obs_ref, latent_ref, weight_ref, sum_ref, order_ref, split_ref, total
):
    def sort(e, at):
        near, far = at
        is_near = src_ref[e] < nodes
        order_ref[jnp.where(is_near, near, far)] = e
        step = is_near.astype(jnp.int32)
        return near + step, far - (1 - step)

    near, _ = lax.fori_loop(0, edges, sort, (jnp.int32(0), jnp.int32(edges - 1)), unroll=8)
    split_ref[0] = near
    total[...] = jnp.zeros_like(total)

    def body(i, valid):
        e = order_ref[jnp.minimum(i, edges - 1)]
        start = pl.multiple_of(jnp.minimum(src_ref[e], nodes - 1) * blk, blk)
        term = lax.dot_general(
            weight_ref[e], latent_ref[:, pl.ds(start, blk)], NT, preferred_element_type=F32
        )
        at = jnp.where(valid, obs_ref[e], obs)
        total[at] += term

    edge_loop(0, near, body)
    sum_ref[...] = total[:obs]


def slot_forward_kernel(
    edges, dom, chan, cap, nodes, obs, src_ref, obs_ref, order_ref, split_ref, sum_ref, weight_ref, *rest
):
    arrived, outs, (pool, total) = rest[:dom], rest[dom : dom + chan], rest[dom + chan :]
    me = lax.axis_index("dom")
    for d in range(dom):
        pool[pl.ds(source(me, d, dom) * cap, cap)] = arrived[d][...]
    total[:obs] = sum_ref[...]

    def body(i, valid):
        e = order_ref[jnp.minimum(i, edges - 1)]
        slot = jnp.maximum(src_ref[e] - nodes, 0)
        term = lax.dot_general(weight_ref[e], pool[slot], NT, preferred_element_type=F32)
        at = jnp.where(valid, obs_ref[e], obs)
        total[at] += term

    edge_loop(split_ref[0], edges, body)
    whole = total.reshape((obs + 1) * total.shape[1], total.shape[2])
    rows = outs[0].shape[0]
    mine = lax.axis_index("chan")
    for d in range(chan):
        start = pl.multiple_of(target(mine, d, chan) * rows, rows)
        outs[d][...] = whole[pl.ds(start, rows), :].astype(BF16)


def mlp_kernel(chan, tile, bias_ref, w_out_ref, g_ref, *rest):
    shares, weights = rest[:chan], rest[chan : 2 * chan]
    obs_ref, outs, (full_w, full_a, grad) = (
        rest[2 * chan],
        rest[2 * chan + 1 : 3 * chan + 1],
        rest[3 * chan + 1 :],
    )
    rows, feat = shares[0].shape
    hidden_width = grad.shape[1]
    for d in range(chan):
        full_w[d * feat : (d + 1) * feat, :] = weights[d][...]
        full_a[:, d * feat : (d + 1) * feat] = shares[d][...]
    mine = lax.axis_index("chan")
    g = g_ref[pl.ds(pl.multiple_of(mine * rows, rows), rows), :]
    out = jnp.zeros(obs_ref.shape, F32)
    for h in range(0, hidden_width, tile):
        cols = slice(h, h + tile)
        pre = lax.dot_general(full_a[...], full_w[:, cols], NN, preferred_element_type=F32)
        pre = pre + bias_ref[:, cols]
        sig = 0.5 * jnp.tanh(0.5 * pre) + 0.5
        hidden = (pre * sig).astype(BF16)
        w_out = w_out_ref[cols, :]
        out += lax.dot_general(hidden, w_out, NN, preferred_element_type=F32)
        back = lax.dot_general(g, w_out, NT, preferred_element_type=F32)
        grad[:, cols] = (back * sig * (1.0 + pre * (1.0 - sig))).astype(BF16)
    obs_ref[...] = out.astype(BF16)
    grad_agg = lax.dot_general(full_w[...], grad[...], NT, preferred_element_type=F32)
    for d in range(chan):
        outs[d][...] = grad_agg[d * feat : (d + 1) * feat].astype(BF16)


def gather_grad(chan, per, blk, shares, rows_grad):
    mine = lax.axis_index("chan")
    rows = shares[0].shape[1]
    for d in range(chan):
        start = target(mine, d, chan)
        if rows >= blk:
            for k in range(per):
                rows_grad[start * per + k] = shares[d][:, k * blk : (k + 1) * blk]
        else:
            split = blk // rows
            for k in range(split):

                @pl.when(start % split == k)
                def _():
                    rows_grad[start // split, :, k * rows : (k + 1) * rows] = shares[d][...]


def slot_backward_kernel(
    edges, dom, chan, cap, blk, nodes, obs, src_ref, obs_ref, order_ref, split_ref, weight_ref, *rest
):
    shares, outs, (rows_grad, total) = rest[:chan], rest[chan : chan + dom], rest[chan + dom :]
    gather_grad(chan, max(1, obs // chan), blk, shares, rows_grad)
    total[...] = jnp.zeros_like(total)

    def body(i, valid):
        e = order_ref[jnp.minimum(i, edges - 1)]
        term = lax.dot_general(rows_grad[obs_ref[e]], weight_ref[e], NN, preferred_element_type=F32)
        at = jnp.where(valid, jnp.maximum(src_ref[e] - nodes, 0), dom * cap)
        total[at] += term

    edge_loop(split_ref[0], edges, body)
    me = lax.axis_index("dom")
    for d in range(dom):
        outs[d][...] = total[pl.ds(source(me, d, dom) * cap, cap)].astype(BF16)


def local_backward_kernel(
    edges, chan, blk, nodes, obs, src_ref, obs_ref, order_ref, split_ref, weight_ref, *rest
):
    shares, (out_ref, rows_grad, total) = rest[:chan], rest[chan:]
    gather_grad(chan, max(1, obs // chan), blk, shares, rows_grad)
    total[...] = jnp.zeros_like(total)

    def body(i, valid):
        e = order_ref[jnp.minimum(i, edges - 1)]
        term = lax.dot_general(rows_grad[obs_ref[e]], weight_ref[e], NN, preferred_element_type=F32)
        at = jnp.where(valid, jnp.minimum(src_ref[e], nodes - 1), nodes)
        total[at] += term

    edge_loop(0, split_ref[0], body)
    out_ref[...] = total[:nodes]


def final_kernel(dom, chan, cap, blk, nodes, blocks_ref, counts_ref, local_ref, *rest):
    returned, rows_in = rest[:dom], rest[dom : dom + chan]
    grad_ref, obs_ref, total = rest[dom + chan :]
    me = lax.axis_index("dom")
    total[...] = local_ref[...]
    for d in range(dom):
        q = target(me, d, dom)
        for s in range(cap):

            @pl.when(s < counts_ref[q])
            def _():
                total[jnp.clip(blocks_ref[q, s], 0, nodes - 1)] += returned[d][s].astype(F32)

    for k in range(nodes):
        grad_ref[:, k * blk : (k + 1) * blk] = total[k].astype(BF16)
    mine = lax.axis_index("chan")
    rows = rows_in[0].shape[0]
    for d in range(chan):
        start = pl.multiple_of(source(mine, d, chan) * rows, rows)
        obs_ref[pl.ds(start, rows), :] = rows_in[d][...]


def gather_weights(w_in, chan):
    if chan & (chan - 1):
        return [w_in] + [send(w_in, "chan", d, chan) for d in range(1, chan)]
    weights = {0: w_in}
    bit = chan // 2
    while bit:
        for d in sorted(weights):
            weights[d | bit] = send(weights[d], "chan", bit, chan)
        bit //= 2
    return [weights[d] for d in range(chan)]


def on_device(
    latent, edge_weight, send_blocks, send_counts, edge_src, edge_obs, w_in, bias, w_out, g_out
):
    dom = lax.axis_size("dom")
    chan = lax.axis_size("chan")
    feat, cols = latent.shape
    edges, blk, _ = edge_weight.shape
    nodes = cols // blk
    cap = send_blocks.shape[1]
    obs_rows, out_width = g_out.shape
    obs = obs_rows // blk
    rows = obs_rows // chan
    hidden_width = w_in.shape[1]
    shape = jax.ShapeDtypeStruct

    outgoing = pl.pallas_call(
        functools.partial(pack_kernel, dom, cap, blk, nodes),
        out_shape=[shape((cap, feat, blk), BF16)] * dom,
        in_specs=smem(2) + vmem(1),
        out_specs=vmem(dom),
        compiler_params=params(),
        name="pack",
    )(send_blocks, send_counts, latent)
    arrived = [outgoing[0]] + [send(outgoing[d], "dom", d, dom) for d in range(1, dom)]
    weights = gather_weights(w_in, chan)

    local_sum, order, split = pl.pallas_call(
        functools.partial(local_forward_kernel, edges, blk, nodes, obs),
        out_shape=[
            shape((obs, blk, feat), F32),
            shape((edges,), jnp.int32),
            shape((1,), jnp.int32),
        ],
        in_specs=smem(2) + vmem(2),
        out_specs=vmem(1) + smem(2),
        scratch_shapes=[pltpu.VMEM((obs + 1, blk, feat), F32)],
        compiler_params=params(),
        name="local_forward",
    )(edge_src, edge_obs, latent, edge_weight)

    shares = pl.pallas_call(
        functools.partial(slot_forward_kernel, edges, dom, chan, cap, nodes, obs),
        out_shape=[shape((rows, feat), BF16)] * chan,
        in_specs=smem(4) + vmem(2 + dom),
        out_specs=vmem(chan),
        scratch_shapes=[
            pltpu.VMEM((dom * cap, feat, blk), BF16),
            pltpu.VMEM((obs + 1, blk, feat), F32),
        ],
        compiler_params=params(),
        name="slot_forward",
    )(edge_src, edge_obs, order, split, local_sum, edge_weight, *arrived)
    shares = [shares[0]] + [send(shares[d], "chan", d, chan) for d in range(1, chan)]

    mlp = pl.pallas_call(
        functools.partial(mlp_kernel, chan, min(512, hidden_width)),
        out_shape=[shape((rows, out_width), BF16)] + [shape((feat, rows), BF16)] * chan,
        in_specs=vmem(3 + 2 * chan),
        out_specs=vmem(1 + chan),
        scratch_shapes=[
            pltpu.VMEM((chan * feat, hidden_width), BF16),
            pltpu.VMEM((rows, chan * feat), BF16),
            pltpu.VMEM((rows, hidden_width), BF16),
        ],
        compiler_params=params(),
        name="mlp",
    )(bias.reshape(1, hidden_width), w_out, g_out, *shares, *weights)
    obs_part, grads = mlp[0], mlp[1:]
    grads = [grads[0]] + [send_back(grads[d], "chan", d, chan) for d in range(1, chan)]
    obs_parts = [obs_part] + [send(obs_part, "chan", d, chan) for d in range(1, chan)]

    slot_grads = pl.pallas_call(
        functools.partial(slot_backward_kernel, edges, dom, chan, cap, blk, nodes, obs),
        out_shape=[shape((cap, feat, blk), BF16)] * dom,
        in_specs=smem(4) + vmem(1 + chan),
        out_specs=vmem(dom),
        scratch_shapes=[
            pltpu.VMEM((obs, feat, blk), BF16),
            pltpu.VMEM((dom * cap + 1, feat, blk), F32),
        ],
        compiler_params=params(),
        name="slot_backward",
    )(edge_src, edge_obs, order, split, edge_weight, *grads)
    returned = [slot_grads[0]] + [
        send_back(slot_grads[d], "dom", d, dom) for d in range(1, dom)
    ]

    local_grad = pl.pallas_call(
        functools.partial(local_backward_kernel, edges, chan, blk, nodes, obs),
        out_shape=shape((nodes, feat, blk), F32),
        in_specs=smem(4) + vmem(1 + chan),
        out_specs=pl.BlockSpec(memory_space=pltpu.VMEM),
        scratch_shapes=[
            pltpu.VMEM((obs, feat, blk), BF16),
            pltpu.VMEM((nodes + 1, feat, blk), F32),
        ],
        compiler_params=params(),
        name="local_backward",
    )(edge_src, edge_obs, order, split, edge_weight, *grads)

    d_latent, obs_out = pl.pallas_call(
        functools.partial(final_kernel, dom, chan, cap, blk, nodes),
        out_shape=[shape((feat, cols), BF16), shape((obs_rows, out_width), BF16)],
        in_specs=smem(2) + vmem(1 + dom + chan),
        out_specs=vmem(2),
        scratch_shapes=[pltpu.VMEM((nodes, feat, blk), F32)],
        compiler_params=params(),
        name="final",
    )(send_blocks, send_counts, local_grad, *returned, *obs_parts)
    return obs_out, d_latent


def solution(mesh):
    return jax.shard_map(
        on_device,
        mesh=mesh,
        in_specs=(
            P("chan", "dom"),
            P("dom", None, None),
            P("dom", None),
            P("dom"),
            P("dom"),
            P("dom"),
            P("chan", None),
            P(),
            P(),
            P("dom", None),
        ),
        out_specs=(P("dom", None), P("chan", "dom")),
        check_vma=False,
    )
```

time: 181 us -> 85.8 us (0.47)
  waiting for transfers between devices: 59 us -> 20.1 us
  matrix products: 36.9 us -> 0 us
  local copies, waits for them, and re-layouts: 33.1 us -> 7.02 us
  starting transfers between devices: 16.3 us -> 36.7 us
  Pallas kernels: 0 us -> 20.2 us
  blocking collectives: 17.2 us -> 0 us
  between operations: 14.2 us -> 0.83 us
  other arithmetic: 3.61 us -> 0 us
    dot_general x8 -> x0, matrix products: 36.9 us -> none  [the longest x1 7.91 us: on_device(): jnp.dot(onehot_obs.T, partial_value.reshape(edge_count, feat_width * bloc...]
    ppermute x0 -> x26, starting transfers between devices: none -> 36.7 us  [the longest x16 23.5 us: send(): lax.ppermute(value, axis, [(i, target(i, shift, count)) for i in range(co...]
    reduce_scatter x1 -> x0, waiting for transfers between devices: 29.5 us -> none  [on_device(): lax.psum_scatter(jnp.dot(rows_w, grad_share, preferred_element_type=jnp.f...]
    all_to_all x3 -> x0, waiting for transfers between devices: 27.2 us -> none  [the longest x1 14.4 us: on_device(): lax.all_to_all(outgoing, 'dom', split_axis=0, concat_axis=0, tiled=True)]
    pallas_call x0 -> x7, Pallas kernels: none -> 20.2 us  [the longest x1 4.83 us: on_device(): pl.pallas_call(functools.partial(slot_forward_kernel, edges, dom, chan, c...]
    ppermute x0 -> x26, waiting for transfers between devices: none -> 20.1 us  [the longest x16 16.9 us: send(): lax.ppermute(value, axis, [(i, target(i, shift, count)) for i in range(co...]
    psum x1 -> x0, blocking collectives: 17.2 us -> none  [on_device(): obs_out = lax.psum(mixed_term, 'chan').astype(jnp.bfloat16)]
    all_to_all x3 -> x0, starting transfers between devices: 16.2 us -> none  [the longest x1 7.25 us: on_device(): lax.all_to_all(outgoing, 'dom', split_axis=0, concat_axis=0, tiled=True)]
  transfers between devices with their start and end apart: 5 -> 26, of which waited for: 4 -> 7; matrix products, arithmetic and copies ran while one was open for 3% -> 1% of each run, Pallas kernels for 0% -> 19%
where the time goes in v1:
time: 85.8 us; the launch traced here: 84.8 us
  starting transfers between devices  36.7 us (43%)
  Pallas kernels  20.2 us (24%)
  waiting for transfers between devices  20.1 us (23%)
  local copies, waits for them, and re-layouts  7.02 us (8%)
    ppermute x16, starting transfers between devices, send(): lax.ppermute(value, axis, [(i, target(i, shift, count)) for i in range(co...  23.5 us
    ppermute x16, waiting for transfers between devices, send(): lax.ppermute(value, axis, [(i, target(i, shift, count)) for i in range(co...  16.9 us
    ppermute x10, starting transfers between devices, send_back(): lax.ppermute(value, axis, [(target(i, shift, count), i) for i in range(co...  13.1 us
    unnamed x29, local copies, waits for them, and re-layouts  7.02 us
    pallas_call x1, Pallas kernels, on_device(): pl.pallas_call(functools.partial(slot_forward_kernel, edges, dom, chan, c...  4.83 us
    pallas_call x1, Pallas kernels, on_device(): pl.pallas_call(functools.partial(slot_backward_kernel, edges, dom, chan,...  3.98 us
    pallas_call x1, Pallas kernels, on_device(): pl.pallas_call(functools.partial(local_forward_kernel, edges, blk, nodes,...  3.6 us
    ppermute x10, waiting for transfers between devices, send_back(): lax.ppermute(value, axis, [(target(i, shift, count), i) for i in range(co...  3.12 us
  transfers between devices with their start and end apart: 26, of which 7 were waited for; matrix products, arithmetic and copies ran while one was open for 1% of the time, Pallas kernels for 19%

profile of v1, /device:TPU:0, one launch (start us, length us, event | category | flops | bytes accessed | tf_op | source)
XLA Modules:
  0.0 84.8 jit_solution(17009798477809485892)
XLA Ops:
  0.6 3.0 %collective-permute-start.11 = (bf16[128,2048]{1,0:T(8,128)(2,1)}, bf16[128,2048]{1,0:T(8,128)(2,1)S(1)}, u32[]{:S(2)}, u32[]{:S(2)}) collective-permute-start(bf16[128,2048]{1,0:T(8,128)(2,1)} %rest_4_.1), channel_id=1, source_target_pairs={{0,2},{1,3},{2,0},{3,1},{4,6},{5,7},{6,4},{7,5},{8,10},{9,11},{10,... | collective-permute-start | bytes 1572872 | tf_op jit(solution)/shard_map/ppermute | solution.py:30
  3.7 12.1 %collective-permute-done.11.rest_6_ = bf16[128,2048]{1,0:T(8,128)(2,1)S(1)} collective-permute-done((bf16[128,2048]{1,0:T(8,128)(2,1)}, bf16[128,2048]{1,0:T(8,128)(2,1)S(1)}, u32[]{:S(2)}, u32[]{:S(2)}) %collective-permute-start.11) | collective-permute-done | bytes 524320 | tf_op jit(solution)/shard_map/ppermute | solution.py:30
  15.8 0.8 copy.13.blocks_ref
  16.6 1.0 %copy-done.2 = bf16[128,2048]{1,0:T(8,128)(2,1)S(1)} copy-done((bf16[128,2048]{1,0:T(8,128)(2,1)S(1)}, bf16[128,2048]{1,0:T(8,128)(2,1)}, u32[]{:S(2)}) %copy-start.2) | copy-done | bytes 524312
  17.6 0.7 copy-done.12
  18.3 0.9 %pack.1 = (bf16[2,128,128]{2,1,0:T(8,128)(2,1)S(1)}, bf16[2,128,128]{2,1,0:T(8,128)(2,1)S(1)}, bf16[2,128,128]{2,1,0:T(8,128)(2,1)S(1)}, bf16[2,128,128]{2,1,0:T...) custom-call(s32[8,2]{1,0:T(8,128)S(1)} %copy.13.blocks_ref, ...), custom_call_target="tpu_custom_call" | custom-call | tf_op jit(solution)/shard_map/pack/pallas_call | solution.py:262
  19.2 1.8 %collective-permute-start = (bf16[2,128,128]{2,1,0:T(8,128)(2,1)S(1)}, bf16[2,128,128]{2,1,0:T(8,128)(2,1)S(1)}, u32[]{:S(2)}, u32[]{:S(2)}) collective-permute-start(bf16[2,128,128]{2,1,0:T(8,128)(2,1)S(1)} %get-tuple-element.36), channel_id=1, source_target_pairs={{0,4},{4,0},{8,12},{12,8},{16,20},{20,16},{24,28},{28,24},{1,5},{5... | collective-permute-start | bytes 196616 | tf_op jit(solution)/shard_map/ppermute | solution.py:30
  21.0 1.6 %collective-permute-start.1 = (bf16[2,128,128]{2,1,0:T(8,128)(2,1)S(1)}, bf16[2,128,128]{2,1,0:T(8,128)(2,1)S(1)}, u32[]{:S(2)}, u32[]{:S(2)}) collective-permute-start(bf16[2,128,128]{2,1,0:T(8,128)(2,1)S(1)} %get-tuple-element.37), channel_id=1, source_target_pairs={{0,8},{4,12},{8,0},{12,4},{16,24},{20,28},{24,16},{28,20},{1,9},{5... | collective-permute-start | bytes 196616 | tf_op jit(solution)/shard_map/ppermute | solution.py:30
  22.7 1.0 %collective-permute-done.rest_1_ = bf16[2,128,128]{2,1,0:T(8,128)(2,1)S(1)} collective-permute-done((bf16[2,128,128]{2,1,0:T(8,128)(2,1)S(1)}, bf16[2,128,128]{2,1,0:T(8,128)(2,1)S(1)}, u32[]{:S(2)}, u32[]{:S(2)}) %collective-permute-start) | collective-permute-done | bytes 65568 | tf_op jit(solution)/shard_map/ppermute | solution.py:30
  23.7 2.8 %collective-permute-start.3 = (bf16[2,128,128]{2,1,0:T(8,128)(2,1)S(1)}, bf16[2,128,128]{2,1,0:T(8,128)(2,1)S(1)}, u32[]{:S(2)}, u32[]{:S(2)}) collective-permute-start(bf16[2,128,128]{2,1,0:T(8,128)(2,1)S(1)} %get-tuple-element.39), channel_id=1, source_target_pairs={{0,16},{4,20},{8,24},{12,28},{16,0},{20,4},{24,8},{28,12},{1,17},{... | collective-permute-start | bytes 196616 | tf_op jit(solution)/shard_map/ppermute | solution.py:30
  26.6 1.3 %collective-permute-start.4 = (bf16[2,128,128]{2,1,0:T(8,128)(2,1)S(1)}, bf16[2,128,128]{2,1,0:T(8,128)(2,1)S(1)}, u32[]{:S(2)}, u32[]{:S(2)}) collective-permute-start(bf16[2,128,128]{2,1,0:T(8,128)(2,1)S(1)} %get-tuple-element.40), channel_id=1, source_target_pairs={{0,20},{4,16},{8,28},{12,24},{16,4},{20,0},{24,12},{28,8},{1,21},{... | collective-permute-start | bytes 196616 | tf_op jit(solution)/shard_map/ppermute | solution.py:30
  27.8 3.6 %collective-permute-start.5 = (bf16[2,128,128]{2,1,0:T(8,128)(2,1)S(1)}, bf16[2,128,128]{2,1,0:T(8,128)(2,1)S(1)}, u32[]{:S(2)}, u32[]{:S(2)}) collective-permute-start(bf16[2,128,128]{2,1,0:T(8,128)(2,1)S(1)} %get-tuple-element.41), channel_id=1, source_target_pairs={{0,24},{4,28},{8,16},{12,20},{16,8},{20,12},{24,0},{28,4},{1,25},{... | collective-permute-start | bytes 196616 | tf_op jit(solution)/shard_map/ppermute | solution.py:30
  31.4 5.2 %collective-permute-start.6 = (bf16[2,128,128]{2,1,0:T(8,128)(2,1)S(1)}, bf16[2,128,128]{2,1,0:T(8,128)(2,1)S(1)}, u32[]{:S(2)}, u32[]{:S(2)}) collective-permute-start(bf16[2,128,128]{2,1,0:T(8,128)(2,1)S(1)} %get-tuple-element.42), channel_id=1, source_target_pairs={{0,28},{4,24},{8,20},{12,16},{16,12},{20,8},{24,4},{28,0},{1,29},{... | collective-permute-start | bytes 196616 | tf_op jit(solution)/shard_map/ppermute | solution.py:30
  36.6 2.2 %copy-done = bf16[128,128,128]{2,1,0:T(8,128)(2,1)S(1)} copy-done((bf16[128,128,128]{2,1,0:T(8,128)(2,1)S(1)}, bf16[128,128,128]{2,1,0:T(8,128)(2,1)}, u32[]{:S(2)}) %copy-start) | copy-done | bytes 4194328
  38.8 1.0 %copy-done.3 = bf16[128,2048]{1,0:T(8,128)(2,1)S(1)} copy-done((bf16[128,2048]{1,0:T(8,128)(2,1)S(1)}, bf16[128,2048]{1,0:T(8,128)(2,1)}, u32[]{:S(2)}) %copy-start.3) | copy-done | bytes 524312
  41.2 3.6 %local_forward.1 = (f32[8,128,128]{2,1,0:T(8,128)S(1)}, s32[128]{0:T(128)S(1)}, s32[1]{0:T(128)}) custom-call(s32[128]{0:T(128)S(1)} %copy-done.8, s32[128]{0:T(128)S(1)} %copy-done.10, bf16[128,2048]{1,0:T(8,128)(2,1)S(1)} %copy-done.3, bf16[128,128,128]{2,1,0:T(8,128)(2,1)S(1)} %copy-done), custom_call_target="tpu_custom_call" | custom-call | tf_op jit(solution)/shard_map/local_forward/pallas_call | solution.py:273
  44.9 4.8 %slot_forward.1 = (bf16[256,128]{1,0:T(8,128)(2,1)S(1)}, bf16[256,128]{1,0:T(8,128)(2,1)S(1)}, bf16[256,128]{1,0:T(8,128)(2,1)S(1)}, bf16[256,128]{1,0:T(8,128)(2,1)S(1)}) custom-call(s32[128]{0:T(128)S(1)} %copy-done.8, s32[128]{0:T(128)S(1)} %copy-done.10, s32[128]{0:T(128)S(1)} %get-tuple-element.32.order_ref, s32[1]{0:T(128)} %get-tuple-element.33.split_ref, ...), custom_call_target="tpu_custom_call" | custom-call | tf_op jit(solution)/shard_map/slot_forward/pallas_call | solution.py:287
  49.8 1.6 %collective-permute-start.8 = (bf16[256,128]{1,0:T(8,128)(2,1)S(1)}, bf16[256,128]{1,0:T(8,128)(2,1)S(1)}, u32[]{:S(2)}, u32[]{:S(2)}) collective-permute-start(bf16[256,128]{1,0:T(8,128)(2,1)S(1)} %get-tuple-element.45), channel_id=1, source_target_pairs={{0,2},{1,3},{2,0},{3,1},{4,6},{5,7},{6,4},{7,5},{8,10},{9,11},{10,... | collective-permute-start | bytes 196616 | tf_op jit(solution)/shard_map/ppermute | solution.py:30
  51.7 2.6 %collective-permute-done.8.rest_2_ = bf16[256,128]{1,0:T(8,128)(2,1)S(1)} collective-permute-done((bf16[256,128]{1,0:T(8,128)(2,1)S(1)}, bf16[256,128]{1,0:T(8,128)(2,1)S(1)}, u32[]{:S(2)}, u32[]{:S(2)}) %collective-permute-start.8) | collective-permute-done | bytes 65568 | tf_op jit(solution)/shard_map/ppermute | solution.py:30
  54.3 1.1 %collective-permute-done.9.rest_3_ = bf16[256,128]{1,0:T(8,128)(2,1)S(1)} collective-permute-done((bf16[256,128]{1,0:T(8,128)(2,1)S(1)}, bf16[256,128]{1,0:T(8,128)(2,1)S(1)}, u32[]{:S(2)}, u32[]{:S(2)}) %collective-permute-start.9) | collective-permute-done | bytes 65568 | tf_op jit(solution)/shard_map/ppermute | solution.py:30
  55.5 2.3 %mlp.1 = (bf16[256,128]{1,0:T(8,128)(2,1)S(1)}, bf16[128,256]{1,0:T(8,128)(2,1)S(1)}, bf16[128,256]{1,0:T(8,128)(2,1)S(1)}, bf16[128,256]{1,0:T(8,128)(2,1)S(1)}, bf16[128,256]{1,0:T(8,128)(2,1)S(1)}) custom-call(f32[1,2048]{1,0:T(1,128)S(1)} %bitcast.1, bf16[2048,128]{1,0:T(8,128)(2,1)S(1)} %copy-done.4, bf16[1024,128]{1,0:T(8,128)(2,1)S(1)} %copy-done.6, ...), custom_call_target="tpu_custom_call" | custom-call | tf_op jit(solution)/shard_map/mlp/pallas_call | solution.py:301
  58.0 1.5 %collective-permute-start.14 = (bf16[128,256]{1,0:T(8,128)(2,1)S(1)}, bf16[128,256]{1,0:T(8,128)(2,1)S(1)}, u32[]{:S(2)}, u32[]{:S(2)}) collective-permute-start(bf16[128,256]{1,0:T(8,128)(2,1)S(1)} %get-tuple-element.49), channel_id=1, source_target_pairs={{2,0},{3,1},{0,2},{1,3},{6,4},{7,5},{4,6},{5,7},{10,8},{11,9},{8,1... | collective-permute-start | bytes 196616 | tf_op jit(solution)/shard_map/ppermute | solution.py:34
  59.7 1.5 %collective-permute-start.25 = (bf16[256,128]{1,0:T(8,128)(2,1)S(1)}, bf16[256,128]{1,0:T(8,128)(2,1)S(1)}, u32[]{:S(2)}, u32[]{:S(2)}) collective-permute-start(bf16[256,128]{1,0:T(8,128)(2,1)S(1)} %get-tuple-element.59.rest_8_), channel_id=1, source_target_pairs={{0,3},{1,2},{2,1},{3,0},{4,7},{5,6},{6,5},{7,4},{8,11},{9,10},{10,... | collective-permute-start | bytes 196616 | tf_op jit(solution)/shard_map/ppermute | solution.py:30
  62.3 1.4 %collective-permute-done.15.rest_3_ = bf16[128,256]{1,0:T(8,128)(2,1)S(1)} collective-permute-done((bf16[128,256]{1,0:T(8,128)(2,1)S(1)}, bf16[128,256]{1,0:T(8,128)(2,1)S(1)}, u32[]{:S(2)}, u32[]{:S(2)}) %collective-permute-start.15) | collective-permute-done | bytes 65568 | tf_op jit(solution)/shard_map/ppermute | solution.py:34
  63.7 4.0 %slot_backward.1 = (bf16[2,128,128]{2,1,0:T(8,128)(2,1)S(1)}, bf16[2,128,128]{2,1,0:T(8,128)(2,1)S(1)}, bf16[2,128,128]{2,1,0:T(8,128)(2,1)S(1)}, bf16[2,128,128...) custom-call(s32[128]{0:T(128)S(1)} %copy-done.9, ...), custom_call_target="tpu_custom_call" | custom-call | tf_op jit(solution)/shard_map/slot_backward/pallas_call | solution.py:318
  67.7 1.0 %collective-permute-start.16 = (bf16[2,128,128]{2,1,0:T(8,128)(2,1)S(1)}, bf16[2,128,128]{2,1,0:T(8,128)(2,1)S(1)}, u32[]{:S(2)}, u32[]{:S(2)}) collective-permute-start(bf16[2,128,128]{2,1,0:T(8,128)(2,1)S(1)} %get-tuple-element.52), channel_id=1, source_target_pairs={{4,0},{0,4},{12,8},{8,12},{20,16},{16,20},{28,24},{24,28},{5,1},{1... | collective-permute-start | bytes 196616 | tf_op jit(solution)/shard_map/ppermute | solution.py:34
  68.7 2.6 %collective-permute-start.18 = (bf16[2,128,128]{2,1,0:T(8,128)(2,1)S(1)}, bf16[2,128,128]{2,1,0:T(8,128)(2,1)S(1)}, u32[]{:S(2)}, u32[]{:S(2)}) collective-permute-start(bf16[2,128,128]{2,1,0:T(8,128)(2,1)S(1)} %get-tuple-element.54), channel_id=1, source_target_pairs={{12,0},{8,4},{4,8},{0,12},{28,16},{24,20},{20,24},{16,28},{13,1},{... | collective-permute-start | bytes 196616 | tf_op jit(solution)/shard_map/ppermute | solution.py:34
  71.3 3.3 %collective-permute-start.20 = (bf16[2,128,128]{2,1,0:T(8,128)(2,1)S(1)}, bf16[2,128,128]{2,1,0:T(8,128)(2,1)S(1)}, u32[]{:S(2)}, u32[]{:S(2)}) collective-permute-start(bf16[2,128,128]{2,1,0:T(8,128)(2,1)S(1)} %get-tuple-element.56), channel_id=1, source_target_pairs={{20,0},{16,4},{28,8},{24,12},{4,16},{0,20},{12,24},{8,28},{21,1},{... | collective-permute-start | bytes 196616 | tf_op jit(solution)/shard_map/ppermute | solution.py:34
  74.6 4.3 %collective-permute-start.22 = (bf16[2,128,128]{2,1,0:T(8,128)(2,1)S(1)}, bf16[2,128,128]{2,1,0:T(8,128)(2,1)S(1)}, u32[]{:S(2)}, u32[]{:S(2)}) collective-permute-start(bf16[2,128,128]{2,1,0:T(8,128)(2,1)S(1)} %get-tuple-element.58), channel_id=1, source_target_pairs={{28,0},{24,4},{20,8},{16,12},{12,16},{8,20},{4,24},{0,28},{29,1},{... | collective-permute-start | bytes 196616 | tf_op jit(solution)/shard_map/ppermute | solution.py:34
  79.0 2.8 %local_backward.1.local_ref = f32[16,128,128]{2,1,0:T(8,128)S(1)} custom-call(s32[128]{0:T(128)S(1)} %copy-done.9, s32[128]{0:T(128)S(1)} %copy-done.11, s32[128]{0:T(128)S(1)} %get-tuple-element.32.order_ref, s32[1]{0:T(128)} %get-tuple-element.33.split_ref, bf16[128,128,128]{2,1,0:T(8,128)(2,1)S(1)} %copy-done.1, ...), custom_call_target="tpu_custom_call" | custom-call | tf_op jit(solution)/shard_map/local_backward/pallas_call | solution.py:334
  81.7 1.2 %collective-permute-done.20.rest_5_ = bf16[2,128,128]{2,1,0:T(8,128)(2,1)S(1)} collective-permute-done((bf16[2,128,128]{2,1,0:T(8,128)(2,1)S(1)}, bf16[2,128,128]{2,1,0:T(8,128)(2,1)S(1)}, u32[]{:S(2)}, u32[]{:S(2)}) %collective-permute-start.20) | collective-permute-done | bytes 65568 | tf_op jit(solution)/shard_map/ppermute | solution.py:34
  82.9 1.9 %final.1 = (bf16[128,2048]{1,0:T(8,128)(2,1)}, bf16[1024,128]{1,0:T(8,128)(2,1)}) custom-call(s32[8,2]{1,0:T(8,128)S(1)} %copy.13.blocks_ref, s32[8]{0:T(128)S(1)} %copy-done.13, f32[16,128,128]{2,1,0:T(8,128)S(1)} %local_backward.1.local_ref, bf16[2,128,128]{2,1,0:T(8,128)(2,1)S(1)} %get-tuple-element.51.rest_0_, ...), custom_call_target="tpu_custom_call" | custom-call | tf_op jit(solution)/shard_map/final/pallas_call | solution.py:347
  (56 shorter events, 3.6 us)
Async XLA Ops:
  0.6 15.2 %collective-permute-start.11 = (bf16[128,2048]{1,0:T(8,128)(2,1)}, bf16[128,2048]{1,0:T(8,128)(2,1)S(1)}, u32[]{:S(2)}, u32[]{:S(2)}) collective-permute-start(bf16[128,2048]{1,0:T(8,128)(2,1)} %rest_4_.1), channel_id=1, source_target_pairs={{0,2},{1,3},{2,0},{3,1},{4,6},{5,7},{6,4},{7,5},{8,10},{9,11},{10,... | collective-permute-start | bytes 1572872 | tf_op jit(solution)/shard_map/ppermute | solution.py:30
  3.7 51.8 %collective-permute-start.10 = (bf16[128,2048]{1,0:T(8,128)(2,1)}, bf16[128,2048]{1,0:T(8,128)(2,1)S(1)}, u32[]{:S(2)}, u32[]{:S(2)}) collective-permute-start(bf16[128,2048]{1,0:T(8,128)(2,1)} %rest_4_.1), channel_id=1, source_target_pairs={{0,1},{1,0},{2,3},{3,2},{4,5},{5,4},{6,7},{7,6},{8,9},{9,8},{10,11... | collective-permute-start | bytes 1572872 | tf_op jit(solution)/shard_map/ppermute | solution.py:30
  15.8 39.6 %collective-permute-start.12 = (bf16[128,2048]{1,0:T(8,128)(2,1)S(1)}, bf16[128,2048]{1,0:T(8,128)(2,1)S(1)}, u32[]{:S(2)}, u32[]{:S(2)}) collective-permute-start(bf16[128,2048]{1,0:T(8,128)(2,1)S(1)} %collective-permute-done.11.rest_6_), channel_id=1, source_target_pairs={{0,1},{1,0},{2,3},{3,2},{4,5},{5,4},{6,7},{7,6},{8,9},{9,8},{10,11... | collective-permute-start | bytes 1572872 | tf_op jit(solution)/shard_map/ppermute | solution.py:30
  19.2 4.6 %collective-permute-start = (bf16[2,128,128]{2,1,0:T(8,128)(2,1)S(1)}, bf16[2,128,128]{2,1,0:T(8,128)(2,1)S(1)}, u32[]{:S(2)}, u32[]{:S(2)}) collective-permute-start(bf16[2,128,128]{2,1,0:T(8,128)(2,1)S(1)} %get-tuple-element.36), channel_id=1, source_target_pairs={{0,4},{4,0},{8,12},{12,8},{16,20},{20,16},{24,28},{28,24},{1,5},{5... | collective-permute-start | bytes 196616 | tf_op jit(solution)/shard_map/ppermute | solution.py:30
  21.0 5.6 %collective-permute-start.1 = (bf16[2,128,128]{2,1,0:T(8,128)(2,1)S(1)}, bf16[2,128,128]{2,1,0:T(8,128)(2,1)S(1)}, u32[]{:S(2)}, u32[]{:S(2)}) collective-permute-start(bf16[2,128,128]{2,1,0:T(8,128)(2,1)S(1)} %get-tuple-element.37), channel_id=1, source_target_pairs={{0,8},{4,12},{8,0},{12,4},{16,24},{20,28},{24,16},{28,20},{1,9},{5... | collective-permute-start | bytes 196616 | tf_op jit(solution)/shard_map/ppermute | solution.py:30
  22.5 5.3 %collective-permute-start.2 = (bf16[2,128,128]{2,1,0:T(8,128)(2,1)S(1)}, bf16[2,128,128]{2,1,0:T(8,128)(2,1)S(1)}, u32[]{:S(2)}, u32[]{:S(2)}) collective-permute-start(bf16[2,128,128]{2,1,0:T(8,128)(2,1)S(1)} %get-tuple-element.38), channel_id=1, source_target_pairs={{0,12},{4,8},{8,4},{12,0},{16,28},{20,24},{24,20},{28,16},{1,13},{... | collective-permute-start | bytes 196616 | tf_op jit(solution)/shard_map/ppermute | solution.py:30
  23.7 7.7 %collective-permute-start.3 = (bf16[2,128,128]{2,1,0:T(8,128)(2,1)S(1)}, bf16[2,128,128]{2,1,0:T(8,128)(2,1)S(1)}, u32[]{:S(2)}, u32[]{:S(2)}) collective-permute-start(bf16[2,128,128]{2,1,0:T(8,128)(2,1)S(1)} %get-tuple-element.39), channel_id=1, source_target_pairs={{0,16},{4,20},{8,24},{12,28},{16,0},{20,4},{24,8},{28,12},{1,17},{... | collective-permute-start | bytes 196616 | tf_op jit(solution)/shard_map/ppermute | solution.py:30
  26.6 18.2 %collective-permute-start.4 = (bf16[2,128,128]{2,1,0:T(8,128)(2,1)S(1)}, bf16[2,128,128]{2,1,0:T(8,128)(2,1)S(1)}, u32[]{:S(2)}, u32[]{:S(2)}) collective-permute-start(bf16[2,128,128]{2,1,0:T(8,128)(2,1)S(1)} %get-tuple-element.40), channel_id=1, source_target_pairs={{0,20},{4,16},{8,28},{12,24},{16,4},{20,0},{24,12},{28,8},{1,21},{... | collective-permute-start | bytes 196616 | tf_op jit(solution)/shard_map/ppermute | solution.py:30
  27.8 17.0 %collective-permute-start.5 = (bf16[2,128,128]{2,1,0:T(8,128)(2,1)S(1)}, bf16[2,128,128]{2,1,0:T(8,128)(2,1)S(1)}, u32[]{:S(2)}, u32[]{:S(2)}) collective-permute-start(bf16[2,128,128]{2,1,0:T(8,128)(2,1)S(1)} %get-tuple-element.41), channel_id=1, source_target_pairs={{0,24},{4,28},{8,16},{12,20},{16,8},{20,12},{24,0},{28,4},{1,25},{... | collective-permute-start | bytes 196616 | tf_op jit(solution)/shard_map/ppermute | solution.py:30
  31.4 13.4 %collective-permute-start.6 = (bf16[2,128,128]{2,1,0:T(8,128)(2,1)S(1)}, bf16[2,128,128]{2,1,0:T(8,128)(2,1)S(1)}, u32[]{:S(2)}, u32[]{:S(2)}) collective-permute-start(bf16[2,128,128]{2,1,0:T(8,128)(2,1)S(1)} %get-tuple-element.42), channel_id=1, source_target_pairs={{0,28},{4,24},{8,20},{12,16},{16,12},{20,8},{24,4},{28,0},{1,29},{... | collective-permute-start | bytes 196616 | tf_op jit(solution)/shard_map/ppermute | solution.py:30
  41.2 14.3 %copy-start.5 = (bf16[128,2048]{1,0:T(8,128)(2,1)S(1)}, bf16[128,2048]{1,0:T(8,128)(2,1)}, u32[]{:S(2)}) copy-start(bf16[128,2048]{1,0:T(8,128)(2,1)} %rest_4_.1) | copy-start | bytes 1572868
  41.2 14.3 %copy-start.6 = (bf16[1024,128]{1,0:T(8,128)(2,1)S(1)}, bf16[1024,128]{1,0:T(8,128)(2,1)}, u32[]{:S(2)}) copy-start(bf16[1024,128]{1,0:T(8,128)(2,1)} %g_ref.1) | copy-start | bytes 786436
  41.2 14.3 %copy-start.7 = (f32[2048]{0:T(1024)S(1)}, f32[2048]{0:T(1024)}, u32[]{:S(2)}) copy-start(f32[2048]{0:T(1024)} %param.17) | copy-start | bytes 24580
  44.9 18.9 %copy-start.9 = (s32[128]{0:T(128)S(1)}, s32[128]{0:T(128)}, u32[]{:S(2)}) copy-start(s32[128]{0:T(128)} %src_ref.7) | copy-start | bytes 1540
  44.9 18.9 %copy-start.11 = (s32[128]{0:T(128)S(1)}, s32[128]{0:T(128)}, u32[]{:S(2)}) copy-start(s32[128]{0:T(128)} %obs_ref.7) | copy-start | bytes 1540
  49.7 1.9 %collective-permute-start.7 = (bf16[256,128]{1,0:T(8,128)(2,1)S(1)}, bf16[256,128]{1,0:T(8,128)(2,1)S(1)}, u32[]{:S(2)}, u32[]{:S(2)}) collective-permute-start(bf16[256,128]{1,0:T(8,128)(2,1)S(1)} %get-tuple-element.44), channel_id=1, source_target_pairs={{0,1},{1,0},{2,3},{3,2},{4,5},{5,4},{6,7},{7,6},{8,9},{9,8},{10,11... | collective-permute-start | bytes 196616 | tf_op jit(solution)/shard_map/ppermute | solution.py:30
  49.8 4.5 %collective-permute-start.8 = (bf16[256,128]{1,0:T(8,128)(2,1)S(1)}, bf16[256,128]{1,0:T(8,128)(2,1)S(1)}, u32[]{:S(2)}, u32[]{:S(2)}) collective-permute-start(bf16[256,128]{1,0:T(8,128)(2,1)S(1)} %get-tuple-element.45), channel_id=1, source_target_pairs={{0,2},{1,3},{2,0},{3,1},{4,6},{5,7},{6,4},{7,5},{8,10},{9,11},{10,... | collective-permute-start | bytes 196616 | tf_op jit(solution)/shard_map/ppermute | solution.py:30
  51.4 4.0 %collective-permute-start.9 = (bf16[256,128]{1,0:T(8,128)(2,1)S(1)}, bf16[256,128]{1,0:T(8,128)(2,1)S(1)}, u32[]{:S(2)}, u32[]{:S(2)}) collective-permute-start(bf16[256,128]{1,0:T(8,128)(2,1)S(1)} %get-tuple-element.46), channel_id=1, source_target_pairs={{0,3},{1,2},{2,1},{3,0},{4,7},{5,6},{6,5},{7,4},{8,11},{9,10},{10,... | collective-permute-start | bytes 196616 | tf_op jit(solution)/shard_map/ppermute | solution.py:30
  57.8 4.0 %collective-permute-start.13 = (bf16[128,256]{1,0:T(8,128)(2,1)S(1)}, bf16[128,256]{1,0:T(8,128)(2,1)S(1)}, u32[]{:S(2)}, u32[]{:S(2)}) collective-permute-start(bf16[128,256]{1,0:T(8,128)(2,1)S(1)} %get-tuple-element.48), channel_id=1, source_target_pairs={{1,0},{0,1},{3,2},{2,3},{5,4},{4,5},{7,6},{6,7},{9,8},{8,9},{11,10... | collective-permute-start | bytes 196616 | tf_op jit(solution)/shard_map/ppermute | solution.py:34
  58.0 4.3 %collective-permute-start.14 = (bf16[128,256]{1,0:T(8,128)(2,1)S(1)}, bf16[128,256]{1,0:T(8,128)(2,1)S(1)}, u32[]{:S(2)}, u32[]{:S(2)}) collective-permute-start(bf16[128,256]{1,0:T(8,128)(2,1)S(1)} %get-tuple-element.49), channel_id=1, source_target_pairs={{2,0},{3,1},{0,2},{1,3},{6,4},{7,5},{4,6},{5,7},{10,8},{11,9},{8,1... | collective-permute-start | bytes 196616 | tf_op jit(solution)/shard_map/ppermute | solution.py:34
  59.5 4.3 %collective-permute-start.15 = (bf16[128,256]{1,0:T(8,128)(2,1)S(1)}, bf16[128,256]{1,0:T(8,128)(2,1)S(1)}, u32[]{:S(2)}, u32[]{:S(2)}) collective-permute-start(bf16[128,256]{1,0:T(8,128)(2,1)S(1)} %get-tuple-element.50), channel_id=1, source_target_pairs={{3,0},{2,1},{1,2},{0,3},{7,4},{6,5},{5,6},{4,7},{11,8},{10,9},{9,1... | collective-permute-start | bytes 196616 | tf_op jit(solution)/shard_map/ppermute | solution.py:34
  59.7 9.0 %collective-permute-start.25 = (bf16[256,128]{1,0:T(8,128)(2,1)S(1)}, bf16[256,128]{1,0:T(8,128)(2,1)S(1)}, u32[]{:S(2)}, u32[]{:S(2)}) collective-permute-start(bf16[256,128]{1,0:T(8,128)(2,1)S(1)} %get-tuple-element.59.rest_8_), channel_id=1, source_target_pairs={{0,3},{1,2},{2,1},{3,0},{4,7},{5,6},{6,5},{7,4},{8,11},{9,10},{10,... | collective-permute-start | bytes 196616 | tf_op jit(solution)/shard_map/ppermute | solution.py:30
  61.2 10.1 %collective-permute-start.24 = (bf16[256,128]{1,0:T(8,128)(2,1)S(1)}, bf16[256,128]{1,0:T(8,128)(2,1)S(1)}, u32[]{:S(2)}, u32[]{:S(2)}) collective-permute-start(bf16[256,128]{1,0:T(8,128)(2,1)S(1)} %get-tuple-element.59.rest_8_), channel_id=1, source_target_pairs={{0,2},{1,3},{2,0},{3,1},{4,6},{5,7},{6,4},{7,5},{8,10},{9,11},{10,... | collective-permute-start | bytes 196616 | tf_op jit(solution)/shard_map/ppermute | solution.py:30
  61.8 9.5 %collective-permute-start.23 = (bf16[256,128]{1,0:T(8,128)(2,1)S(1)}, bf16[256,128]{1,0:T(8,128)(2,1)S(1)}, u32[]{:S(2)}, u32[]{:S(2)}) collective-permute-start(bf16[256,128]{1,0:T(8,128)(2,1)S(1)} %get-tuple-element.59.rest_8_), channel_id=1, source_target_pairs={{0,1},{1,0},{2,3},{3,2},{4,5},{5,4},{6,7},{7,6},{8,9},{9,8},{10,11... | collective-permute-start | bytes 196616 | tf_op jit(solution)/shard_map/ppermute | solution.py:30
  63.7 19.2 %copy-start.13 = (s32[8]{0:T(128)S(1)}, s32[8]{0:T(128)}, u32[]{:S(2)}) copy-start(s32[8]{0:T(128)} %counts_ref.3) | copy-start | bytes 100
  67.7 6.9 %collective-permute-start.16 = (bf16[2,128,128]{2,1,0:T(8,128)(2,1)S(1)}, bf16[2,128,128]{2,1,0:T(8,128)(2,1)S(1)}, u32[]{:S(2)}, u32[]{:S(2)}) collective-permute-start(bf16[2,128,128]{2,1,0:T(8,128)(2,1)S(1)} %get-tuple-element.52), channel_id=1, source_target_pairs={{4,0},{0,4},{12,8},{8,12},{20,16},{16,20},{28,24},{24,28},{5,1},{1... | collective-permute-start | bytes 196616 | tf_op jit(solution)/shard_map/ppermute | solution.py:34
  68.7 5.9 %collective-permute-start.17 = (bf16[2,128,128]{2,1,0:T(8,128)(2,1)S(1)}, bf16[2,128,128]{2,1,0:T(8,128)(2,1)S(1)}, u32[]{:S(2)}, u32[]{:S(2)}) collective-permute-start(bf16[2,128,128]{2,1,0:T(8,128)(2,1)S(1)} %get-tuple-element.53), channel_id=1, source_target_pairs={{8,0},{12,4},{0,8},{4,12},{24,16},{28,20},{16,24},{20,28},{9,1},{1... | collective-permute-start | bytes 196616 | tf_op jit(solution)/shard_map/ppermute | solution.py:34
  68.7 13.0 %collective-permute-start.18 = (bf16[2,128,128]{2,1,0:T(8,128)(2,1)S(1)}, bf16[2,128,128]{2,1,0:T(8,128)(2,1)S(1)}, u32[]{:S(2)}, u32[]{:S(2)}) collective-permute-start(bf16[2,128,128]{2,1,0:T(8,128)(2,1)S(1)} %get-tuple-element.54), channel_id=1, source_target_pairs={{12,0},{8,4},{4,8},{0,12},{28,16},{24,20},{20,24},{16,28},{13,1},{... | collective-permute-start | bytes 196616 | tf_op jit(solution)/shard_map/ppermute | solution.py:34
  71.3 10.4 %collective-permute-start.19 = (bf16[2,128,128]{2,1,0:T(8,128)(2,1)S(1)}, bf16[2,128,128]{2,1,0:T(8,128)(2,1)S(1)}, u32[]{:S(2)}, u32[]{:S(2)}) collective-permute-start(bf16[2,128,128]{2,1,0:T(8,128)(2,1)S(1)} %get-tuple-element.55), channel_id=1, source_target_pairs={{16,0},{20,4},{24,8},{28,12},{0,16},{4,20},{8,24},{12,28},{17,1},{... | collective-permute-start | bytes 196616 | tf_op jit(solution)/shard_map/ppermute | solution.py:34
  71.3 11.6 %collective-permute-start.20 = (bf16[2,128,128]{2,1,0:T(8,128)(2,1)S(1)}, bf16[2,128,128]{2,1,0:T(8,128)(2,1)S(1)}, u32[]{:S(2)}, u32[]{:S(2)}) collective-permute-start(bf16[2,128,128]{2,1,0:T(8,128)(2,1)S(1)} %get-tuple-element.56), channel_id=1, source_target_pairs={{20,0},{16,4},{28,8},{24,12},{4,16},{0,20},{12,24},{8,28},{21,1},{... | collective-permute-start | bytes 196616 | tf_op jit(solution)/shard_map/ppermute | solution.py:34
  74.6 8.3 %collective-permute-start.21 = (bf16[2,128,128]{2,1,0:T(8,128)(2,1)S(1)}, bf16[2,128,128]{2,1,0:T(8,128)(2,1)S(1)}, u32[]{:S(2)}, u32[]{:S(2)}) collective-permute-start(bf16[2,128,128]{2,1,0:T(8,128)(2,1)S(1)} %get-tuple-element.57), channel_id=1, source_target_pairs={{24,0},{28,4},{16,8},{20,12},{8,16},{12,20},{0,24},{4,28},{25,1},{... | collective-permute-start | bytes 196616 | tf_op jit(solution)/shard_map/ppermute | solution.py:34
  74.6 8.3 %collective-permute-start.22 = (bf16[2,128,128]{2,1,0:T(8,128)(2,1)S(1)}, bf16[2,128,128]{2,1,0:T(8,128)(2,1)S(1)}, u32[]{:S(2)}, u32[]{:S(2)}) collective-permute-start(bf16[2,128,128]{2,1,0:T(8,128)(2,1)S(1)} %get-tuple-element.58), channel_id=1, source_target_pairs={{28,0},{24,4},{20,8},{16,12},{12,16},{8,20},{4,24},{0,28},{29,1},{... | collective-permute-start | bytes 196616 | tf_op jit(solution)/shard_map/ppermute | solution.py:34
  (8 other events, 24.1 us)

commit v2 on v1

v2 whole, which is shorter than its diff:
```python
import functools

import jax
import jax.numpy as jnp
from jax import lax
from jax.experimental import pallas as pl
from jax.experimental.pallas import tpu as pltpu
from jax.sharding import PartitionSpec as P

F32 = jnp.float32
BF16 = jnp.bfloat16
UNROLL = 32
NT = (((1,), (1,)), ((), ()))
NN = (((1,), (0,)), ((), ()))


def target(index, shift, count):
    if count & (count - 1) == 0:
        return index ^ shift
    return (index + shift) % count


def source(index, shift, count):
    if count & (count - 1) == 0:
        return index ^ shift
    return (index + count - shift) % count


def send(value, axis, shift, count):
    return lax.ppermute(value, axis, [(i, target(i, shift, count)) for i in range(count)])


def send_back(value, axis, shift, count):
    return lax.ppermute(value, axis, [(target(i, shift, count), i) for i in range(count)])


def vmem(count):
    return [pl.BlockSpec(memory_space=pltpu.VMEM)] * count


def smem(count):
    return [pl.BlockSpec(memory_space=pltpu.SMEM)] * count


def hbm(count):
    return [pl.BlockSpec(memory_space=pltpu.HBM)] * count


def params():
    return pltpu.CompilerParams(vmem_limit_bytes=48 * 1024 * 1024)


def is_near(shift, dom):
    return shift < (dom + 1) // 2


def fetch(pairs, sems):
    copies = [pltpu.make_async_copy(a, b, sems.at[i]) for i, (a, b) in enumerate(pairs)]
    for copy in copies:
        copy.start()
    return copies


def pack_kernel(dom, cap, blk, nodes, blocks_hbm, counts_hbm, latent_hbm, *rest):
    outs, (blocks_ref, counts_ref, latent_ref, sems) = rest[:dom], rest[dom:]
    pairs = ((latent_hbm, latent_ref), (blocks_hbm, blocks_ref), (counts_hbm, counts_ref))
    for copy in fetch(pairs, sems):
        copy.wait()
    me = lax.axis_index("dom")
    for d in range(dom):
        q = target(me, d, dom)
        for s in range(cap):
            block = jnp.clip(blocks_ref[s, q], 0, nodes - 1)
            value = latent_ref[:, pl.ds(pl.multiple_of(block * blk, blk), blk)]
            outs[d][s] = jnp.where(s < counts_ref[q], value, jnp.zeros_like(value))


class Plan:
    def __init__(self, edges):
        self.edges = edges
        self.length = edges + UNROLL

    def size(self):
        return 9 * self.length + 3

    def at(self, kind, field):
        return (kind * 3 + field) * self.length

    def make(self, ref, src_ref, obs_ref, nodes, obs, dom, cap):
        me = lax.axis_index("dom")
        near_of = [
            functools.reduce(
                jnp.logical_or, [source(me, d, dom) == p for d in range(dom) if is_near(d, dom)]
            ).astype(jnp.int32)
            for p in range(dom)
        ]
        near_bits = None
        if dom <= 16:
            near_bits = sum(near_of[p] << p for p in range(dom))

        def one(e, counts):
            src = src_ref[e]
            slot = jnp.maximum(src - nodes, 0)
            p = slot // cap
            if near_bits is not None:
                near = (near_bits >> p) & 1
            else:
                near = is_near(lax.rem(me - p + dom, dom), dom).astype(jnp.int32)
            local = (src < nodes).astype(jnp.int32)
            near = (1 - local) * near
            far = 1 - local - near
            kind = near + 2 * far
            i = local * counts[0] + near * counts[1] + far * counts[2]
            base = kind * 3 * self.length + i
            ref[base] = e
            ref[base + self.length] = jnp.where(local == 1, src, slot)
            ref[base + 2 * self.length] = obs_ref[e]
            return counts[0] + local, counts[1] + near, counts[2] + far

        zero = jnp.int32(0)
        counts = lax.fori_loop(0, self.edges, one, (zero, zero, zero), unroll=4)
        for kind in range(3):
            trash = nodes if kind == 0 else dom * cap
            start = counts[kind]

            def fill(i, carry):
                base = kind * 3 * self.length + start + i
                ref[base] = 0
                ref[base + self.length] = trash
                ref[base + 2 * self.length] = obs
                return carry

            lax.fori_loop(0, UNROLL, fill, 0, unroll=4)
            ref[9 * self.length + kind] = start

    def run(self, ref, kind, body):
        def step(t, carry):
            for u in range(UNROLL):
                i = kind * 3 * self.length + t * UNROLL + u
                body(ref[i], ref[i + self.length], ref[i + 2 * self.length])
            return carry

        count = ref[9 * self.length + kind]
        lax.fori_loop(0, (count + UNROLL - 1) // UNROLL, step, 0)


def local_forward_kernel(
    plan, dom, cap, blk, nodes, obs, src_hbm, obs_hbm, latent_hbm, weight_hbm, sum_ref, plan_ref, weight_ref, *rest
):
    src_ref, obs_ref, latent_ref, pool, sems = rest
    pairs = (
        (src_hbm, src_ref),
        (obs_hbm, obs_ref),
        (latent_hbm, latent_ref),
        (weight_hbm, weight_ref),
    )
    copies = fetch(pairs, sems)
    copies[0].wait()
    copies[1].wait()
    plan.make(plan_ref, src_ref, obs_ref, nodes, obs, dom, cap)
    copies[2].wait()
    for k in range(nodes):
        pool[k] = latent_ref[:, k * blk : (k + 1) * blk].T
    sum_ref[...] = jnp.zeros_like(sum_ref)
    copies[3].wait()

    def body(e, k, j):
        sum_ref[j] += lax.dot_general(weight_ref[e], pool[k], NN, preferred_element_type=F32)

    plan.run(plan_ref, 0, body)


def add_slots(plan, kind, shifts, dom, cap, plan_ref, weight_ref, arrived, pool, total):
    me = lax.axis_index("dom")
    for d, value in zip(shifts, arrived):
        start = source(me, d, dom) * cap
        for s in range(cap):
            pool[start + s] = value[s].T

    def body(e, k, j):
        total[j] += lax.dot_general(weight_ref[e], pool[k], NN, preferred_element_type=F32)

    plan.run(plan_ref, kind, body)


def near_forward_kernel(plan, shifts, dom, cap, plan_ref, sum_ref, weight_ref, *rest):
    arrived, (out_ref, pool) = rest[: len(shifts)], rest[len(shifts) :]
    out_ref[...] = sum_ref[...]
    add_slots(plan, 1, shifts, dom, cap, plan_ref, weight_ref, arrived, pool, out_ref)


def far_forward_kernel(plan, shifts, dom, cap, chan, plan_ref, sum_ref, weight_ref, *rest):
    count = len(shifts)
    arrived, outs, (pool, total) = rest[:count], rest[count : count + chan], rest[count + chan :]
    total[...] = sum_ref[...]
    add_slots(plan, 2, shifts, dom, cap, plan_ref, weight_ref, arrived, pool, total)
    whole = total.reshape(total.shape[0] * total.shape[1], total.shape[2])
    rows = outs[0].shape[0]
    mine = lax.axis_index("chan")
    for d in range(chan):
        start = pl.multiple_of(target(mine, d, chan) * rows, rows)
        outs[d][...] = whole[pl.ds(start, rows), :].astype(BF16)


def mlp_kernel(chan, tile, bias_ref, w_out_ref, g_ref, *rest):
    shares, weights = rest[:chan], rest[chan : 2 * chan]
    obs_ref, outs, (full_w, full_a, grad) = (
        rest[2 * chan],
        rest[2 * chan + 1 : 3 * chan + 1],
        rest[3 * chan + 1 :],
    )
    rows, feat = shares[0].shape
    hidden_width = grad.shape[1]
    for d in range(chan):
        full_w[d * feat : (d + 1) * feat, :] = weights[d][...]
        full_a[:, d * feat : (d + 1) * feat] = shares[d][...]
    mine = lax.axis_index("chan")
    g = g_ref[pl.ds(pl.multiple_of(mine * rows, rows), rows), :]
    out = jnp.zeros(obs_ref.shape, F32)
    for h in range(0, hidden_width, tile):
        cols = slice(h, h + tile)
        pre = lax.dot_general(full_a[...], full_w[:, cols], NN, preferred_element_type=F32)
        pre = pre + bias_ref[:, cols]
        sig = 0.5 * jnp.tanh(0.5 * pre) + 0.5
        hidden = (pre * sig).astype(BF16)
        w_out = w_out_ref[cols, :]
        out += lax.dot_general(hidden, w_out, NN, preferred_element_type=F32)
        back = lax.dot_general(g, w_out, NT, preferred_element_type=F32)
        grad[:, cols] = (back * sig * (1.0 + pre * (1.0 - sig))).astype(BF16)
    obs_ref[...] = out.astype(BF16)
    grad_agg = lax.dot_general(full_w[...], grad[...], NT, preferred_element_type=F32)
    for d in range(chan):
        outs[d][...] = grad_agg[d * feat : (d + 1) * feat].astype(BF16)


def gather_grad(chan, per, blk, shares, rows_grad):
    mine = lax.axis_index("chan")
    rows = shares[0].shape[1]
    for d in range(chan):
        start = target(mine, d, chan)
        if rows >= blk:
            for k in range(per):
                rows_grad[start * per + k] = shares[d][:, k * blk : (k + 1) * blk]
        else:
            split = blk // rows
            for k in range(split):

                @pl.when(start % split == k)
                def _():
                    rows_grad[start // split, :, k * rows : (k + 1) * rows] = shares[d][...]


def slot_gradients(plan, kind, shifts, dom, cap, plan_ref, weight_ref, rows_grad, outs, total):
    total[...] = jnp.zeros_like(total)

    def body(e, k, j):
        total[k] += lax.dot_general(rows_grad[j], weight_ref[e], NN, preferred_element_type=F32)

    plan.run(plan_ref, kind, body)
    me = lax.axis_index("dom")
    for d, out in zip(shifts, outs):
        out[...] = total[pl.ds(source(me, d, dom) * cap, cap)].astype(BF16)


def far_backward_kernel(plan, shifts, dom, cap, chan, blk, obs, plan_ref, weight_ref, *rest):
    shares, rows_grad, (*outs, total) = rest[:chan], rest[chan], rest[chan + 1 :]
    gather_grad(chan, max(1, obs // chan), blk, shares, rows_grad)
    slot_gradients(plan, 2, shifts, dom, cap, plan_ref, weight_ref, rows_grad, outs, total)


def near_backward_kernel(plan, shifts, dom, cap, plan_ref, weight_ref, rows_grad, *rest):
    *outs, total = rest
    slot_gradients(plan, 1, shifts, dom, cap, plan_ref, weight_ref, rows_grad, outs, total)


def local_backward_kernel(plan, plan_ref, weight_ref, rows_grad, total):
    total[...] = jnp.zeros_like(total)

    def body(e, k, j):
        total[k] += lax.dot_general(rows_grad[j], weight_ref[e], NN, preferred_element_type=F32)

    plan.run(plan_ref, 0, body)


def rows_kernel(chan, *rest):
    parts, obs_ref = rest[:chan], rest[chan]
    mine = lax.axis_index("chan")
    rows = parts[0].shape[0]
    for d in range(chan):
        start = pl.multiple_of(source(mine, d, chan) * rows, rows)
        obs_ref[pl.ds(start, rows), :] = parts[d][...]


def final_kernel(dom, cap, blk, nodes, blocks_hbm, counts_hbm, local_ref, *rest):
    returned, (grad_ref, total, blocks_ref, counts_ref, sems) = rest[:dom], rest[dom:]
    copies = fetch(((blocks_hbm, blocks_ref), (counts_hbm, counts_ref)), sems)
    total[...] = local_ref[:nodes]
    for copy in copies:
        copy.wait()
    me = lax.axis_index("dom")
    for d in range(dom):
        q = target(me, d, dom)
        for s in range(cap):
            value = returned[d][s].astype(F32)
            value = jnp.where(s < counts_ref[q], value, jnp.zeros_like(value))
            total[jnp.clip(blocks_ref[s, q], 0, nodes - 1)] += value
    for k in range(nodes):
        grad_ref[:, k * blk : (k + 1) * blk] = total[k].astype(BF16)


def after(value, *others):
    return lax.optimization_barrier((value, *others))[0]


def on_device(
    latent, edge_weight, send_blocks, send_counts, edge_src, edge_obs, w_in, bias, w_out, g_out
):
    dom = lax.axis_size("dom")
    chan = lax.axis_size("chan")
    feat, cols = latent.shape
    edges, blk, _ = edge_weight.shape
    nodes = cols // blk
    cap = send_blocks.shape[1]
    obs_rows, out_width = g_out.shape
    obs = obs_rows // blk
    rows = obs_rows // chan
    hidden_width = w_in.shape[1]
    shape = jax.ShapeDtypeStruct
    plan = Plan(edges)
    near = [d for d in range(dom) if is_near(d, dom)]
    far = [d for d in range(dom) if not is_near(d, dom)]
    tables = (send_blocks.T, send_counts)
    i32 = jnp.int32

    outgoing = pl.pallas_call(
        functools.partial(pack_kernel, dom, cap, blk, nodes),
        out_shape=[shape((cap, feat, blk), BF16)] * dom,
        in_specs=hbm(3),
        out_specs=vmem(dom),
        scratch_shapes=[
            pltpu.SMEM((cap, dom), i32),
            pltpu.SMEM((dom,), i32),
            pltpu.VMEM((feat, cols), BF16),
            pltpu.SemaphoreType.DMA((3,)),
        ],
        compiler_params=params(),
        name="pack",
    )(*tables, latent)
    arrived = {0: outgoing[0]}
    for d in far + near[1:]:
        arrived[d] = send(outgoing[d], "dom", d, dom)

    w_mine = after(w_in, outgoing[0])
    weights = {0: w_mine}
    late = chan // 2 if chan & (chan - 1) == 0 else 0
    if late:
        weights[late] = send(w_mine, "chan", late, chan)
        bit = late // 2
        while bit:
            for d in [d for d in sorted(weights) if d < late]:
                weights[d | bit] = send(weights[d], "chan", bit, chan)
            bit //= 2
    else:
        for d in range(1, chan):
            weights[d] = send(w_mine, "chan", d, chan)

    local_sum, table, weight = pl.pallas_call(
        functools.partial(local_forward_kernel, plan, dom, cap, blk, nodes, obs),
        out_shape=[
            shape((obs + 1, blk, feat), F32),
            shape((plan.size(),), i32),
            shape(edge_weight.shape, BF16),
        ],
        in_specs=hbm(4),
        out_specs=vmem(1) + smem(1) + vmem(1),
        scratch_shapes=[
            pltpu.SMEM((edges,), i32),
            pltpu.SMEM((edges,), i32),
            pltpu.VMEM((feat, cols), BF16),
            pltpu.VMEM((nodes + 1, blk, feat), BF16),
            pltpu.SemaphoreType.DMA((4,)),
        ],
        compiler_params=params(),
        name="local_forward",
    )(edge_src, edge_obs, latent, edge_weight)

    pool = pltpu.VMEM((dom * cap + 1, blk, feat), BF16)
    near_sum = pl.pallas_call(
        functools.partial(near_forward_kernel, plan, near, dom, cap),
        out_shape=shape((obs + 1, blk, feat), F32),
        in_specs=smem(1) + vmem(2 + len(near)),
        out_specs=pl.BlockSpec(memory_space=pltpu.VMEM),
        scratch_shapes=[pool],
        compiler_params=params(),
        name="near_forward",
    )(table, local_sum, weight, *[arrived[d] for d in near])

    shares = pl.pallas_call(
        functools.partial(far_forward_kernel, plan, far, dom, cap, chan),
        out_shape=[shape((rows, feat), BF16)] * chan,
        in_specs=smem(1) + vmem(2 + len(far)),
        out_specs=vmem(chan),
        scratch_shapes=[pool, pltpu.VMEM((obs + 1, blk, feat), F32)],
        compiler_params=params(),
        name="far_forward",
    )(table, near_sum, weight, *[arrived[d] for d in far])
    if late:
        weights[late] = after(weights[late], shares[0])
        bit = late // 2
        while bit:
            for d in [d for d in sorted(weights) if d >= late]:
                weights[d | bit] = send(weights[d], "chan", bit, chan)
            bit //= 2
    shares = [shares[0]] + [send(shares[d], "chan", d, chan) for d in range(1, chan)]

    mlp = pl.pallas_call(
        functools.partial(mlp_kernel, chan, min(512, hidden_width)),
        out_shape=[shape((rows, out_width), BF16)] + [shape((feat, rows), BF16)] * chan,
        in_specs=vmem(3 + 2 * chan),
        out_specs=vmem(1 + chan),
        scratch_shapes=[
            pltpu.VMEM((chan * feat, hidden_width), BF16),
            pltpu.VMEM((rows, chan * feat), BF16),
            pltpu.VMEM((rows, hidden_width), BF16),
        ],
        compiler_params=params(),
        name="mlp",
    )(bias.reshape(1, hidden_width), w_out, g_out, *shares, *[weights[d] for d in range(chan)])
    obs_part, grads = mlp[0], mlp[1:]
    grads = [grads[0]] + [send_back(grads[d], "chan", d, chan) for d in range(1, chan)]

    slots = pltpu.VMEM((dom * cap + 1, feat, blk), F32)
    slot_shape = shape((cap, feat, blk), BF16)
    rows_grad, *far_grads = pl.pallas_call(
        functools.partial(far_backward_kernel, plan, far, dom, cap, chan, blk, obs),
        out_shape=[shape((obs + 1, feat, blk), BF16)] + [slot_shape] * len(far),
        in_specs=smem(1) + vmem(1 + chan),
        out_specs=vmem(1 + len(far)),
        scratch_shapes=[slots],
        compiler_params=params(),
        name="far_backward",
    )(table, weight, *grads)
    returned = {d: send_back(value, "dom", d, dom) for d, value in zip(far, far_grads)}

    near_grads = pl.pallas_call(
        functools.partial(near_backward_kernel, plan, near, dom, cap),
        out_shape=[slot_shape] * len(near),
        in_specs=smem(1) + vmem(2),
        out_specs=vmem(len(near)),
        scratch_shapes=[slots],
        compiler_params=params(),
        name="near_backward",
    )(table, weight, rows_grad)
    returned[0] = near_grads[0]
    for d, value in zip(near[1:], near_grads[1:]):
        returned[d] = send_back(value, "dom", d, dom)

    obs_part = after(obs_part, near_grads[0])
    obs_parts = [obs_part] + [send(obs_part, "chan", d, chan) for d in range(1, chan)]

    local_grad = pl.pallas_call(
        functools.partial(local_backward_kernel, plan),
        out_shape=shape((nodes + 1, feat, blk), F32),
        in_specs=smem(1) + vmem(2),
        out_specs=pl.BlockSpec(memory_space=pltpu.VMEM),
        compiler_params=params(),
        name="local_backward",
    )(table, weight, after(rows_grad, near_grads[0]))

    obs_out = pl.pallas_call(
        functools.partial(rows_kernel, chan),
        out_shape=shape((obs_rows, out_width), BF16),
        in_specs=vmem(chan),
        out_specs=pl.BlockSpec(memory_space=pltpu.VMEM),
        compiler_params=params(),
        name="rows",
    )(*obs_parts)

    d_latent = pl.pallas_call(
        functools.partial(final_kernel, dom, cap, blk, nodes),
        out_shape=shape((feat, cols), BF16),
        in_specs=hbm(2) + vmem(1 + dom),
        out_specs=pl.BlockSpec(memory_space=pltpu.VMEM),
        scratch_shapes=[
            pltpu.VMEM((nodes, feat, blk), F32),
            pltpu.SMEM((cap, dom), i32),
            pltpu.SMEM((dom,), i32),
            pltpu.SemaphoreType.DMA((2,)),
        ],
        compiler_params=params(),
        name="final",
    )(*tables, local_grad, *[returned[d] for d in range(dom)])
    return obs_out, d_latent


def solution(mesh):
    return jax.shard_map(
        on_device,
        mesh=mesh,
        in_specs=(
            P("chan", "dom"),
            P("dom", None, None),
            P("dom", None),
            P("dom"),
            P("dom"),
            P("dom"),
            P("chan", None),
            P(),
            P(),
            P("dom", None),
        ),
        out_specs=(P("dom", None), P("chan", "dom")),
        check_vma=False,
    )
```

time: 85.8 us -> 67.5 us (0.79)
  waiting for transfers between devices: 20.1 us -> 10.8 us
  starting transfers between devices: 36.7 us -> 32.3 us
  local copies, waits for them, and re-layouts: 7.02 us -> 4.76 us
  Pallas kernels: 20.2 us -> 18.5 us
    ppermute x16, waiting for transfers between devices: 16.9 us -> 3.63 us  [send(): lax.ppermute(value, axis, [(i, target(i, shift, count)) for i in range(co...]
    ppermute x16, starting transfers between devices: 23.5 us -> 19 us  [send(): lax.ppermute(value, axis, [(i, target(i, shift, count)) for i in range(co...]
    ppermute x10, waiting for transfers between devices: 3.12 us -> 7.22 us  [send_back(): lax.ppermute(value, axis, [(target(i, shift, count), i) for i in range(co...]
    unnamed x29 -> x24, local copies, waits for them, and re-layouts: 7.02 us -> 4.76 us
    pallas_call x5 -> x8, Pallas kernels: 17.1 us -> 15.4 us  [the longest x1 4.41 us: on_device(): pl.pallas_call(functools.partial(local_forward_kernel, plan, dom, cap, bl...]
  transfers between devices with their start and end apart: 26 -> 26, of which waited for: 7 -> 6; matrix products, arithmetic and copies ran while one was open for 1% -> 0% of each run, Pallas kernels for 19% -> 15%
where the time goes in v2:
time: 67.5 us; the launch traced here: 67.2 us
  starting transfers between devices  32.3 us (48%)
  Pallas kernels  18.5 us (27%)
  waiting for transfers between devices  10.8 us (16%)
  local copies, waits for them, and re-layouts  4.76 us (7%)
  between operations  0.84 us (1%)
    ppermute x16, starting transfers between devices, send(): lax.ppermute(value, axis, [(i, target(i, shift, count)) for i in range(co...  19 us
    ppermute x10, starting transfers between devices, send_back(): lax.ppermute(value, axis, [(target(i, shift, count), i) for i in range(co...  13.3 us
    ppermute x10, waiting for transfers between devices, send_back(): lax.ppermute(value, axis, [(target(i, shift, count), i) for i in range(co...  7.22 us
    unnamed x24, local copies, waits for them, and re-layouts  4.76 us
    pallas_call x1, Pallas kernels, on_device(): pl.pallas_call(functools.partial(local_forward_kernel, plan, dom, cap, bl...  4.41 us
    ppermute x16, waiting for transfers between devices, send(): lax.ppermute(value, axis, [(i, target(i, shift, count)) for i in range(co...  3.63 us
    pallas_call x1, Pallas kernels, on_device(): pl.pallas_call(functools.partial(mlp_kernel, chan, min(512, hidden_width)...  2.33 us
    pallas_call x1, Pallas kernels, on_device(): pl.pallas_call(functools.partial(far_forward_kernel, plan, far, dom, cap,...  1.78 us
  transfers between devices with their start and end apart: 26, of which 6 were waited for; matrix products, arithmetic and copies ran while one was open for 0% of the time, Pallas kernels for 15%

profile of v2, /device:TPU:0, one launch (start us, length us, event | category | flops | bytes accessed | tf_op | source)
XLA Modules:
  0.0 67.2 jit_solution(11964482857677925859)
XLA Ops:
  0.6 1.0 %copy-done = bf16[128,2048]{1,0:T(8,128)(2,1)S(1)} copy-done((bf16[128,2048]{1,0:T(8,128)(2,1)S(1)}, bf16[128,2048]{1,0:T(8,128)(2,1)}, u32[]{:S(2)}) %copy-start) | copy-done | bytes 524312
  3.0 0.8 %pack.1 = (bf16[2,128,128]{2,1,0:T(8,128)(2,1)S(1)}, bf16[2,128,128]{2,1,0:T(8,128)(2,1)S(1)}, bf16[2,128,128]{2,1,0:T(8,128)(2,1)S(1)}, bf16[2,128,128]{2,1,0:T...) custom-call(s32[2,8]{1,0:T(2,128)S(1)} %bitcast.3, ...), custom_call_target="tpu_custom_call" | custom-call | tf_op jit(solution)/shard_map/pack/pallas_call | solution.py:335
  3.8 3.0 %collective-permute-start.11 = (bf16[128,2048]{1,0:T(8,128)(2,1)}, bf16[128,2048]{1,0:T(8,128)(2,1)S(1)}, u32[]{:S(2)}, u32[]{:S(2)}) collective-permute-start(bf16[128,2048]{1,0:T(8,128)(2,1)} %rest_4_), channel_id=1, source_target_pairs={{0,2},{1,3},{2,0},{3,1},{4,6},{5,7},{6,4},{7,5},{8,10},{9,11},{10,... | collective-permute-start | bytes 1572872 | tf_op jit(solution)/shard_map/ppermute | solution.py:30
  6.8 1.5 %collective-permute-start = (bf16[2,128,128]{2,1,0:T(8,128)(2,1)S(1)}, bf16[2,128,128]{2,1,0:T(8,128)(2,1)S(1)}, u32[]{:S(2)}, u32[]{:S(2)}) collective-permute-start(bf16[2,128,128]{2,1,0:T(8,128)(2,1)S(1)} %get-tuple-element.39), channel_id=1, source_target_pairs={{0,4},{4,0},{8,12},{12,8},{16,20},{20,16},{24,28},{28,24},{1,5},{5... | collective-permute-start | bytes 196616 | tf_op jit(solution)/shard_map/ppermute | solution.py:30
  8.3 1.6 %collective-permute-start.1 = (bf16[2,128,128]{2,1,0:T(8,128)(2,1)S(1)}, bf16[2,128,128]{2,1,0:T(8,128)(2,1)S(1)}, u32[]{:S(2)}, u32[]{:S(2)}) collective-permute-start(bf16[2,128,128]{2,1,0:T(8,128)(2,1)S(1)} %get-tuple-element.40), channel_id=1, source_target_pairs={{0,8},{4,12},{8,0},{12,4},{16,24},{20,28},{24,16},{28,20},{1,9},{5... | collective-permute-start | bytes 196616 | tf_op jit(solution)/shard_map/ppermute | solution.py:30
  10.3 2.6 %collective-permute-start.3 = (bf16[2,128,128]{2,1,0:T(8,128)(2,1)S(1)}, bf16[2,128,128]{2,1,0:T(8,128)(2,1)S(1)}, u32[]{:S(2)}, u32[]{:S(2)}) collective-permute-start(bf16[2,128,128]{2,1,0:T(8,128)(2,1)S(1)} %get-tuple-element.42), channel_id=1, source_target_pairs={{0,16},{4,20},{8,24},{12,28},{16,0},{20,4},{24,8},{28,12},{1,17},{... | collective-permute-start | bytes 196616 | tf_op jit(solution)/shard_map/ppermute | solution.py:30
  12.9 1.7 %collective-permute-start.4 = (bf16[2,128,128]{2,1,0:T(8,128)(2,1)S(1)}, bf16[2,128,128]{2,1,0:T(8,128)(2,1)S(1)}, u32[]{:S(2)}, u32[]{:S(2)}) collective-permute-start(bf16[2,128,128]{2,1,0:T(8,128)(2,1)S(1)} %get-tuple-element.43), channel_id=1, source_target_pairs={{0,20},{4,16},{8,28},{12,24},{16,4},{20,0},{24,12},{28,8},{1,21},{... | collective-permute-start | bytes 196616 | tf_op jit(solution)/shard_map/ppermute | solution.py:30
  14.6 3.2 %collective-permute-start.5 = (bf16[2,128,128]{2,1,0:T(8,128)(2,1)S(1)}, bf16[2,128,128]{2,1,0:T(8,128)(2,1)S(1)}, u32[]{:S(2)}, u32[]{:S(2)}) collective-permute-start(bf16[2,128,128]{2,1,0:T(8,128)(2,1)S(1)} %get-tuple-element.44), channel_id=1, source_target_pairs={{0,24},{4,28},{8,16},{12,20},{16,8},{20,12},{24,0},{28,4},{1,25},{... | collective-permute-start | bytes 196616 | tf_op jit(solution)/shard_map/ppermute | solution.py:30
  17.8 0.7 %collective-permute-start.6 = (bf16[2,128,128]{2,1,0:T(8,128)(2,1)S(1)}, bf16[2,128,128]{2,1,0:T(8,128)(2,1)S(1)}, u32[]{:S(2)}, u32[]{:S(2)}) collective-permute-start(bf16[2,128,128]{2,1,0:T(8,128)(2,1)S(1)} %get-tuple-element.45), channel_id=1, source_target_pairs={{0,28},{4,24},{8,20},{12,16},{16,12},{20,8},{24,4},{28,0},{1,29},{... | collective-permute-start | bytes 196616 | tf_op jit(solution)/shard_map/ppermute | solution.py:30
  18.5 1.0 %copy-done.1 = bf16[128,2048]{1,0:T(8,128)(2,1)S(1)} copy-done((bf16[128,2048]{1,0:T(8,128)(2,1)S(1)}, bf16[128,2048]{1,0:T(8,128)(2,1)}, u32[]{:S(2)}) %copy-start.1) | copy-done | bytes 524312
  20.8 4.4 %local_forward.1 = (f32[9,128,128]{2,1,0:T(8,128)S(1)}, s32[1443]{0:T(1024)S(1)}, bf16[128,128,128]{2,1,0:T(8,128)(2,1)S(1)}) custom-call(s32[128]{0:T(128)S(1)} %copy-done.10, s32[128]{0:T(128)S(1)} %copy-done.11, bf16[128,2048]{1,0:T(8,128)(2,1)S(1)} %copy-done.1, bf16[128,128,128]{2,1,0:T(8,128)(2,1)} %weight_hbm.1), custom_call_target="tpu_custom_call" | custom-call | tf_op jit(solution)/shard_map/local_forward/pallas_call | solution.py:367
  25.3 1.7 %near_forward.1.sum_ref = f32[9,128,128]{2,1,0:T(8,128)S(1)} custom-call(s32[1443]{0:T(1024)S(1)} %get-tuple-element.35.plan_ref, f32[9,128,128]{2,1,0:T(8,128)S(1)} %get-tuple-element.36.sum_ref, bf16[128,128,128]{2,1,0:T(8,128)(2,1)S(1)} %get-tuple-element.37.weight_ref, bf16[2,128,128]{2,1,0:T(8,128)(2,1)S(1)} %get-tuple-element.38.rest_0_, ...), custom_call_target="tpu_custom_call" | custom-call | tf_op jit(solution)/shard_map/near_forward/pallas_call | solution.py:388
  27.2 1.8 %far_forward.1 = (bf16[256,128]{1,0:T(8,128)(2,1)S(1)}, bf16[256,128]{1,0:T(8,128)(2,1)S(1)}, bf16[256,128]{1,0:T(8,128)(2,1)S(1)}, bf16[256,128]{1,0:T(8,128)(2,1)S(1)}) custom-call(s32[1443]{0:T(1024)S(1)} %get-tuple-element.35.plan_ref, f32[9,128,128]{2,1,0:T(8,128)S(1)} %near_forward.1.sum_ref, bf16[128,128,128]{2,1,0:T(8,128)(2,1)S(1)} %get-tuple-element.37.weight_ref, ...), custom_call_target="tpu_custom_call" | custom-call | tf_op jit(solution)/shard_map/far_forward/pallas_call | solution.py:398
  30.1 1.3 %collective-permute-start.9 = (bf16[256,128]{1,0:T(8,128)(2,1)S(1)}, bf16[256,128]{1,0:T(8,128)(2,1)S(1)}, u32[]{:S(2)}, u32[]{:S(2)}) collective-permute-start(bf16[256,128]{1,0:T(8,128)(2,1)S(1)} %get-tuple-element.49), channel_id=1, source_target_pairs={{0,3},{1,2},{2,1},{3,0},{4,7},{5,6},{6,5},{7,4},{8,11},{9,10},{10,... | collective-permute-start | bytes 196616 | tf_op jit(solution)/shard_map/ppermute | solution.py:30
  31.4 3.1 %collective-permute-done.8.rest_2_ = bf16[256,128]{1,0:T(8,128)(2,1)S(1)} collective-permute-done((bf16[256,128]{1,0:T(8,128)(2,1)S(1)}, bf16[256,128]{1,0:T(8,128)(2,1)S(1)}, u32[]{:S(2)}, u32[]{:S(2)}) %collective-permute-start.8) | collective-permute-done | bytes 65568 | tf_op jit(solution)/shard_map/ppermute | solution.py:30
  35.0 2.3 %mlp.1 = (bf16[256,128]{1,0:T(8,128)(2,1)S(1)}, bf16[128,256]{1,0:T(8,128)(2,1)S(1)}, bf16[128,256]{1,0:T(8,128)(2,1)S(1)}, bf16[128,256]{1,0:T(8,128)(2,1)S(1)}, bf16[128,256]{1,0:T(8,128)(2,1)S(1)}) custom-call(f32[1,2048]{1,0:T(1,128)S(1)} %bitcast.2, bf16[2048,128]{1,0:T(8,128)(2,1)S(1)} %copy-done.2, bf16[1024,128]{1,0:T(8,128)(2,1)S(1)} %copy-done.4, ...), custom_call_target="tpu_custom_call" | custom-call | tf_op jit(solution)/shard_map/mlp/pallas_call | solution.py:416
  38.3 1.0 %collective-permute-start.15 = (bf16[128,256]{1,0:T(8,128)(2,1)S(1)}, bf16[128,256]{1,0:T(8,128)(2,1)S(1)}, u32[]{:S(2)}, u32[]{:S(2)}) collective-permute-start(bf16[128,256]{1,0:T(8,128)(2,1)S(1)} %get-tuple-element.56), channel_id=1, source_target_pairs={{3,0},{2,1},{1,2},{0,3},{7,4},{6,5},{5,6},{4,7},{11,8},{10,9},{9,1... | collective-permute-start | bytes 196616 | tf_op jit(solution)/shard_map/ppermute | solution.py:34
  39.3 3.4 %collective-permute-done.14.rest_2_ = bf16[128,256]{1,0:T(8,128)(2,1)S(1)} collective-permute-done((bf16[128,256]{1,0:T(8,128)(2,1)S(1)}, bf16[128,256]{1,0:T(8,128)(2,1)S(1)}, u32[]{:S(2)}, u32[]{:S(2)}) %collective-permute-start.14) | collective-permute-done | bytes 65568 | tf_op jit(solution)/shard_map/ppermute | solution.py:34
  42.7 1.7 %far_backward.1 = (bf16[9,128,128]{2,1,0:T(8,128)(2,1)S(1)}, bf16[2,128,128]{2,1,0:T(8,128)(2,1)S(1)}, bf16[2,128,128]{2,1,0:T(8,128)(2,1)S(1)}, bf16[2,128,128]...) custom-call(s32[1443]{0:T(1024)S(1)} %get-tuple-element.35.plan_ref, bf16[128,128,128]{2,1,0:T(8,128)(2,1)S(1)} %get-tuple-element.37.weight_ref, ...), custom_call_target="tpu_custom_call" | custom-call | tf_op jit(solution)/shard_map/far_backward/pallas_call | solution.py:434
  44.4 1.7 %near_backward.1 = (bf16[2,128,128]{2,1,0:T(8,128)(2,1)S(1)}, bf16[2,128,128]{2,1,0:T(8,128)(2,1)S(1)}, bf16[2,128,128]{2,1,0:T(8,128)(2,1)S(1)}, bf16[2,128,128]{2,1,0:T(8,128)(2,1)S(1)}) custom-call(s32[1443]{0:T(1024)S(1)} %get-tuple-element.35.plan_ref, bf16[128,128,128]{2,1,0:T(8,128)(2,1)S(1)} %get-tuple-element.37.weight_ref, ...), custom_call_target="tpu_custom_call" | custom-call | tf_op jit(solution)/shard_map/near_backward/pallas_call | solution.py:445
  46.2 1.5 %collective-permute-start.19 = (bf16[2,128,128]{2,1,0:T(8,128)(2,1)S(1)}, bf16[2,128,128]{2,1,0:T(8,128)(2,1)S(1)}, u32[]{:S(2)}, u32[]{:S(2)}) collective-permute-start(bf16[2,128,128]{2,1,0:T(8,128)(2,1)S(1)} %get-tuple-element.61), channel_id=1, source_target_pairs={{4,0},{0,4},{12,8},{8,12},{20,16},{16,20},{28,24},{24,28},{5,1},{1... | collective-permute-start | bytes 196616 | tf_op jit(solution)/shard_map/ppermute | solution.py:34
  48.1 1.3 %collective-permute-start.17 = (bf16[256,128]{1,0:T(8,128)(2,1)S(1)}, bf16[256,128]{1,0:T(8,128)(2,1)S(1)}, u32[]{:S(2)}, u32[]{:S(2)}) collective-permute-start(bf16[256,128]{1,0:T(8,128)(2,1)S(1)} %get-tuple-element.59.rest_0_), channel_id=1, source_target_pairs={{0,2},{1,3},{2,0},{3,1},{4,6},{5,7},{6,4},{7,5},{8,10},{9,11},{10,... | collective-permute-start | bytes 196616 | tf_op jit(solution)/shard_map/ppermute | solution.py:30
  50.0 0.7 %collective-permute-done.19.rest_1_ = bf16[2,128,128]{2,1,0:T(8,128)(2,1)S(1)} collective-permute-done((bf16[2,128,128]{2,1,0:T(8,128)(2,1)S(1)}, bf16[2,128,128]{2,1,0:T(8,128)(2,1)S(1)}, u32[]{:S(2)}, u32[]{:S(2)}) %collective-permute-start.19) | collective-permute-done | bytes 65568 | tf_op jit(solution)/shard_map/ppermute | solution.py:34
  50.7 1.3 %collective-permute-start.21 = (bf16[2,128,128]{2,1,0:T(8,128)(2,1)S(1)}, bf16[2,128,128]{2,1,0:T(8,128)(2,1)S(1)}, u32[]{:S(2)}, u32[]{:S(2)}) collective-permute-start(bf16[2,128,128]{2,1,0:T(8,128)(2,1)S(1)} %get-tuple-element.63), channel_id=1, source_target_pairs={{12,0},{8,4},{4,8},{0,12},{28,16},{24,20},{20,24},{16,28},{13,1},{... | collective-permute-start | bytes 196616 | tf_op jit(solution)/shard_map/ppermute | solution.py:34
  52.1 3.2 %collective-permute-start.22 = (bf16[2,128,128]{2,1,0:T(8,128)(2,1)S(1)}, bf16[2,128,128]{2,1,0:T(8,128)(2,1)S(1)}, u32[]{:S(2)}, u32[]{:S(2)}) collective-permute-start(bf16[2,128,128]{2,1,0:T(8,128)(2,1)S(1)} %get-tuple-element.64), channel_id=1, source_target_pairs={{16,0},{20,4},{24,8},{28,12},{0,16},{4,20},{8,24},{12,28},{17,1},{... | collective-permute-start | bytes 196616 | tf_op jit(solution)/shard_map/ppermute | solution.py:34
  55.4 3.2 %collective-permute-start.24 = (bf16[2,128,128]{2,1,0:T(8,128)(2,1)S(1)}, bf16[2,128,128]{2,1,0:T(8,128)(2,1)S(1)}, u32[]{:S(2)}, u32[]{:S(2)}) collective-permute-start(bf16[2,128,128]{2,1,0:T(8,128)(2,1)S(1)} %get-tuple-element.66), channel_id=1, source_target_pairs={{24,0},{28,4},{16,8},{20,12},{8,16},{12,20},{0,24},{4,28},{25,1},{... | collective-permute-start | bytes 196616 | tf_op jit(solution)/shard_map/ppermute | solution.py:34
  58.5 1.6 %collective-permute-start.25 = (bf16[2,128,128]{2,1,0:T(8,128)(2,1)S(1)}, bf16[2,128,128]{2,1,0:T(8,128)(2,1)S(1)}, u32[]{:S(2)}, u32[]{:S(2)}) collective-permute-start(bf16[2,128,128]{2,1,0:T(8,128)(2,1)S(1)} %get-tuple-element.67), channel_id=1, source_target_pairs={{28,0},{24,4},{20,8},{16,12},{12,16},{8,20},{4,24},{0,28},{29,1},{... | collective-permute-start | bytes 196616 | tf_op jit(solution)/shard_map/ppermute | solution.py:34
  60.1 1.7 %local_backward.1.local_ref = f32[17,128,128]{2,1,0:T(8,128)S(1)} custom-call(s32[1443]{0:T(1024)S(1)} %get-tuple-element.35.plan_ref, bf16[128,128,128]{2,1,0:T(8,128)(2,1)S(1)} %get-tuple-element.37.weight_ref, bf16[9,128,128]{2,1,0:T(8,128)(2,1)S(1)} %get-tuple-element.60.rows_grad), custom_call_target="tpu_custom_call" | custom-call | tf_op jit(solution)/shard_map/local_backward/pallas_call | solution.py:461
  61.8 0.7 %rows.1 = bf16[1024,128]{1,0:T(8,128)(2,1)} custom-call(bf16[256,128]{1,0:T(8,128)(2,1)S(1)} %get-tuple-element.59.rest_0_, bf16[256,128]{1,0:T(8,128)(2,1)S(1)} %collective-permute-done.16.rest_1_, bf16[256,128]{1,0:T(8,128)(2,1)S(1)} %collective-permute-done.17.rest_2_, bf16[256,128]{1,0:T(8,128)(2,1)S(1)} %collective-permute-done.18.rest_3_), custom_call_target="tpu_custom_call" | custom-call | tf_op jit(solution)/shard_map/rows/pallas_call | solution.py:470
  62.5 1.7 %collective-permute-done.23.rest_5_ = bf16[2,128,128]{2,1,0:T(8,128)(2,1)S(1)} collective-permute-done((bf16[2,128,128]{2,1,0:T(8,128)(2,1)S(1)}, bf16[2,128,128]{2,1,0:T(8,128)(2,1)S(1)}, u32[]{:S(2)}, u32[]{:S(2)}) %collective-permute-start.23) | collective-permute-done | bytes 65568 | tf_op jit(solution)/shard_map/ppermute | solution.py:34
  64.3 1.3 %collective-permute-done.25.rest_7_ = bf16[2,128,128]{2,1,0:T(8,128)(2,1)S(1)} collective-permute-done((bf16[2,128,128]{2,1,0:T(8,128)(2,1)S(1)}, bf16[2,128,128]{2,1,0:T(8,128)(2,1)S(1)}, u32[]{:S(2)}, u32[]{:S(2)}) %collective-permute-start.25) | collective-permute-done | bytes 65568 | tf_op jit(solution)/shard_map/ppermute | solution.py:34
  65.6 1.6 %final.1 = bf16[128,2048]{1,0:T(8,128)(2,1)} custom-call(s32[2,8]{1,0:T(2,128)S(1)} %bitcast.4, s32[8]{0:T(128)S(1)} %copy-done.9, f32[17,128,128]{2,1,0:T(8,128)S(1)} %local_backward.1.local_ref, bf16[2,128,128]{2,1,0:T(8,128)(2,1)S(1)} %get-tuple-element.58.rest_0_, bf16[2,128,128]{2,1,0:T(8,128)(2,1)S(1)} %collective-permute-done.19.rest_1_, ...), custom_call_target="tpu_custom_call" | custom-call | tf_op jit(solution)/shard_map/final/pallas_call | solution.py:479
  (54 shorter events, 6.8 us)
Async XLA Ops:
  3.8 25.2 %collective-permute-start.11 = (bf16[128,2048]{1,0:T(8,128)(2,1)}, bf16[128,2048]{1,0:T(8,128)(2,1)S(1)}, u32[]{:S(2)}, u32[]{:S(2)}) collective-permute-start(bf16[128,2048]{1,0:T(8,128)(2,1)} %rest_4_), channel_id=1, source_target_pairs={{0,2},{1,3},{2,0},{3,1},{4,6},{5,7},{6,4},{7,5},{8,10},{9,11},{10,... | collective-permute-start | bytes 1572872 | tf_op jit(solution)/shard_map/ppermute | solution.py:30
  6.8 6.1 %collective-permute-start = (bf16[2,128,128]{2,1,0:T(8,128)(2,1)S(1)}, bf16[2,128,128]{2,1,0:T(8,128)(2,1)S(1)}, u32[]{:S(2)}, u32[]{:S(2)}) collective-permute-start(bf16[2,128,128]{2,1,0:T(8,128)(2,1)S(1)} %get-tuple-element.39), channel_id=1, source_target_pairs={{0,4},{4,0},{8,12},{12,8},{16,20},{20,16},{24,28},{28,24},{1,5},{5... | collective-permute-start | bytes 196616 | tf_op jit(solution)/shard_map/ppermute | solution.py:30
  8.3 6.3 %collective-permute-start.1 = (bf16[2,128,128]{2,1,0:T(8,128)(2,1)S(1)}, bf16[2,128,128]{2,1,0:T(8,128)(2,1)S(1)}, u32[]{:S(2)}, u32[]{:S(2)}) collective-permute-start(bf16[2,128,128]{2,1,0:T(8,128)(2,1)S(1)} %get-tuple-element.40), channel_id=1, source_target_pairs={{0,8},{4,12},{8,0},{12,4},{16,24},{20,28},{24,16},{28,20},{1,9},{5... | collective-permute-start | bytes 196616 | tf_op jit(solution)/shard_map/ppermute | solution.py:30
  9.9 7.9 %collective-permute-start.2 = (bf16[2,128,128]{2,1,0:T(8,128)(2,1)S(1)}, bf16[2,128,128]{2,1,0:T(8,128)(2,1)S(1)}, u32[]{:S(2)}, u32[]{:S(2)}) collective-permute-start(bf16[2,128,128]{2,1,0:T(8,128)(2,1)S(1)} %get-tuple-element.41), channel_id=1, source_target_pairs={{0,12},{4,8},{8,4},{12,0},{16,28},{20,24},{24,20},{28,16},{1,13},{... | collective-permute-start | bytes 196616 | tf_op jit(solution)/shard_map/ppermute | solution.py:30
  10.3 16.7 %collective-permute-start.3 = (bf16[2,128,128]{2,1,0:T(8,128)(2,1)S(1)}, bf16[2,128,128]{2,1,0:T(8,128)(2,1)S(1)}, u32[]{:S(2)}, u32[]{:S(2)}) collective-permute-start(bf16[2,128,128]{2,1,0:T(8,128)(2,1)S(1)} %get-tuple-element.42), channel_id=1, source_target_pairs={{0,16},{4,20},{8,24},{12,28},{16,0},{20,4},{24,8},{28,12},{1,17},{... | collective-permute-start | bytes 196616 | tf_op jit(solution)/shard_map/ppermute | solution.py:30
  12.9 14.2 %collective-permute-start.4 = (bf16[2,128,128]{2,1,0:T(8,128)(2,1)S(1)}, bf16[2,128,128]{2,1,0:T(8,128)(2,1)S(1)}, u32[]{:S(2)}, u32[]{:S(2)}) collective-permute-start(bf16[2,128,128]{2,1,0:T(8,128)(2,1)S(1)} %get-tuple-element.43), channel_id=1, source_target_pairs={{0,20},{4,16},{8,28},{12,24},{16,4},{20,0},{24,12},{28,8},{1,21},{... | collective-permute-start | bytes 196616 | tf_op jit(solution)/shard_map/ppermute | solution.py:30
  14.6 12.6 %collective-permute-start.5 = (bf16[2,128,128]{2,1,0:T(8,128)(2,1)S(1)}, bf16[2,128,128]{2,1,0:T(8,128)(2,1)S(1)}, u32[]{:S(2)}, u32[]{:S(2)}) collective-permute-start(bf16[2,128,128]{2,1,0:T(8,128)(2,1)S(1)} %get-tuple-element.44), channel_id=1, source_target_pairs={{0,24},{4,28},{8,16},{12,20},{16,8},{20,12},{24,0},{28,4},{1,25},{... | collective-permute-start | bytes 196616 | tf_op jit(solution)/shard_map/ppermute | solution.py:30
  17.8 9.4 %collective-permute-start.6 = (bf16[2,128,128]{2,1,0:T(8,128)(2,1)S(1)}, bf16[2,128,128]{2,1,0:T(8,128)(2,1)S(1)}, u32[]{:S(2)}, u32[]{:S(2)}) collective-permute-start(bf16[2,128,128]{2,1,0:T(8,128)(2,1)S(1)} %get-tuple-element.45), channel_id=1, source_target_pairs={{0,28},{4,24},{8,20},{12,16},{16,12},{20,8},{24,4},{28,0},{1,29},{... | collective-permute-start | bytes 196616 | tf_op jit(solution)/shard_map/ppermute | solution.py:30
  20.8 6.2 %copy-start.3 = (bf16[128,2048]{1,0:T(8,128)(2,1)S(1)}, bf16[128,2048]{1,0:T(8,128)(2,1)}, u32[]{:S(2)}) copy-start(bf16[128,2048]{1,0:T(8,128)(2,1)} %rest_4_) | copy-start | bytes 1572868
  25.3 9.7 %copy-start.2 = (bf16[2048,128]{1,0:T(8,128)(2,1)S(1)}, bf16[2048,128]{1,0:T(8,128)(2,1)}, u32[]{:S(2)}) copy-start(bf16[2048,128]{1,0:T(8,128)(2,1)} %w_out_ref.1) | copy-start | bytes 1572868
  25.3 9.7 %copy-start.4 = (bf16[1024,128]{1,0:T(8,128)(2,1)S(1)}, bf16[1024,128]{1,0:T(8,128)(2,1)}, u32[]{:S(2)}) copy-start(bf16[1024,128]{1,0:T(8,128)(2,1)} %g_ref.1) | copy-start | bytes 786436
  25.3 9.7 %copy-start.5 = (f32[2048]{0:T(1024)S(1)}, f32[2048]{0:T(1024)}, u32[]{:S(2)}) copy-start(f32[2048]{0:T(1024)} %param.17) | copy-start | bytes 24580
  27.1 7.9 %collective-permute-start.10 = (bf16[128,2048]{1,0:T(8,128)(2,1)S(1)}, bf16[128,2048]{1,0:T(8,128)(2,1)S(1)}, u32[]{:S(2)}, u32[]{:S(2)}) collective-permute-start(bf16[128,2048]{1,0:T(8,128)(2,1)S(1)} %copy-done.3), channel_id=1, source_target_pairs={{0,1},{1,0},{2,3},{3,2},{4,5},{5,4},{6,7},{7,6},{8,9},{9,8},{10,11... | collective-permute-start | bytes 1572872 | tf_op jit(solution)/shard_map/ppermute | solution.py:30
  29.0 6.0 %collective-permute-start.12 = (bf16[128,2048]{1,0:T(8,128)(2,1)S(1)}, bf16[128,2048]{1,0:T(8,128)(2,1)S(1)}, u32[]{:S(2)}, u32[]{:S(2)}) collective-permute-start(bf16[128,2048]{1,0:T(8,128)(2,1)S(1)} %collective-permute-done.11.rest_6_), channel_id=1, source_target_pairs={{0,1},{1,0},{2,3},{3,2},{4,5},{5,4},{6,7},{7,6},{8,9},{9,8},{10,11... | collective-permute-start | bytes 1572872 | tf_op jit(solution)/shard_map/ppermute | solution.py:30
  29.5 1.9 %collective-permute-start.7 = (bf16[256,128]{1,0:T(8,128)(2,1)S(1)}, bf16[256,128]{1,0:T(8,128)(2,1)S(1)}, u32[]{:S(2)}, u32[]{:S(2)}) collective-permute-start(bf16[256,128]{1,0:T(8,128)(2,1)S(1)} %get-tuple-element.47), channel_id=1, source_target_pairs={{0,1},{1,0},{2,3},{3,2},{4,5},{5,4},{6,7},{7,6},{8,9},{9,8},{10,11... | collective-permute-start | bytes 196616 | tf_op jit(solution)/shard_map/ppermute | solution.py:30
  29.6 4.9 %collective-permute-start.8 = (bf16[256,128]{1,0:T(8,128)(2,1)S(1)}, bf16[256,128]{1,0:T(8,128)(2,1)S(1)}, u32[]{:S(2)}, u32[]{:S(2)}) collective-permute-start(bf16[256,128]{1,0:T(8,128)(2,1)S(1)} %get-tuple-element.48), channel_id=1, source_target_pairs={{0,2},{1,3},{2,0},{3,1},{4,6},{5,7},{6,4},{7,5},{8,10},{9,11},{10,... | collective-permute-start | bytes 196616 | tf_op jit(solution)/shard_map/ppermute | solution.py:30
  30.1 4.9 %collective-permute-start.9 = (bf16[256,128]{1,0:T(8,128)(2,1)S(1)}, bf16[256,128]{1,0:T(8,128)(2,1)S(1)}, u32[]{:S(2)}, u32[]{:S(2)}) collective-permute-start(bf16[256,128]{1,0:T(8,128)(2,1)S(1)} %get-tuple-element.49), channel_id=1, source_target_pairs={{0,3},{1,2},{2,1},{3,0},{4,7},{5,6},{6,5},{7,4},{8,11},{9,10},{10,... | collective-permute-start | bytes 196616 | tf_op jit(solution)/shard_map/ppermute | solution.py:30
  37.4 1.9 %collective-permute-start.13 = (bf16[128,256]{1,0:T(8,128)(2,1)S(1)}, bf16[128,256]{1,0:T(8,128)(2,1)S(1)}, u32[]{:S(2)}, u32[]{:S(2)}) collective-permute-start(bf16[128,256]{1,0:T(8,128)(2,1)S(1)} %get-tuple-element.54), channel_id=1, source_target_pairs={{1,0},{0,1},{3,2},{2,3},{5,4},{4,5},{7,6},{6,7},{9,8},{8,9},{11,10... | collective-permute-start | bytes 196616 | tf_op jit(solution)/shard_map/ppermute | solution.py:34
  37.7 5.0 %collective-permute-start.14 = (bf16[128,256]{1,0:T(8,128)(2,1)S(1)}, bf16[128,256]{1,0:T(8,128)(2,1)S(1)}, u32[]{:S(2)}, u32[]{:S(2)}) collective-permute-start(bf16[128,256]{1,0:T(8,128)(2,1)S(1)} %get-tuple-element.55), channel_id=1, source_target_pairs={{2,0},{3,1},{0,2},{1,3},{6,4},{7,5},{4,6},{5,7},{10,8},{11,9},{8,1... | collective-permute-start | bytes 196616 | tf_op jit(solution)/shard_map/ppermute | solution.py:34
  38.3 4.4 %collective-permute-start.15 = (bf16[128,256]{1,0:T(8,128)(2,1)S(1)}, bf16[128,256]{1,0:T(8,128)(2,1)S(1)}, u32[]{:S(2)}, u32[]{:S(2)}) collective-permute-start(bf16[128,256]{1,0:T(8,128)(2,1)S(1)} %get-tuple-element.56), channel_id=1, source_target_pairs={{3,0},{2,1},{1,2},{0,3},{7,4},{6,5},{5,6},{4,7},{11,8},{10,9},{9,1... | collective-permute-start | bytes 196616 | tf_op jit(solution)/shard_map/ppermute | solution.py:34
  46.1 19.5 %copy-start.7 = (s32[8,2]{0,1:T(2,128)S(1)}, s32[8,2]{0,1:T(2,128)}, u32[]{:S(2)}) copy-start(s32[8,2]{0,1:T(2,128)} %param.12) | copy-start | bytes 196
  46.1 19.5 %copy-start.9 = (s32[8]{0:T(128)S(1)}, s32[8]{0:T(128)}, u32[]{:S(2)}) copy-start(s32[8]{0:T(128)} %counts_hbm.3) | copy-start | bytes 100
  46.2 4.6 %collective-permute-start.19 = (bf16[2,128,128]{2,1,0:T(8,128)(2,1)S(1)}, bf16[2,128,128]{2,1,0:T(8,128)(2,1)S(1)}, u32[]{:S(2)}, u32[]{:S(2)}) collective-permute-start(bf16[2,128,128]{2,1,0:T(8,128)(2,1)S(1)} %get-tuple-element.61), channel_id=1, source_target_pairs={{4,0},{0,4},{12,8},{8,12},{20,16},{16,20},{28,24},{24,28},{5,1},{1... | collective-permute-start | bytes 196616 | tf_op jit(solution)/shard_map/ppermute | solution.py:34
  47.6 4.4 %collective-permute-start.20 = (bf16[2,128,128]{2,1,0:T(8,128)(2,1)S(1)}, bf16[2,128,128]{2,1,0:T(8,128)(2,1)S(1)}, u32[]{:S(2)}, u32[]{:S(2)}) collective-permute-start(bf16[2,128,128]{2,1,0:T(8,128)(2,1)S(1)} %get-tuple-element.62), channel_id=1, source_target_pairs={{8,0},{12,4},{0,8},{4,12},{24,16},{28,20},{16,24},{20,28},{9,1},{1... | collective-permute-start | bytes 196616 | tf_op jit(solution)/shard_map/ppermute | solution.py:34
  48.1 7.2 %collective-permute-start.16 = (bf16[256,128]{1,0:T(8,128)(2,1)S(1)}, bf16[256,128]{1,0:T(8,128)(2,1)S(1)}, u32[]{:S(2)}, u32[]{:S(2)}) collective-permute-start(bf16[256,128]{1,0:T(8,128)(2,1)S(1)} %get-tuple-element.59.rest_0_), channel_id=1, source_target_pairs={{0,1},{1,0},{2,3},{3,2},{4,5},{5,4},{6,7},{7,6},{8,9},{9,8},{10,11... | collective-permute-start | bytes 196616 | tf_op jit(solution)/shard_map/ppermute | solution.py:30
  48.1 7.2 %collective-permute-start.17 = (bf16[256,128]{1,0:T(8,128)(2,1)S(1)}, bf16[256,128]{1,0:T(8,128)(2,1)S(1)}, u32[]{:S(2)}, u32[]{:S(2)}) collective-permute-start(bf16[256,128]{1,0:T(8,128)(2,1)S(1)} %get-tuple-element.59.rest_0_), channel_id=1, source_target_pairs={{0,2},{1,3},{2,0},{3,1},{4,6},{5,7},{6,4},{7,5},{8,10},{9,11},{10,... | collective-permute-start | bytes 196616 | tf_op jit(solution)/shard_map/ppermute | solution.py:30
  49.4 9.1 %collective-permute-start.18 = (bf16[256,128]{1,0:T(8,128)(2,1)S(1)}, bf16[256,128]{1,0:T(8,128)(2,1)S(1)}, u32[]{:S(2)}, u32[]{:S(2)}) collective-permute-start(bf16[256,128]{1,0:T(8,128)(2,1)S(1)} %get-tuple-element.59.rest_0_), channel_id=1, source_target_pairs={{0,3},{1,2},{2,1},{3,0},{4,7},{5,6},{6,5},{7,4},{8,11},{9,10},{10,... | collective-permute-start | bytes 196616 | tf_op jit(solution)/shard_map/ppermute | solution.py:30
  50.7 11.8 %collective-permute-start.21 = (bf16[2,128,128]{2,1,0:T(8,128)(2,1)S(1)}, bf16[2,128,128]{2,1,0:T(8,128)(2,1)S(1)}, u32[]{:S(2)}, u32[]{:S(2)}) collective-permute-start(bf16[2,128,128]{2,1,0:T(8,128)(2,1)S(1)} %get-tuple-element.63), channel_id=1, source_target_pairs={{12,0},{8,4},{4,8},{0,12},{28,16},{24,20},{20,24},{16,28},{13,1},{... | collective-permute-start | bytes 196616 | tf_op jit(solution)/shard_map/ppermute | solution.py:34
  52.1 10.4 %collective-permute-start.22 = (bf16[2,128,128]{2,1,0:T(8,128)(2,1)S(1)}, bf16[2,128,128]{2,1,0:T(8,128)(2,1)S(1)}, u32[]{:S(2)}, u32[]{:S(2)}) collective-permute-start(bf16[2,128,128]{2,1,0:T(8,128)(2,1)S(1)} %get-tuple-element.64), channel_id=1, source_target_pairs={{16,0},{20,4},{24,8},{28,12},{0,16},{4,20},{8,24},{12,28},{17,1},{... | collective-permute-start | bytes 196616 | tf_op jit(solution)/shard_map/ppermute | solution.py:34
  55.3 8.9 %collective-permute-start.23 = (bf16[2,128,128]{2,1,0:T(8,128)(2,1)S(1)}, bf16[2,128,128]{2,1,0:T(8,128)(2,1)S(1)}, u32[]{:S(2)}, u32[]{:S(2)}) collective-permute-start(bf16[2,128,128]{2,1,0:T(8,128)(2,1)S(1)} %get-tuple-element.65), channel_id=1, source_target_pairs={{20,0},{16,4},{28,8},{24,12},{4,16},{0,20},{12,24},{8,28},{21,1},{... | collective-permute-start | bytes 196616 | tf_op jit(solution)/shard_map/ppermute | solution.py:34
  55.4 8.9 %collective-permute-start.24 = (bf16[2,128,128]{2,1,0:T(8,128)(2,1)S(1)}, bf16[2,128,128]{2,1,0:T(8,128)(2,1)S(1)}, u32[]{:S(2)}, u32[]{:S(2)}) collective-permute-start(bf16[2,128,128]{2,1,0:T(8,128)(2,1)S(1)} %get-tuple-element.66), channel_id=1, source_target_pairs={{24,0},{28,4},{16,8},{20,12},{8,16},{12,20},{0,24},{4,28},{25,1},{... | collective-permute-start | bytes 196616 | tf_op jit(solution)/shard_map/ppermute | solution.py:34
  58.5 7.1 %collective-permute-start.25 = (bf16[2,128,128]{2,1,0:T(8,128)(2,1)S(1)}, bf16[2,128,128]{2,1,0:T(8,128)(2,1)S(1)}, u32[]{:S(2)}, u32[]{:S(2)}) collective-permute-start(bf16[2,128,128]{2,1,0:T(8,128)(2,1)S(1)} %get-tuple-element.67), channel_id=1, source_target_pairs={{28,0},{24,4},{20,8},{16,12},{12,16},{8,20},{4,24},{0,28},{29,1},{... | collective-permute-start | bytes 196616 | tf_op jit(solution)/shard_map/ppermute | solution.py:34
  (6 other events, 4.7 us)

commit v3 on v2

--- a/solution.py
+++ b/solution.py
@@ -44,6 +44,14 @@
 
 def hbm(count):
     return [pl.BlockSpec(memory_space=pltpu.HBM)] * count
+
+
+def in_hbm(*values):
+    return [pltpu.with_memory_space_constraint(v, pltpu.HBM) for v in values]
+
+
+def cost(products):
+    return pl.CostEstimate(flops=products * 2**24, bytes_accessed=2**10, transcendentals=0)
 
 
 def params():
@@ -88,24 +96,19 @@
 
     def make(self, ref, src_ref, obs_ref, nodes, obs, dom, cap):
         me = lax.axis_index("dom")
-        near_of = [
-            functools.reduce(
-                jnp.logical_or, [source(me, d, dom) == p for d in range(dom) if is_near(d, dom)]
-            ).astype(jnp.int32)
-            for p in range(dom)
-        ]
-        near_bits = None
-        if dom <= 16:
-            near_bits = sum(near_of[p] << p for p in range(dom))
+        mask = None
+        if dom * cap <= 31:
+            bits = (1 << cap) - 1
+            mask = sum(bits << (source(me, d, dom) * cap) for d in range(dom) if is_near(d, dom))
 
         def one(e, counts):
             src = src_ref[e]
             slot = jnp.maximum(src - nodes, 0)
-            p = slot // cap
-            if near_bits is not None:
-                near = (near_bits >> p) & 1
+            if mask is not None:
+                near = lax.shift_right_logical(mask, slot) & 1
             else:
-                near = is_near(lax.rem(me - p + dom, dom), dom).astype(jnp.int32)
+                shift = lax.rem(me - lax.div(slot, cap) + dom, dom)
+                near = is_near(shift, dom).astype(jnp.int32)
             local = (src < nodes).astype(jnp.int32)
             near = (1 - local) * near
             far = 1 - local - near
@@ -144,10 +147,12 @@
         lax.fori_loop(0, (count + UNROLL - 1) // UNROLL, step, 0)
 
 
-def local_forward_kernel(
-    plan, dom, cap, blk, nodes, obs, src_hbm, obs_hbm, latent_hbm, weight_hbm, sum_ref, plan_ref, weight_ref, *rest
+def first_forward_kernel(
+    plan, shifts, dom, cap, blk, nodes, obs, src_hbm, obs_hbm, latent_hbm, weight_hbm, *rest
 ):
-    src_ref, obs_ref, latent_ref, pool, sems = rest
+    count = len(shifts)
+    arrived, (sum_ref, plan_ref, weight_ref) = rest[:count], rest[count : count + 3]
+    src_ref, obs_ref, latent_ref, pool, slots, sems = rest[count + 3 :]
     pairs = (
         (src_hbm, src_ref),
         (obs_hbm, obs_ref),
@@ -155,19 +160,20 @@
         (weight_hbm, weight_ref),
     )
     copies = fetch(pairs, sems)
+    sum_ref[...] = jnp.zeros_like(sum_ref)
     copies[0].wait()
     copies[1].wait()
     plan.make(plan_ref, src_ref, obs_ref, nodes, obs, dom, cap)
     copies[2].wait()
     for k in range(nodes):
         pool[k] = latent_ref[:, k * blk : (k + 1) * blk].T
-    sum_ref[...] = jnp.zeros_like(sum_ref)
     copies[3].wait()
 
     def body(e, k, j):
         sum_ref[j] += lax.dot_general(weight_ref[e], pool[k], NN, preferred_element_type=F32)
 
     plan.run(plan_ref, 0, body)
+    add_slots(plan, 1, shifts, dom, cap, plan_ref, weight_ref, arrived, slots, sum_ref)
 
 
 def add_slots(plan, kind, shifts, dom, cap, plan_ref, weight_ref, arrived, pool, total):
@@ -181,12 +187,6 @@
         total[j] += lax.dot_general(weight_ref[e], pool[k], NN, preferred_element_type=F32)
 
     plan.run(plan_ref, kind, body)
-
-
-def near_forward_kernel(plan, shifts, dom, cap, plan_ref, sum_ref, weight_ref, *rest):
-    arrived, (out_ref, pool) = rest[: len(shifts)], rest[len(shifts) :]
-    out_ref[...] = sum_ref[...]
-    add_slots(plan, 1, shifts, dom, cap, plan_ref, weight_ref, arrived, pool, out_ref)
 
 
 def far_forward_kernel(plan, shifts, dom, cap, chan, plan_ref, sum_ref, weight_ref, *rest):
@@ -268,12 +268,9 @@
     slot_gradients(plan, 2, shifts, dom, cap, plan_ref, weight_ref, rows_grad, outs, total)
 
 
-def near_backward_kernel(plan, shifts, dom, cap, plan_ref, weight_ref, rows_grad, *rest):
-    *outs, total = rest
-    slot_gradients(plan, 1, shifts, dom, cap, plan_ref, weight_ref, rows_grad, outs, total)
-
-
-def local_backward_kernel(plan, plan_ref, weight_ref, rows_grad, total):
+def rest_backward_kernel(plan, shifts, dom, cap, plan_ref, weight_ref, rows_grad, *rest):
+    *outs, total, slots = rest
+    slot_gradients(plan, 1, shifts, dom, cap, plan_ref, weight_ref, rows_grad, outs, slots)
     total[...] = jnp.zeros_like(total)
 
     def body(e, k, j):
@@ -291,19 +288,20 @@
         obs_ref[pl.ds(start, rows), :] = parts[d][...]
 
 
-def final_kernel(dom, cap, blk, nodes, blocks_hbm, counts_hbm, local_ref, *rest):
-    returned, (grad_ref, total, blocks_ref, counts_ref, sems) = rest[:dom], rest[dom:]
-    copies = fetch(((blocks_hbm, blocks_ref), (counts_hbm, counts_ref)), sems)
-    total[...] = local_ref[:nodes]
-    for copy in copies:
-        copy.wait()
+def add_returned(shifts, dom, cap, nodes, blocks_ref, counts_ref, returned, total):
     me = lax.axis_index("dom")
-    for d in range(dom):
+    for d, values in zip(shifts, returned):
         q = target(me, d, dom)
         for s in range(cap):
-            value = returned[d][s].astype(F32)
+            value = values[s].astype(F32)
             value = jnp.where(s < counts_ref[q], value, jnp.zeros_like(value))
             total[jnp.clip(blocks_ref[s, q], 0, nodes - 1)] += value
+
+
+def final_kernel(dom, cap, blk, nodes, blocks_ref, counts_ref, local_ref, *rest):
+    returned, (grad_ref, total) = rest[:dom], rest[dom:]
+    total[...] = local_ref[:nodes]
+    add_returned(range(dom), dom, cap, nodes, blocks_ref, counts_ref, returned, total)
     for k in range(nodes):
         grad_ref[:, k * blk : (k + 1) * blk] = total[k].astype(BF16)
 
@@ -345,55 +343,40 @@
         ],
         compiler_params=params(),
         name="pack",
-    )(*tables, latent)
+    )(*in_hbm(*tables, latent))
     arrived = {0: outgoing[0]}
-    for d in far + near[1:]:
+    for d in near[1:] + far:
         arrived[d] = send(outgoing[d], "dom", d, dom)
-
-    w_mine = after(w_in, outgoing[0])
-    weights = {0: w_mine}
+    weights = {0: after(w_in, outgoing[0])}
     late = chan // 2 if chan & (chan - 1) == 0 else 0
     if late:
-        weights[late] = send(w_mine, "chan", late, chan)
-        bit = late // 2
-        while bit:
-            for d in [d for d in sorted(weights) if d < late]:
-                weights[d | bit] = send(weights[d], "chan", bit, chan)
-            bit //= 2
+        weights[late] = send(weights[0], "chan", late, chan)
     else:
         for d in range(1, chan):
-            weights[d] = send(w_mine, "chan", d, chan)
-
-    local_sum, table, weight = pl.pallas_call(
-        functools.partial(local_forward_kernel, plan, dom, cap, blk, nodes, obs),
+            weights[d] = send(weights[0], "chan", d, chan)
+
+    pool = pltpu.VMEM((dom * cap + 1, blk, feat), BF16)
+    first_sum, table, weight = pl.pallas_call(
+        functools.partial(first_forward_kernel, plan, near, dom, cap, blk, nodes, obs),
         out_shape=[
             shape((obs + 1, blk, feat), F32),
             shape((plan.size(),), i32),
             shape(edge_weight.shape, BF16),
         ],
-        in_specs=hbm(4),
+        in_specs=hbm(4) + vmem(len(near)),
         out_specs=vmem(1) + smem(1) + vmem(1),
         scratch_shapes=[
             pltpu.SMEM((edges,), i32),
             pltpu.SMEM((edges,), i32),
             pltpu.VMEM((feat, cols), BF16),
             pltpu.VMEM((nodes + 1, blk, feat), BF16),
+            pool,
             pltpu.SemaphoreType.DMA((4,)),
         ],
         compiler_params=params(),
-        name="local_forward",
-    )(edge_src, edge_obs, latent, edge_weight)
-
-    pool = pltpu.VMEM((dom * cap + 1, blk, feat), BF16)
-    near_sum = pl.pallas_call(
-        functools.partial(near_forward_kernel, plan, near, dom, cap),
-        out_shape=shape((obs + 1, blk, feat), F32),
-        in_specs=smem(1) + vmem(2 + len(near)),
-        out_specs=pl.BlockSpec(memory_space=pltpu.VMEM),
-        scratch_shapes=[pool],
-        compiler_params=params(),
-        name="near_forward",
-    )(table, local_sum, weight, *[arrived[d] for d in near])
+        cost_estimate=cost(edges),
+        name="first_forward",
+    )(*in_hbm(edge_src, edge_obs, latent, edge_weight), *[arrived[d] for d in near])
 
     shares = pl.pallas_call(
         functools.partial(far_forward_kernel, plan, far, dom, cap, chan),
@@ -403,12 +386,13 @@
         scratch_shapes=[pool, pltpu.VMEM((obs + 1, blk, feat), F32)],
         compiler_params=params(),
         name="far_forward",
-    )(table, near_sum, weight, *[arrived[d] for d in far])
+    )(table, first_sum, weight, *[arrived[d] for d in far])
     if late:
+        weights[0] = after(weights[0], first_sum)
         weights[late] = after(weights[late], shares[0])
         bit = late // 2
         while bit:
-            for d in [d for d in sorted(weights) if d >= late]:
+            for d in sorted(weights):
                 weights[d | bit] = send(weights[d], "chan", bit, chan)
             bit //= 2
     shares = [shares[0]] + [send(shares[d], "chan", d, chan) for d in range(1, chan)]
@@ -441,32 +425,25 @@
         name="far_backward",
     )(table, weight, *grads)
     returned = {d: send_back(value, "dom", d, dom) for d, value in zip(far, far_grads)}
-
-    near_grads = pl.pallas_call(
-        functools.partial(near_backward_kernel, plan, near, dom, cap),
-        out_shape=[slot_shape] * len(near),
+    obs_part = after(obs_part, rows_grad)
+    obs_parts = [obs_part, send(obs_part, "chan", 1, chan)]
+
+    *near_grads, local_grad = pl.pallas_call(
+        functools.partial(rest_backward_kernel, plan, near, dom, cap),
+        out_shape=[slot_shape] * len(near) + [shape((nodes + 1, feat, blk), F32)],
         in_specs=smem(1) + vmem(2),
-        out_specs=vmem(len(near)),
+        out_specs=vmem(len(near) + 1),
         scratch_shapes=[slots],
         compiler_params=params(),
-        name="near_backward",
-    )(table, weight, rows_grad)
+        cost_estimate=cost(edges),
+        name="rest_backward",
+    )(table, weight, after(rows_grad, obs_parts[1]))
     returned[0] = near_grads[0]
     for d, value in zip(near[1:], near_grads[1:]):
         returned[d] = send_back(value, "dom", d, dom)
 
-    obs_part = after(obs_part, near_grads[0])
-    obs_parts = [obs_part] + [send(obs_part, "chan", d, chan) for d in range(1, chan)]
-
-    local_grad = pl.pallas_call(
-        functools.partial(local_backward_kernel, plan),
-        out_shape=shape((nodes + 1, feat, blk), F32),
-        in_specs=smem(1) + vmem(2),
-        out_specs=pl.BlockSpec(memory_space=pltpu.VMEM),
-        compiler_params=params(),
-        name="local_backward",
-    )(table, weight, after(rows_grad, near_grads[0]))
-
+    obs_part = after(obs_part, local_grad)
+    obs_parts += [send(obs_part, "chan", d, chan) for d in range(2, chan)]
     obs_out = pl.pallas_call(
         functools.partial(rows_kernel, chan),
         out_shape=shape((obs_rows, out_width), BF16),
@@ -479,14 +456,9 @@
     d_latent = pl.pallas_call(
         functools.partial(final_kernel, dom, cap, blk, nodes),
         out_shape=shape((feat, cols), BF16),
-        in_specs=hbm(2) + vmem(1 + dom),
+        in_specs=smem(2) + vmem(1 + dom),
         out_specs=pl.BlockSpec(memory_space=pltpu.VMEM),
-        scratch_shapes=[
-            pltpu.VMEM((nodes, feat, blk), F32),
-            pltpu.SMEM((cap, dom), i32),
-            pltpu.SMEM((dom,), i32),
-            pltpu.SemaphoreType.DMA((2,)),
-        ],
+        scratch_shapes=[pltpu.VMEM((nodes, feat, blk), F32)],
         compiler_params=params(),
         name="final",
     )(*tables, local_grad, *[returned[d] for d in range(dom)])

time: 67.5 us -> 62.1 us (0.920)
  local copies, waits for them, and re-layouts: 4.76 us -> 0.03 us
  waiting for transfers between devices: 10.8 us -> 11.9 us
  Pallas kernels: 18.5 us -> 17.6 us
    unnamed x24 -> x12, local copies, waits for them, and re-layouts: 4.76 us -> 0.03 us
    pallas_call x4 -> x2, Pallas kernels: 9.51 us -> 8.03 us  [the longest x1 5.31 us: on_device(): pl.pallas_call(functools.partial(first_forward_kernel, plan, near, dom, c...]
    ppermute x16, starting transfers between devices: 19 us -> 18.2 us  [send(): lax.ppermute(value, axis, [(i, target(i, shift, count)) for i in range(co...]
    ppermute x16, waiting for transfers between devices: 3.63 us -> 4.38 us  [send(): lax.ppermute(value, axis, [(i, target(i, shift, count)) for i in range(co...]
  transfers between devices with their start and end apart: 26 -> 26, of which waited for: 6 -> 8; matrix products, arithmetic and copies ran while one was open for 0% -> 0% of each run, Pallas kernels for 15% -> 17%
where the time goes in v3:
time: 62.1 us; the launch traced here: 62 us
  starting transfers between devices  31.7 us (51%)
  Pallas kernels  17.6 us (28%)
  waiting for transfers between devices  11.9 us (19%)
  between operations  0.81 us (1%)
    ppermute x16, starting transfers between devices, send(): lax.ppermute(value, axis, [(i, target(i, shift, count)) for i in range(co...  18.2 us
    ppermute x10, starting transfers between devices, send_back(): lax.ppermute(value, axis, [(target(i, shift, count), i) for i in range(co...  13.5 us
    ppermute x10, waiting for transfers between devices, send_back(): lax.ppermute(value, axis, [(target(i, shift, count), i) for i in range(co...  7.51 us
    pallas_call x1, Pallas kernels, on_device(): pl.pallas_call(functools.partial(first_forward_kernel, plan, near, dom, c...  5.31 us
    ppermute x16, waiting for transfers between devices, send(): lax.ppermute(value, axis, [(i, target(i, shift, count)) for i in range(co...  4.38 us
    pallas_call x1, Pallas kernels, on_device(): pl.pallas_call(functools.partial(rest_backward_kernel, plan, near, dom, c...  2.72 us
    pallas_call x1, Pallas kernels, on_device(): pl.pallas_call(functools.partial(mlp_kernel, chan, min(512, hidden_width)...  2.33 us
    pallas_call x1, Pallas kernels, on_device(): pl.pallas_call(functools.partial(far_forward_kernel, plan, far, dom, cap,...  1.77 us
  transfers between devices with their start and end apart: 26, of which 8 were waited for; matrix products, arithmetic and copies ran while one was open for 0% of the time, Pallas kernels for 17%

profile of v3, /device:TPU:0, one launch (start us, length us, event | category | flops | bytes accessed | tf_op | source)
XLA Modules:
  0.0 62.0 jit_solution(7984260910403199039)
XLA Ops:
  0.6 1.3 %pack.1 = (bf16[2,128,128]{2,1,0:T(8,128)(2,1)S(1)}, bf16[2,128,128]{2,1,0:T(8,128)(2,1)S(1)}, bf16[2,128,128]{2,1,0:T(8,128)(2,1)S(1)}, bf16[2,128,128]{2,1,0:T...) custom-call(s32[2,8]{1,0:T(2,128)} %bitcast.3, ...), custom_call_target="tpu_custom_call" | custom-call | tf_op jit(solution)/shard_map/pack/pallas_call | solution.py:333
  2.0 3.0 %collective-permute-start.11 = (bf16[128,2048]{1,0:T(8,128)(2,1)}, bf16[128,2048]{1,0:T(8,128)(2,1)S(1)}, u32[]{:S(2)}, u32[]{:S(2)}) collective-permute-start(bf16[128,2048]{1,0:T(8,128)(2,1)} %rest_4_), channel_id=1, source_target_pairs={{0,2},{1,3},{2,0},{3,1},{4,6},{5,7},{6,4},{7,5},{8,10},{9,11},{10,... | collective-permute-start | bytes 1572872 | tf_op jit(solution)/shard_map/ppermute | solution.py:30
  5.0 1.5 %collective-permute-start = (bf16[2,128,128]{2,1,0:T(8,128)(2,1)S(1)}, bf16[2,128,128]{2,1,0:T(8,128)(2,1)S(1)}, u32[]{:S(2)}, u32[]{:S(2)}) collective-permute-start(bf16[2,128,128]{2,1,0:T(8,128)(2,1)S(1)} %get-tuple-element.39), channel_id=1, source_target_pairs={{0,4},{4,0},{8,12},{12,8},{16,20},{20,16},{24,28},{28,24},{1,5},{5... | collective-permute-start | bytes 196616 | tf_op jit(solution)/shard_map/ppermute | solution.py:30
  6.5 1.6 %collective-permute-start.1 = (bf16[2,128,128]{2,1,0:T(8,128)(2,1)S(1)}, bf16[2,128,128]{2,1,0:T(8,128)(2,1)S(1)}, u32[]{:S(2)}, u32[]{:S(2)}) collective-permute-start(bf16[2,128,128]{2,1,0:T(8,128)(2,1)S(1)} %get-tuple-element.40), channel_id=1, source_target_pairs={{0,8},{4,12},{8,0},{12,4},{16,24},{20,28},{24,16},{28,20},{1,9},{5... | collective-permute-start | bytes 196616 | tf_op jit(solution)/shard_map/ppermute | solution.py:30
  8.5 2.6 %collective-permute-start.3 = (bf16[2,128,128]{2,1,0:T(8,128)(2,1)S(1)}, bf16[2,128,128]{2,1,0:T(8,128)(2,1)S(1)}, u32[]{:S(2)}, u32[]{:S(2)}) collective-permute-start(bf16[2,128,128]{2,1,0:T(8,128)(2,1)S(1)} %get-tuple-element.45), channel_id=1, source_target_pairs={{0,16},{4,20},{8,24},{12,28},{16,0},{20,4},{24,8},{28,12},{1,17},{... | collective-permute-start | bytes 196616 | tf_op jit(solution)/shard_map/ppermute | solution.py:30
  11.1 1.7 %collective-permute-start.4 = (bf16[2,128,128]{2,1,0:T(8,128)(2,1)S(1)}, bf16[2,128,128]{2,1,0:T(8,128)(2,1)S(1)}, u32[]{:S(2)}, u32[]{:S(2)}) collective-permute-start(bf16[2,128,128]{2,1,0:T(8,128)(2,1)S(1)} %get-tuple-element.46), channel_id=1, source_target_pairs={{0,20},{4,16},{8,28},{12,24},{16,4},{20,0},{24,12},{28,8},{1,21},{... | collective-permute-start | bytes 196616 | tf_op jit(solution)/shard_map/ppermute | solution.py:30
  12.8 3.2 %collective-permute-start.5 = (bf16[2,128,128]{2,1,0:T(8,128)(2,1)S(1)}, bf16[2,128,128]{2,1,0:T(8,128)(2,1)S(1)}, u32[]{:S(2)}, u32[]{:S(2)}) collective-permute-start(bf16[2,128,128]{2,1,0:T(8,128)(2,1)S(1)} %get-tuple-element.47), channel_id=1, source_target_pairs={{0,24},{4,28},{8,16},{12,20},{16,8},{20,12},{24,0},{28,4},{1,25},{... | collective-permute-start | bytes 196616 | tf_op jit(solution)/shard_map/ppermute | solution.py:30
  15.9 0.7 %collective-permute-start.6 = (bf16[2,128,128]{2,1,0:T(8,128)(2,1)S(1)}, bf16[2,128,128]{2,1,0:T(8,128)(2,1)S(1)}, u32[]{:S(2)}, u32[]{:S(2)}) collective-permute-start(bf16[2,128,128]{2,1,0:T(8,128)(2,1)S(1)} %get-tuple-element.48), channel_id=1, source_target_pairs={{0,28},{4,24},{8,20},{12,16},{16,12},{20,8},{24,4},{28,0},{1,29},{... | collective-permute-start | bytes 196616 | tf_op jit(solution)/shard_map/ppermute | solution.py:30
  16.7 5.3 %first_forward.1 = (f32[9,128,128]{2,1,0:T(8,128)S(1)}, s32[1443]{0:T(1024)S(1)}, bf16[128,128,128]{2,1,0:T(8,128)(2,1)S(1)}) custom-call(s32[128]{0:T(128)} %src_hbm.1, s32[128]{0:T(128)} %obs_hbm.1, bf16[128,2048]{1,0:T(8,128)(2,1)} %latent_hbm.3, bf16[128,128,128]{2,1,0:T(8,128)(2,1)} %weight_hbm.1, bf16[2,128,128]{2,1,0:T(8,128)(2,1)S(1)} %get-tuple-element.38.rest_0_, ...), custom_call_target="tpu_custom_call" | custom-call | flops 2147483648 | bytes 1024 | tf_op jit(solution)/shard_map/first_forward/pallas_call | solution.py:359
  22.1 0.9 %collective-permute-done.6.rest_3_ = bf16[2,128,128]{2,1,0:T(8,128)(2,1)S(1)} collective-permute-done((bf16[2,128,128]{2,1,0:T(8,128)(2,1)S(1)}, bf16[2,128,128]{2,1,0:T(8,128)(2,1)S(1)}, u32[]{:S(2)}, u32[]{:S(2)}) %collective-permute-start.6) | collective-permute-done | bytes 65568 | tf_op jit(solution)/shard_map/ppermute | solution.py:30
  23.0 1.8 %far_forward.1 = (bf16[256,128]{1,0:T(8,128)(2,1)S(1)}, bf16[256,128]{1,0:T(8,128)(2,1)S(1)}, bf16[256,128]{1,0:T(8,128)(2,1)S(1)}, bf16[256,128]{1,0:T(8,128)(2,1)S(1)}) custom-call(s32[1443]{0:T(1024)S(1)} %get-tuple-element.42.plan_ref, f32[9,128,128]{2,1,0:T(8,128)S(1)} %get-tuple-element.43.sum_ref, ...), custom_call_target="tpu_custom_call" | custom-call | tf_op jit(solution)/shard_map/far_forward/pallas_call | solution.py:381
  24.9 0.5 collective-permute-start.7
  25.4 0.5 collective-permute-start.8
  25.9 0.9 %collective-permute-start.9 = (bf16[256,128]{1,0:T(8,128)(2,1)S(1)}, bf16[256,128]{1,0:T(8,128)(2,1)S(1)}, u32[]{:S(2)}, u32[]{:S(2)}) collective-permute-start(bf16[256,128]{1,0:T(8,128)(2,1)S(1)} %get-tuple-element.52), channel_id=1, source_target_pairs={{0,3},{1,2},{2,1},{3,0},{4,7},{5,6},{6,5},{7,4},{8,11},{9,10},{10,... | collective-permute-start | bytes 196616 | tf_op jit(solution)/shard_map/ppermute | solution.py:30
  26.9 3.4 %collective-permute-done.8.rest_2_ = bf16[256,128]{1,0:T(8,128)(2,1)S(1)} collective-permute-done((bf16[256,128]{1,0:T(8,128)(2,1)S(1)}, bf16[256,128]{1,0:T(8,128)(2,1)S(1)}, u32[]{:S(2)}, u32[]{:S(2)}) %collective-permute-start.8) | collective-permute-done | bytes 65568 | tf_op jit(solution)/shard_map/ppermute | solution.py:30
  30.3 2.3 %mlp.1 = (bf16[256,128]{1,0:T(8,128)(2,1)S(1)}, bf16[128,256]{1,0:T(8,128)(2,1)S(1)}, bf16[128,256]{1,0:T(8,128)(2,1)S(1)}, bf16[128,256]{1,0:T(8,128)(2,1)S(1)}, bf16[128,256]{1,0:T(8,128)(2,1)S(1)}) custom-call(f32[1,2048]{1,0:T(1,128)S(1)} %bitcast.2, bf16[2048,128]{1,0:T(8,128)(2,1)S(1)} %copy-done, bf16[1024,128]{1,0:T(8,128)(2,1)S(1)} %copy-done.2, ...), custom_call_target="tpu_custom_call" | custom-call | tf_op jit(solution)/shard_map/mlp/pallas_call | solution.py:400
  32.7 0.6 collective-permute-start.13
  33.2 1.1 %collective-permute-start.14 = (bf16[128,256]{1,0:T(8,128)(2,1)S(1)}, bf16[128,256]{1,0:T(8,128)(2,1)S(1)}, u32[]{:S(2)}, u32[]{:S(2)}) collective-permute-start(bf16[128,256]{1,0:T(8,128)(2,1)S(1)} %get-tuple-element.59), channel_id=1, source_target_pairs={{2,0},{3,1},{0,2},{1,3},{6,4},{7,5},{4,6},{5,7},{10,8},{11,9},{8,1... | collective-permute-start | bytes 196616 | tf_op jit(solution)/shard_map/ppermute | solution.py:34
  34.7 3.1 %collective-permute-done.14.rest_2_ = bf16[128,256]{1,0:T(8,128)(2,1)S(1)} collective-permute-done((bf16[128,256]{1,0:T(8,128)(2,1)S(1)}, bf16[128,256]{1,0:T(8,128)(2,1)S(1)}, u32[]{:S(2)}, u32[]{:S(2)}) %collective-permute-start.14) | collective-permute-done | bytes 65568 | tf_op jit(solution)/shard_map/ppermute | solution.py:34
  37.8 0.8 %collective-permute-done.15.rest_3_ = bf16[128,256]{1,0:T(8,128)(2,1)S(1)} collective-permute-done((bf16[128,256]{1,0:T(8,128)(2,1)S(1)}, bf16[128,256]{1,0:T(8,128)(2,1)S(1)}, u32[]{:S(2)}, u32[]{:S(2)}) %collective-permute-start.15) | collective-permute-done | bytes 65568 | tf_op jit(solution)/shard_map/ppermute | solution.py:34
  38.6 1.7 %far_backward.1 = (bf16[9,128,128]{2,1,0:T(8,128)(2,1)S(1)}, bf16[2,128,128]{2,1,0:T(8,128)(2,1)S(1)}, bf16[2,128,128]{2,1,0:T(8,128)(2,1)S(1)}, bf16[2,128,128]...) custom-call(s32[1443]{0:T(1024)S(1)} %get-tuple-element.42.plan_ref, bf16[128,128,128]{2,1,0:T(8,128)(2,1)S(1)} %get-tuple-element.44.weight_ref, ...), custom_call_target="tpu_custom_call" | custom-call | tf_op jit(solution)/shard_map/far_backward/pallas_call | solution.py:418
  40.5 2.5 %collective-permute-start.22 = (bf16[2,128,128]{2,1,0:T(8,128)(2,1)S(1)}, bf16[2,128,128]{2,1,0:T(8,128)(2,1)S(1)}, u32[]{:S(2)}, u32[]{:S(2)}) collective-permute-start(bf16[2,128,128]{2,1,0:T(8,128)(2,1)S(1)} %get-tuple-element.70), channel_id=1, source_target_pairs={{16,0},{20,4},{24,8},{28,12},{0,16},{4,20},{8,24},{12,28},{17,1},{... | collective-permute-start | bytes 196616 | tf_op jit(solution)/shard_map/ppermute | solution.py:34
  43.1 0.7 %collective-permute-start.23 = (bf16[2,128,128]{2,1,0:T(8,128)(2,1)S(1)}, bf16[2,128,128]{2,1,0:T(8,128)(2,1)S(1)}, u32[]{:S(2)}, u32[]{:S(2)}) collective-permute-start(bf16[2,128,128]{2,1,0:T(8,128)(2,1)S(1)} %get-tuple-element.71), channel_id=1, source_target_pairs={{20,0},{16,4},{28,8},{24,12},{4,16},{0,20},{12,24},{8,28},{21,1},{... | collective-permute-start | bytes 196616 | tf_op jit(solution)/shard_map/ppermute | solution.py:34
  43.7 2.7 %rest_backward.1 = (bf16[2,128,128]{2,1,0:T(8,128)(2,1)S(1)}, bf16[2,128,128]{2,1,0:T(8,128)(2,1)S(1)}, bf16[2,128,128]{2,1,0:T(8,128)(2,1)S(1)}, bf16[2,128,128]{2,1,0:T(8,128)(2,1)S(1)}, f32[17,128,128]{2,1,0:T(8,128)S(1)}) custom-call(s32[1443]{0:T(1024)S(1)} %get-tuple-element.42.plan_ref, bf16[128,128,128]{2,1,0:T(8,128)(2,1)S(1)} %get-tuple-element.44.weight_ref, ...), custom_call_target="tpu_custom_call" | custom-call | flops 2147483648 | bytes 1024 | tf_op jit(solution)/shard_map/rest_backward/pallas_call | solution.py:431
  46.9 0.8 %collective-permute-start.17 = (bf16[256,128]{1,0:T(8,128)(2,1)S(1)}, bf16[256,128]{1,0:T(8,128)(2,1)S(1)}, u32[]{:S(2)}, u32[]{:S(2)}) collective-permute-start(bf16[256,128]{1,0:T(8,128)(2,1)S(1)} %get-tuple-element.65.rest_0_), channel_id=1, source_target_pairs={{0,2},{1,3},{2,0},{3,1},{4,6},{5,7},{6,4},{7,5},{8,10},{9,11},{10,... | collective-permute-start | bytes 196616 | tf_op jit(solution)/shard_map/ppermute | solution.py:30
  47.7 3.2 %collective-permute-start.24 = (bf16[2,128,128]{2,1,0:T(8,128)(2,1)S(1)}, bf16[2,128,128]{2,1,0:T(8,128)(2,1)S(1)}, u32[]{:S(2)}, u32[]{:S(2)}) collective-permute-start(bf16[2,128,128]{2,1,0:T(8,128)(2,1)S(1)} %get-tuple-element.72), channel_id=1, source_target_pairs={{24,0},{28,4},{16,8},{20,12},{8,16},{12,20},{0,24},{4,28},{25,1},{... | collective-permute-start | bytes 196616 | tf_op jit(solution)/shard_map/ppermute | solution.py:34
  50.8 1.7 %collective-permute-start.25 = (bf16[2,128,128]{2,1,0:T(8,128)(2,1)S(1)}, bf16[2,128,128]{2,1,0:T(8,128)(2,1)S(1)}, u32[]{:S(2)}, u32[]{:S(2)}) collective-permute-start(bf16[2,128,128]{2,1,0:T(8,128)(2,1)S(1)} %get-tuple-element.73), channel_id=1, source_target_pairs={{28,0},{24,4},{20,8},{16,12},{12,16},{8,20},{4,24},{0,28},{29,1},{... | collective-permute-start | bytes 196616 | tf_op jit(solution)/shard_map/ppermute | solution.py:34
  53.0 3.0 %collective-permute-start.21 = (bf16[2,128,128]{2,1,0:T(8,128)(2,1)S(1)}, bf16[2,128,128]{2,1,0:T(8,128)(2,1)S(1)}, u32[]{:S(2)}, u32[]{:S(2)}) collective-permute-start(bf16[2,128,128]{2,1,0:T(8,128)(2,1)S(1)} %get-tuple-element.69), channel_id=1, source_target_pairs={{12,0},{8,4},{4,8},{0,12},{28,16},{24,20},{20,24},{16,28},{13,1},{... | collective-permute-start | bytes 196616 | tf_op jit(solution)/shard_map/ppermute | solution.py:34
  56.0 0.7 %rows.1 = bf16[1024,128]{1,0:T(8,128)(2,1)} custom-call(bf16[256,128]{1,0:T(8,128)(2,1)S(1)} %get-tuple-element.65.rest_0_, bf16[256,128]{1,0:T(8,128)(2,1)S(1)} %collective-permute-done.16.rest_1_, bf16[256,128]{1,0:T(8,128)(2,1)S(1)} %collective-permute-done.17.rest_2_, bf16[256,128]{1,0:T(8,128)(2,1)S(1)} %collective-permute-done.18.rest_3_), custom_call_target="tpu_custom_call" | custom-call | tf_op jit(solution)/shard_map/rows/pallas_call | solution.py:447
  56.7 1.7 %collective-permute-done.25.rest_7_ = bf16[2,128,128]{2,1,0:T(8,128)(2,1)S(1)} collective-permute-done((bf16[2,128,128]{2,1,0:T(8,128)(2,1)S(1)}, bf16[2,128,128]{2,1,0:T(8,128)(2,1)S(1)}, u32[]{:S(2)}, u32[]{:S(2)}) %collective-permute-start.25) | collective-permute-done | bytes 65568 | tf_op jit(solution)/shard_map/ppermute | solution.py:34
  58.6 1.7 %collective-permute-done.21.rest_3_ = bf16[2,128,128]{2,1,0:T(8,128)(2,1)S(1)} collective-permute-done((bf16[2,128,128]{2,1,0:T(8,128)(2,1)S(1)}, bf16[2,128,128]{2,1,0:T(8,128)(2,1)S(1)}, u32[]{:S(2)}, u32[]{:S(2)}) %collective-permute-start.21) | collective-permute-done | bytes 65568 | tf_op jit(solution)/shard_map/ppermute | solution.py:34
  60.3 1.7 %final.1 = bf16[128,2048]{1,0:T(8,128)(2,1)} custom-call(s32[2,8]{1,0:T(2,128)S(1)} %bitcast.4, s32[8]{0:T(128)S(1)} %copy-done.5, f32[17,128,128]{2,1,0:T(8,128)S(1)} %get-tuple-element.64.local_ref, bf16[2,128,128]{2,1,0:T(8,128)(2,1)S(1)} %get-tuple-element.66.rest_0_, bf16[2,128,128]{2,1,0:T(8,128)(2,1)S(1)} %collective-permute-done.19.rest_1_, ...), custom_call_target="tpu_custom_call" | custom-call | tf_op jit(solution)/shard_map/final/pallas_call | solution.py:456
  (40 shorter events, 2.3 us)
Async XLA Ops:
  0.6 21.4 %copy-start.1 = (bf16[128,2048]{1,0:T(8,128)(2,1)S(1)}, bf16[128,2048]{1,0:T(8,128)(2,1)}, u32[]{:S(2)}) copy-start(bf16[128,2048]{1,0:T(8,128)(2,1)} %rest_4_) | copy-start | bytes 1572868
  2.0 22.8 %collective-permute-start.11 = (bf16[128,2048]{1,0:T(8,128)(2,1)}, bf16[128,2048]{1,0:T(8,128)(2,1)S(1)}, u32[]{:S(2)}, u32[]{:S(2)}) collective-permute-start(bf16[128,2048]{1,0:T(8,128)(2,1)} %rest_4_), channel_id=1, source_target_pairs={{0,2},{1,3},{2,0},{3,1},{4,6},{5,7},{6,4},{7,5},{8,10},{9,11},{10,... | collective-permute-start | bytes 1572872 | tf_op jit(solution)/shard_map/ppermute | solution.py:30
  5.0 6.1 %collective-permute-start = (bf16[2,128,128]{2,1,0:T(8,128)(2,1)S(1)}, bf16[2,128,128]{2,1,0:T(8,128)(2,1)S(1)}, u32[]{:S(2)}, u32[]{:S(2)}) collective-permute-start(bf16[2,128,128]{2,1,0:T(8,128)(2,1)S(1)} %get-tuple-element.39), channel_id=1, source_target_pairs={{0,4},{4,0},{8,12},{12,8},{16,20},{20,16},{24,28},{28,24},{1,5},{5... | collective-permute-start | bytes 196616 | tf_op jit(solution)/shard_map/ppermute | solution.py:30
  6.5 6.3 %collective-permute-start.1 = (bf16[2,128,128]{2,1,0:T(8,128)(2,1)S(1)}, bf16[2,128,128]{2,1,0:T(8,128)(2,1)S(1)}, u32[]{:S(2)}, u32[]{:S(2)}) collective-permute-start(bf16[2,128,128]{2,1,0:T(8,128)(2,1)S(1)} %get-tuple-element.40), channel_id=1, source_target_pairs={{0,8},{4,12},{8,0},{12,4},{16,24},{20,28},{24,16},{28,20},{1,9},{5... | collective-permute-start | bytes 196616 | tf_op jit(solution)/shard_map/ppermute | solution.py:30
  8.1 7.9 %collective-permute-start.2 = (bf16[2,128,128]{2,1,0:T(8,128)(2,1)S(1)}, bf16[2,128,128]{2,1,0:T(8,128)(2,1)S(1)}, u32[]{:S(2)}, u32[]{:S(2)}) collective-permute-start(bf16[2,128,128]{2,1,0:T(8,128)(2,1)S(1)} %get-tuple-element.41), channel_id=1, source_target_pairs={{0,12},{4,8},{8,4},{12,0},{16,28},{20,24},{24,20},{28,16},{1,13},{... | collective-permute-start | bytes 196616 | tf_op jit(solution)/shard_map/ppermute | solution.py:30
  8.5 13.5 %collective-permute-start.3 = (bf16[2,128,128]{2,1,0:T(8,128)(2,1)S(1)}, bf16[2,128,128]{2,1,0:T(8,128)(2,1)S(1)}, u32[]{:S(2)}, u32[]{:S(2)}) collective-permute-start(bf16[2,128,128]{2,1,0:T(8,128)(2,1)S(1)} %get-tuple-element.45), channel_id=1, source_target_pairs={{0,16},{4,20},{8,24},{12,28},{16,0},{20,4},{24,8},{28,12},{1,17},{... | collective-permute-start | bytes 196616 | tf_op jit(solution)/shard_map/ppermute | solution.py:30
  11.1 11.0 %collective-permute-start.4 = (bf16[2,128,128]{2,1,0:T(8,128)(2,1)S(1)}, bf16[2,128,128]{2,1,0:T(8,128)(2,1)S(1)}, u32[]{:S(2)}, u32[]{:S(2)}) collective-permute-start(bf16[2,128,128]{2,1,0:T(8,128)(2,1)S(1)} %get-tuple-element.46), channel_id=1, source_target_pairs={{0,20},{4,16},{8,28},{12,24},{16,4},{20,0},{24,12},{28,8},{1,21},{... | collective-permute-start | bytes 196616 | tf_op jit(solution)/shard_map/ppermute | solution.py:30
  12.8 9.3 %collective-permute-start.5 = (bf16[2,128,128]{2,1,0:T(8,128)(2,1)S(1)}, bf16[2,128,128]{2,1,0:T(8,128)(2,1)S(1)}, u32[]{:S(2)}, u32[]{:S(2)}) collective-permute-start(bf16[2,128,128]{2,1,0:T(8,128)(2,1)S(1)} %get-tuple-element.47), channel_id=1, source_target_pairs={{0,24},{4,28},{8,16},{12,20},{16,8},{20,12},{24,0},{28,4},{1,25},{... | collective-permute-start | bytes 196616 | tf_op jit(solution)/shard_map/ppermute | solution.py:30
  15.9 7.1 %collective-permute-start.6 = (bf16[2,128,128]{2,1,0:T(8,128)(2,1)S(1)}, bf16[2,128,128]{2,1,0:T(8,128)(2,1)S(1)}, u32[]{:S(2)}, u32[]{:S(2)}) collective-permute-start(bf16[2,128,128]{2,1,0:T(8,128)(2,1)S(1)} %get-tuple-element.48), channel_id=1, source_target_pairs={{0,28},{4,24},{8,20},{12,16},{16,12},{20,8},{24,4},{28,0},{1,29},{... | collective-permute-start | bytes 196616 | tf_op jit(solution)/shard_map/ppermute | solution.py:30
  22.0 8.3 %copy-start = (bf16[2048,128]{1,0:T(8,128)(2,1)S(1)}, bf16[2048,128]{1,0:T(8,128)(2,1)}, u32[]{:S(2)}) copy-start(bf16[2048,128]{1,0:T(8,128)(2,1)} %w_out_ref.1) | copy-start | bytes 1572868
  22.0 8.3 %copy-start.2 = (bf16[1024,128]{1,0:T(8,128)(2,1)S(1)}, bf16[1024,128]{1,0:T(8,128)(2,1)}, u32[]{:S(2)}) copy-start(bf16[1024,128]{1,0:T(8,128)(2,1)} %g_ref.1) | copy-start | bytes 786436
  22.0 8.3 %copy-start.3 = (f32[2048]{0:T(1024)S(1)}, f32[2048]{0:T(1024)}, u32[]{:S(2)}) copy-start(f32[2048]{0:T(1024)} %param.17) | copy-start | bytes 24580
  22.0 8.2 %collective-permute-start.10 = (bf16[128,2048]{1,0:T(8,128)(2,1)S(1)}, bf16[128,2048]{1,0:T(8,128)(2,1)S(1)}, u32[]{:S(2)}, u32[]{:S(2)}) collective-permute-start(bf16[128,2048]{1,0:T(8,128)(2,1)S(1)} %copy-done.1), channel_id=1, source_target_pairs={{0,1},{1,0},{2,3},{3,2},{4,5},{5,4},{6,7},{7,6},{8,9},{9,8},{10,11... | collective-permute-start | bytes 1572872 | tf_op jit(solution)/shard_map/ppermute | solution.py:30
  24.8 5.5 %collective-permute-start.12 = (bf16[128,2048]{1,0:T(8,128)(2,1)S(1)}, bf16[128,2048]{1,0:T(8,128)(2,1)S(1)}, u32[]{:S(2)}, u32[]{:S(2)}) collective-permute-start(bf16[128,2048]{1,0:T(8,128)(2,1)S(1)} %collective-permute-done.11.rest_6_), channel_id=1, source_target_pairs={{0,1},{1,0},{2,3},{3,2},{4,5},{5,4},{6,7},{7,6},{8,9},{9,8},{10,11... | collective-permute-start | bytes 1572872 | tf_op jit(solution)/shard_map/ppermute | solution.py:30
  24.9 2.0 %collective-permute-start.7 = (bf16[256,128]{1,0:T(8,128)(2,1)S(1)}, bf16[256,128]{1,0:T(8,128)(2,1)S(1)}, u32[]{:S(2)}, u32[]{:S(2)}) collective-permute-start(bf16[256,128]{1,0:T(8,128)(2,1)S(1)} %get-tuple-element.50), channel_id=1, source_target_pairs={{0,1},{1,0},{2,3},{3,2},{4,5},{5,4},{6,7},{7,6},{8,9},{9,8},{10,11... | collective-permute-start | bytes 196616 | tf_op jit(solution)/shard_map/ppermute | solution.py:30
  25.4 4.9 %collective-permute-start.8 = (bf16[256,128]{1,0:T(8,128)(2,1)S(1)}, bf16[256,128]{1,0:T(8,128)(2,1)S(1)}, u32[]{:S(2)}, u32[]{:S(2)}) collective-permute-start(bf16[256,128]{1,0:T(8,128)(2,1)S(1)} %get-tuple-element.51), channel_id=1, source_target_pairs={{0,2},{1,3},{2,0},{3,1},{4,6},{5,7},{6,4},{7,5},{8,10},{9,11},{10,... | collective-permute-start | bytes 196616 | tf_op jit(solution)/shard_map/ppermute | solution.py:30
  25.9 4.4 %collective-permute-start.9 = (bf16[256,128]{1,0:T(8,128)(2,1)S(1)}, bf16[256,128]{1,0:T(8,128)(2,1)S(1)}, u32[]{:S(2)}, u32[]{:S(2)}) collective-permute-start(bf16[256,128]{1,0:T(8,128)(2,1)S(1)} %get-tuple-element.52), channel_id=1, source_target_pairs={{0,3},{1,2},{2,1},{3,0},{4,7},{5,6},{6,5},{7,4},{8,11},{9,10},{10,... | collective-permute-start | bytes 196616 | tf_op jit(solution)/shard_map/ppermute | solution.py:30
  32.7 2.0 %collective-permute-start.13 = (bf16[128,256]{1,0:T(8,128)(2,1)S(1)}, bf16[128,256]{1,0:T(8,128)(2,1)S(1)}, u32[]{:S(2)}, u32[]{:S(2)}) collective-permute-start(bf16[128,256]{1,0:T(8,128)(2,1)S(1)} %get-tuple-element.58), channel_id=1, source_target_pairs={{1,0},{0,1},{3,2},{2,3},{5,4},{4,5},{7,6},{6,7},{9,8},{8,9},{11,10... | collective-permute-start | bytes 196616 | tf_op jit(solution)/shard_map/ppermute | solution.py:34
  33.2 4.5 %collective-permute-start.14 = (bf16[128,256]{1,0:T(8,128)(2,1)S(1)}, bf16[128,256]{1,0:T(8,128)(2,1)S(1)}, u32[]{:S(2)}, u32[]{:S(2)}) collective-permute-start(bf16[128,256]{1,0:T(8,128)(2,1)S(1)} %get-tuple-element.59), channel_id=1, source_target_pairs={{2,0},{3,1},{0,2},{1,3},{6,4},{7,5},{4,6},{5,7},{10,8},{11,9},{8,1... | collective-permute-start | bytes 196616 | tf_op jit(solution)/shard_map/ppermute | solution.py:34
  34.3 4.3 %collective-permute-start.15 = (bf16[128,256]{1,0:T(8,128)(2,1)S(1)}, bf16[128,256]{1,0:T(8,128)(2,1)S(1)}, u32[]{:S(2)}, u32[]{:S(2)}) collective-permute-start(bf16[128,256]{1,0:T(8,128)(2,1)S(1)} %get-tuple-element.60), channel_id=1, source_target_pairs={{3,0},{2,1},{1,2},{0,3},{7,4},{6,5},{5,6},{4,7},{11,8},{10,9},{9,1... | collective-permute-start | bytes 196616 | tf_op jit(solution)/shard_map/ppermute | solution.py:34
  40.4 3.4 %collective-permute-start.16 = (bf16[256,128]{1,0:T(8,128)(2,1)S(1)}, bf16[256,128]{1,0:T(8,128)(2,1)S(1)}, u32[]{:S(2)}, u32[]{:S(2)}) collective-permute-start(bf16[256,128]{1,0:T(8,128)(2,1)S(1)} %get-tuple-element.65.rest_0_), channel_id=1, source_target_pairs={{0,1},{1,0},{2,3},{3,2},{4,5},{5,4},{6,7},{7,6},{8,9},{9,8},{10,11... | collective-permute-start | bytes 196616 | tf_op jit(solution)/shard_map/ppermute | solution.py:30
  40.5 10.3 %collective-permute-start.22 = (bf16[2,128,128]{2,1,0:T(8,128)(2,1)S(1)}, bf16[2,128,128]{2,1,0:T(8,128)(2,1)S(1)}, u32[]{:S(2)}, u32[]{:S(2)}) collective-permute-start(bf16[2,128,128]{2,1,0:T(8,128)(2,1)S(1)} %get-tuple-element.70), channel_id=1, source_target_pairs={{16,0},{20,4},{24,8},{28,12},{0,16},{4,20},{8,24},{12,28},{17,1},{... | collective-permute-start | bytes 196616 | tf_op jit(solution)/shard_map/ppermute | solution.py:34
  43.0 17.2 %copy-start.4 = (s32[8,2]{0,1:T(2,128)S(1)}, s32[8,2]{0,1:T(2,128)}, u32[]{:S(2)}) copy-start(s32[8,2]{0,1:T(2,128)} %param.12) | copy-start | bytes 196
  43.0 17.2 %copy-start.5 = (s32[8]{0:T(128)S(1)}, s32[8]{0:T(128)}, u32[]{:S(2)}) copy-start(s32[8]{0:T(128)} %counts_ref.1) | copy-start | bytes 100
  43.1 9.5 %collective-permute-start.23 = (bf16[2,128,128]{2,1,0:T(8,128)(2,1)S(1)}, bf16[2,128,128]{2,1,0:T(8,128)(2,1)S(1)}, u32[]{:S(2)}, u32[]{:S(2)}) collective-permute-start(bf16[2,128,128]{2,1,0:T(8,128)(2,1)S(1)} %get-tuple-element.71), channel_id=1, source_target_pairs={{20,0},{16,4},{28,8},{24,12},{4,16},{0,20},{12,24},{8,28},{21,1},{... | collective-permute-start | bytes 196616 | tf_op jit(solution)/shard_map/ppermute | solution.py:34
  46.5 6.5 %collective-permute-start.18 = (bf16[256,128]{1,0:T(8,128)(2,1)S(1)}, bf16[256,128]{1,0:T(8,128)(2,1)S(1)}, u32[]{:S(2)}, u32[]{:S(2)}) collective-permute-start(bf16[256,128]{1,0:T(8,128)(2,1)S(1)} %get-tuple-element.65.rest_0_), channel_id=1, source_target_pairs={{0,3},{1,2},{2,1},{3,0},{4,7},{5,6},{6,5},{7,4},{8,11},{9,10},{10,... | collective-permute-start | bytes 196616 | tf_op jit(solution)/shard_map/ppermute | solution.py:30
  46.9 6.1 %collective-permute-start.17 = (bf16[256,128]{1,0:T(8,128)(2,1)S(1)}, bf16[256,128]{1,0:T(8,128)(2,1)S(1)}, u32[]{:S(2)}, u32[]{:S(2)}) collective-permute-start(bf16[256,128]{1,0:T(8,128)(2,1)S(1)} %get-tuple-element.65.rest_0_), channel_id=1, source_target_pairs={{0,2},{1,3},{2,0},{3,1},{4,6},{5,7},{6,4},{7,5},{8,10},{9,11},{10,... | collective-permute-start | bytes 196616 | tf_op jit(solution)/shard_map/ppermute | solution.py:30
  47.7 9.0 %collective-permute-start.24 = (bf16[2,128,128]{2,1,0:T(8,128)(2,1)S(1)}, bf16[2,128,128]{2,1,0:T(8,128)(2,1)S(1)}, u32[]{:S(2)}, u32[]{:S(2)}) collective-permute-start(bf16[2,128,128]{2,1,0:T(8,128)(2,1)S(1)} %get-tuple-element.72), channel_id=1, source_target_pairs={{24,0},{28,4},{16,8},{20,12},{8,16},{12,20},{0,24},{4,28},{25,1},{... | collective-permute-start | bytes 196616 | tf_op jit(solution)/shard_map/ppermute | solution.py:34
  50.8 7.6 %collective-permute-start.25 = (bf16[2,128,128]{2,1,0:T(8,128)(2,1)S(1)}, bf16[2,128,128]{2,1,0:T(8,128)(2,1)S(1)}, u32[]{:S(2)}, u32[]{:S(2)}) collective-permute-start(bf16[2,128,128]{2,1,0:T(8,128)(2,1)S(1)} %get-tuple-element.73), channel_id=1, source_target_pairs={{28,0},{24,4},{20,8},{16,12},{12,16},{8,20},{4,24},{0,28},{29,1},{... | collective-permute-start | bytes 196616 | tf_op jit(solution)/shard_map/ppermute | solution.py:34
  52.5 6.0 %collective-permute-start.19 = (bf16[2,128,128]{2,1,0:T(8,128)(2,1)S(1)}, bf16[2,128,128]{2,1,0:T(8,128)(2,1)S(1)}, u32[]{:S(2)}, u32[]{:S(2)}) collective-permute-start(bf16[2,128,128]{2,1,0:T(8,128)(2,1)S(1)} %get-tuple-element.67), channel_id=1, source_target_pairs={{4,0},{0,4},{12,8},{8,12},{20,16},{16,20},{28,24},{24,28},{5,1},{1... | collective-permute-start | bytes 196616 | tf_op jit(solution)/shard_map/ppermute | solution.py:34
  53.0 5.6 %collective-permute-start.20 = (bf16[2,128,128]{2,1,0:T(8,128)(2,1)S(1)}, bf16[2,128,128]{2,1,0:T(8,128)(2,1)S(1)}, u32[]{:S(2)}, u32[]{:S(2)}) collective-permute-start(bf16[2,128,128]{2,1,0:T(8,128)(2,1)S(1)} %get-tuple-element.68), channel_id=1, source_target_pairs={{8,0},{12,4},{0,8},{4,12},{24,16},{28,20},{16,24},{20,28},{9,1},{1... | collective-permute-start | bytes 196616 | tf_op jit(solution)/shard_map/ppermute | solution.py:34
  53.0 7.3 %collective-permute-start.21 = (bf16[2,128,128]{2,1,0:T(8,128)(2,1)S(1)}, bf16[2,128,128]{2,1,0:T(8,128)(2,1)S(1)}, u32[]{:S(2)}, u32[]{:S(2)}) collective-permute-start(bf16[2,128,128]{2,1,0:T(8,128)(2,1)S(1)} %get-tuple-element.69), channel_id=1, source_target_pairs={{12,0},{8,4},{4,8},{0,12},{28,16},{24,20},{20,24},{16,28},{13,1},{... | collective-permute-start | bytes 196616 | tf_op jit(solution)/shard_map/ppermute | solution.py:34

commit v4 on v3

--- a/solution.py
+++ b/solution.py
@@ -250,27 +250,22 @@
                     rows_grad[start // split, :, k * rows : (k + 1) * rows] = shares[d][...]
 
 
-def slot_gradients(plan, kind, shifts, dom, cap, plan_ref, weight_ref, rows_grad, outs, total):
+def slot_backward_kernel(plan, dom, cap, chan, blk, obs, plan_ref, weight_ref, *rest):
+    shares, rows_grad, (*outs, total) = rest[:chan], rest[chan], rest[chan + 1 :]
+    gather_grad(chan, max(1, obs // chan), blk, shares, rows_grad)
     total[...] = jnp.zeros_like(total)
 
     def body(e, k, j):
         total[k] += lax.dot_general(rows_grad[j], weight_ref[e], NN, preferred_element_type=F32)
 
-    plan.run(plan_ref, kind, body)
+    plan.run(plan_ref, 1, body)
+    plan.run(plan_ref, 2, body)
     me = lax.axis_index("dom")
-    for d, out in zip(shifts, outs):
-        out[...] = total[pl.ds(source(me, d, dom) * cap, cap)].astype(BF16)
-
-
-def far_backward_kernel(plan, shifts, dom, cap, chan, blk, obs, plan_ref, weight_ref, *rest):
-    shares, rows_grad, (*outs, total) = rest[:chan], rest[chan], rest[chan + 1 :]
-    gather_grad(chan, max(1, obs // chan), blk, shares, rows_grad)
-    slot_gradients(plan, 2, shifts, dom, cap, plan_ref, weight_ref, rows_grad, outs, total)
-
-
-def rest_backward_kernel(plan, shifts, dom, cap, plan_ref, weight_ref, rows_grad, *rest):
-    *outs, total, slots = rest
-    slot_gradients(plan, 1, shifts, dom, cap, plan_ref, weight_ref, rows_grad, outs, slots)
+    for d in range(dom):
+        outs[d][...] = total[pl.ds(source(me, d, dom) * cap, cap)].astype(BF16)
+
+
+def local_backward_kernel(plan, plan_ref, weight_ref, rows_grad, total):
     total[...] = jnp.zeros_like(total)
 
     def body(e, k, j):
@@ -395,7 +390,7 @@
             for d in sorted(weights):
                 weights[d | bit] = send(weights[d], "chan", bit, chan)
             bit //= 2
-    shares = [shares[0]] + [send(shares[d], "chan", d, chan) for d in range(1, chan)]
+    shares = {d: send(shares[d], "chan", d, chan) if d else shares[0] for d in reversed(range(chan))}
 
     mlp = pl.pallas_call(
         functools.partial(mlp_kernel, chan, min(512, hidden_width)),
@@ -409,41 +404,32 @@
         ],
         compiler_params=params(),
         name="mlp",
-    )(bias.reshape(1, hidden_width), w_out, g_out, *shares, *[weights[d] for d in range(chan)])
+    )(bias.reshape(1, hidden_width), w_out, g_out, *[shares[d] for d in range(chan)], *[weights[d] for d in range(chan)])
     obs_part, grads = mlp[0], mlp[1:]
-    grads = [grads[0]] + [send_back(grads[d], "chan", d, chan) for d in range(1, chan)]
-
-    slots = pltpu.VMEM((dom * cap + 1, feat, blk), F32)
-    slot_shape = shape((cap, feat, blk), BF16)
-    rows_grad, *far_grads = pl.pallas_call(
-        functools.partial(far_backward_kernel, plan, far, dom, cap, chan, blk, obs),
-        out_shape=[shape((obs + 1, feat, blk), BF16)] + [slot_shape] * len(far),
+    grads = {d: send_back(grads[d], "chan", d, chan) if d else grads[0] for d in reversed(range(chan))}
+    obs_parts = {d: send(obs_part, "chan", d, chan) if d else obs_part for d in reversed(range(chan))}
+
+    rows_grad, *slot_grads = pl.pallas_call(
+        functools.partial(slot_backward_kernel, plan, dom, cap, chan, blk, obs),
+        out_shape=[shape((obs + 1, feat, blk), BF16)] + [shape((cap, feat, blk), BF16)] * dom,
         in_specs=smem(1) + vmem(1 + chan),
-        out_specs=vmem(1 + len(far)),
-        scratch_shapes=[slots],
-        compiler_params=params(),
-        name="far_backward",
-    )(table, weight, *grads)
-    returned = {d: send_back(value, "dom", d, dom) for d, value in zip(far, far_grads)}
-    obs_part = after(obs_part, rows_grad)
-    obs_parts = [obs_part, send(obs_part, "chan", 1, chan)]
-
-    *near_grads, local_grad = pl.pallas_call(
-        functools.partial(rest_backward_kernel, plan, near, dom, cap),
-        out_shape=[slot_shape] * len(near) + [shape((nodes + 1, feat, blk), F32)],
+        out_specs=vmem(1 + dom),
+        scratch_shapes=[pltpu.VMEM((dom * cap + 1, feat, blk), F32)],
+        compiler_params=params(),
+        name="slot_backward",
+    )(table, weight, *[grads[d] for d in range(chan)])
+    returned = [slot_grads[0]] + [send_back(slot_grads[d], "dom", d, dom) for d in range(1, dom)]
+
+    local_grad = pl.pallas_call(
+        functools.partial(local_backward_kernel, plan),
+        out_shape=shape((nodes + 1, feat, blk), F32),
         in_specs=smem(1) + vmem(2),
-        out_specs=vmem(len(near) + 1),
-        scratch_shapes=[slots],
+        out_specs=pl.BlockSpec(memory_space=pltpu.VMEM),
         compiler_params=params(),
         cost_estimate=cost(edges),
-        name="rest_backward",
-    )(table, weight, after(rows_grad, obs_parts[1]))
-    returned[0] = near_grads[0]
-    for d, value in zip(near[1:], near_grads[1:]):
-        returned[d] = send_back(value, "dom", d, dom)
-
-    obs_part = after(obs_part, local_grad)
-    obs_parts += [send(obs_part, "chan", d, chan) for d in range(2, chan)]
+        name="local_backward",
+    )(table, weight, rows_grad)
+
     obs_out = pl.pallas_call(
         functools.partial(rows_kernel, chan),
         out_shape=shape((obs_rows, out_width), BF16),
@@ -451,7 +437,7 @@
         out_specs=pl.BlockSpec(memory_space=pltpu.VMEM),
         compiler_params=params(),
         name="rows",
-    )(*obs_parts)
+    )(*[obs_parts[d] for d in range(chan)])
 
     d_latent = pl.pallas_call(
         functools.partial(final_kernel, dom, cap, blk, nodes),
@@ -461,7 +447,7 @@
         scratch_shapes=[pltpu.VMEM((nodes, feat, blk), F32)],
         compiler_params=params(),
         name="final",
-    )(*tables, local_grad, *[returned[d] for d in range(dom)])
+    )(*tables, local_grad, *returned)
     return obs_out, d_latent
 
 

time: 62.1 us -> 60.1 us (0.968)
  waiting for transfers between devices: 11.9 us -> 8.86 us
    ppermute x10, waiting for transfers between devices: 7.51 us -> 4.47 us  [send_back(): lax.ppermute(value, axis, [(target(i, shift, count), i) for i in range(co...]
    ppermute x16, starting transfers between devices: 18.2 us -> 18.8 us  [send(): lax.ppermute(value, axis, [(i, target(i, shift, count)) for i in range(co...]
  transfers between devices with their start and end apart: 26 -> 26, of which waited for: 8 -> 6; matrix products, arithmetic and copies ran while one was open for 0% -> 0% of each run, Pallas kernels for 17% -> 21%
where the time goes in v4:
time: 60.1 us; the launch traced here: 59.4 us
  starting transfers between devices  32 us (53%)
  Pallas kernels  17.6 us (29%)
  waiting for transfers between devices  8.86 us (15%)
  between operations  0.83 us (1%)
    ppermute x16, starting transfers between devices, send(): lax.ppermute(value, axis, [(i, target(i, shift, count)) for i in range(co...  18.8 us
    ppermute x10, starting transfers between devices, send_back(): lax.ppermute(value, axis, [(target(i, shift, count), i) for i in range(co...  13.2 us
    pallas_call x1, Pallas kernels, on_device(): pl.pallas_call(functools.partial(first_forward_kernel, plan, near, dom, c...  5.31 us
    ppermute x10, waiting for transfers between devices, send_back(): lax.ppermute(value, axis, [(target(i, shift, count), i) for i in range(co...  4.47 us
    ppermute x16, waiting for transfers between devices, send(): lax.ppermute(value, axis, [(i, target(i, shift, count)) for i in range(co...  4.38 us
    pallas_call x1, Pallas kernels, on_device(): pl.pallas_call(functools.partial(slot_backward_kernel, plan, dom, cap, ch...  2.79 us
    pallas_call x1, Pallas kernels, on_device(): pl.pallas_call(functools.partial(mlp_kernel, chan, min(512, hidden_width)...  2.33 us
    pallas_call x1, Pallas kernels, on_device(): pl.pallas_call(functools.partial(far_forward_kernel, plan, far, dom, cap,...  1.77 us
  transfers between devices with their start and end apart: 26, of which 6 were waited for; matrix products, arithmetic and copies ran while one was open for 0% of the time, Pallas kernels for 21%

profile of v4, /device:TPU:0, one launch (start us, length us, event | category | flops | bytes accessed | tf_op | source)
XLA Modules:
  0.0 59.4 jit_solution(2047474068228371695)
XLA Ops:
  0.6 1.3 %pack.1 = (bf16[2,128,128]{2,1,0:T(8,128)(2,1)S(1)}, bf16[2,128,128]{2,1,0:T(8,128)(2,1)S(1)}, bf16[2,128,128]{2,1,0:T(8,128)(2,1)S(1)}, bf16[2,128,128]{2,1,0:T...) custom-call(s32[2,8]{1,0:T(2,128)} %bitcast.3, ...), custom_call_target="tpu_custom_call" | custom-call | tf_op jit(solution)/shard_map/pack/pallas_call | solution.py:328
  2.0 3.0 %collective-permute-start.11 = (bf16[128,2048]{1,0:T(8,128)(2,1)}, bf16[128,2048]{1,0:T(8,128)(2,1)S(1)}, u32[]{:S(2)}, u32[]{:S(2)}) collective-permute-start(bf16[128,2048]{1,0:T(8,128)(2,1)} %rest_4_), channel_id=1, source_target_pairs={{0,2},{1,3},{2,0},{3,1},{4,6},{5,7},{6,4},{7,5},{8,10},{9,11},{10,... | collective-permute-start | bytes 1572872 | tf_op jit(solution)/shard_map/ppermute | solution.py:30
  5.0 1.5 %collective-permute-start = (bf16[2,128,128]{2,1,0:T(8,128)(2,1)S(1)}, bf16[2,128,128]{2,1,0:T(8,128)(2,1)S(1)}, u32[]{:S(2)}, u32[]{:S(2)}) collective-permute-start(bf16[2,128,128]{2,1,0:T(8,128)(2,1)S(1)} %get-tuple-element.35), channel_id=1, source_target_pairs={{0,4},{4,0},{8,12},{12,8},{16,20},{20,16},{24,28},{28,24},{1,5},{5... | collective-permute-start | bytes 196616 | tf_op jit(solution)/shard_map/ppermute | solution.py:30
  6.5 1.6 %collective-permute-start.1 = (bf16[2,128,128]{2,1,0:T(8,128)(2,1)S(1)}, bf16[2,128,128]{2,1,0:T(8,128)(2,1)S(1)}, u32[]{:S(2)}, u32[]{:S(2)}) collective-permute-start(bf16[2,128,128]{2,1,0:T(8,128)(2,1)S(1)} %get-tuple-element.36), channel_id=1, source_target_pairs={{0,8},{4,12},{8,0},{12,4},{16,24},{20,28},{24,16},{28,20},{1,9},{5... | collective-permute-start | bytes 196616 | tf_op jit(solution)/shard_map/ppermute | solution.py:30
  8.5 2.6 %collective-permute-start.3 = (bf16[2,128,128]{2,1,0:T(8,128)(2,1)S(1)}, bf16[2,128,128]{2,1,0:T(8,128)(2,1)S(1)}, u32[]{:S(2)}, u32[]{:S(2)}) collective-permute-start(bf16[2,128,128]{2,1,0:T(8,128)(2,1)S(1)} %get-tuple-element.41), channel_id=1, source_target_pairs={{0,16},{4,20},{8,24},{12,28},{16,0},{20,4},{24,8},{28,12},{1,17},{... | collective-permute-start | bytes 196616 | tf_op jit(solution)/shard_map/ppermute | solution.py:30
  11.1 1.7 %collective-permute-start.4 = (bf16[2,128,128]{2,1,0:T(8,128)(2,1)S(1)}, bf16[2,128,128]{2,1,0:T(8,128)(2,1)S(1)}, u32[]{:S(2)}, u32[]{:S(2)}) collective-permute-start(bf16[2,128,128]{2,1,0:T(8,128)(2,1)S(1)} %get-tuple-element.42), channel_id=1, source_target_pairs={{0,20},{4,16},{8,28},{12,24},{16,4},{20,0},{24,12},{28,8},{1,21},{... | collective-permute-start | bytes 196616 | tf_op jit(solution)/shard_map/ppermute | solution.py:30
  12.8 3.2 %collective-permute-start.5 = (bf16[2,128,128]{2,1,0:T(8,128)(2,1)S(1)}, bf16[2,128,128]{2,1,0:T(8,128)(2,1)S(1)}, u32[]{:S(2)}, u32[]{:S(2)}) collective-permute-start(bf16[2,128,128]{2,1,0:T(8,128)(2,1)S(1)} %get-tuple-element.43), channel_id=1, source_target_pairs={{0,24},{4,28},{8,16},{12,20},{16,8},{20,12},{24,0},{28,4},{1,25},{... | collective-permute-start | bytes 196616 | tf_op jit(solution)/shard_map/ppermute | solution.py:30
  15.9 0.7 %collective-permute-start.6 = (bf16[2,128,128]{2,1,0:T(8,128)(2,1)S(1)}, bf16[2,128,128]{2,1,0:T(8,128)(2,1)S(1)}, u32[]{:S(2)}, u32[]{:S(2)}) collective-permute-start(bf16[2,128,128]{2,1,0:T(8,128)(2,1)S(1)} %get-tuple-element.44), channel_id=1, source_target_pairs={{0,28},{4,24},{8,20},{12,16},{16,12},{20,8},{24,4},{28,0},{1,29},{... | collective-permute-start | bytes 196616 | tf_op jit(solution)/shard_map/ppermute | solution.py:30
  16.7 5.3 %first_forward.1 = (f32[9,128,128]{2,1,0:T(8,128)S(1)}, s32[1443]{0:T(1024)S(1)}, bf16[128,128,128]{2,1,0:T(8,128)(2,1)S(1)}) custom-call(s32[128]{0:T(128)} %src_hbm.1, s32[128]{0:T(128)} %obs_hbm.1, bf16[128,2048]{1,0:T(8,128)(2,1)} %latent_hbm.3, bf16[128,128,128]{2,1,0:T(8,128)(2,1)} %weight_hbm.1, bf16[2,128,128]{2,1,0:T(8,128)(2,1)S(1)} %get-tuple-element.34.rest_0_, ...), custom_call_target="tpu_custom_call" | custom-call | flops 2147483648 | bytes 1024 | tf_op jit(solution)/shard_map/first_forward/pallas_call | solution.py:354
  22.1 0.9 %collective-permute-done.6.rest_3_ = bf16[2,128,128]{2,1,0:T(8,128)(2,1)S(1)} collective-permute-done((bf16[2,128,128]{2,1,0:T(8,128)(2,1)S(1)}, bf16[2,128,128]{2,1,0:T(8,128)(2,1)S(1)}, u32[]{:S(2)}, u32[]{:S(2)}) %collective-permute-start.6) | collective-permute-done | bytes 65568 | tf_op jit(solution)/shard_map/ppermute | solution.py:30
  23.0 1.8 %far_forward.1 = (bf16[256,128]{1,0:T(8,128)(2,1)S(1)}, bf16[256,128]{1,0:T(8,128)(2,1)S(1)}, bf16[256,128]{1,0:T(8,128)(2,1)S(1)}, bf16[256,128]{1,0:T(8,128)(2,1)S(1)}) custom-call(s32[1443]{0:T(1024)S(1)} %get-tuple-element.38.plan_ref, f32[9,128,128]{2,1,0:T(8,128)S(1)} %get-tuple-element.39.sum_ref, ...), custom_call_target="tpu_custom_call" | custom-call | tf_op jit(solution)/shard_map/far_forward/pallas_call | solution.py:376
  24.9 0.5 collective-permute-start.7
  25.4 0.5 collective-permute-start.8
  25.9 0.9 %collective-permute-start.9 = (bf16[256,128]{1,0:T(8,128)(2,1)S(1)}, bf16[256,128]{1,0:T(8,128)(2,1)S(1)}, u32[]{:S(2)}, u32[]{:S(2)}) collective-permute-start(bf16[256,128]{1,0:T(8,128)(2,1)S(1)} %get-tuple-element.48), channel_id=1, source_target_pairs={{0,3},{1,2},{2,1},{3,0},{4,7},{5,6},{6,5},{7,4},{8,11},{9,10},{10,... | collective-permute-start | bytes 196616 | tf_op jit(solution)/shard_map/ppermute | solution.py:30
  26.9 3.4 %collective-permute-done.8.rest_2_ = bf16[256,128]{1,0:T(8,128)(2,1)S(1)} collective-permute-done((bf16[256,128]{1,0:T(8,128)(2,1)S(1)}, bf16[256,128]{1,0:T(8,128)(2,1)S(1)}, u32[]{:S(2)}, u32[]{:S(2)}) %collective-permute-start.8) | collective-permute-done | bytes 65568 | tf_op jit(solution)/shard_map/ppermute | solution.py:30
  30.3 2.3 %mlp.1 = (bf16[256,128]{1,0:T(8,128)(2,1)S(1)}, bf16[128,256]{1,0:T(8,128)(2,1)S(1)}, bf16[128,256]{1,0:T(8,128)(2,1)S(1)}, bf16[128,256]{1,0:T(8,128)(2,1)S(1)}, bf16[128,256]{1,0:T(8,128)(2,1)S(1)}) custom-call(f32[1,2048]{1,0:T(1,128)S(1)} %bitcast.2, bf16[2048,128]{1,0:T(8,128)(2,1)S(1)} %copy-done, bf16[1024,128]{1,0:T(8,128)(2,1)S(1)} %copy-done.2, ...), custom_call_target="tpu_custom_call" | custom-call | tf_op jit(solution)/shard_map/mlp/pallas_call | solution.py:395
  32.7 0.6 collective-permute-start.16
  33.2 1.1 %collective-permute-start.17 = (bf16[128,256]{1,0:T(8,128)(2,1)S(1)}, bf16[128,256]{1,0:T(8,128)(2,1)S(1)}, u32[]{:S(2)}, u32[]{:S(2)}) collective-permute-start(bf16[128,256]{1,0:T(8,128)(2,1)S(1)} %get-tuple-element.55), channel_id=1, source_target_pairs={{2,0},{3,1},{0,2},{1,3},{6,4},{7,5},{4,6},{5,7},{10,8},{11,9},{8,1... | collective-permute-start | bytes 196616 | tf_op jit(solution)/shard_map/ppermute | solution.py:34
  34.7 0.7 %collective-permute-start.13 = (bf16[256,128]{1,0:T(8,128)(2,1)S(1)}, bf16[256,128]{1,0:T(8,128)(2,1)S(1)}, u32[]{:S(2)}, u32[]{:S(2)}) collective-permute-start(bf16[256,128]{1,0:T(8,128)(2,1)S(1)} %get-tuple-element.52.rest_0_), channel_id=1, source_target_pairs={{0,1},{1,0},{2,3},{3,2},{4,5},{5,4},{6,7},{7,6},{8,9},{9,8},{10,11... | collective-permute-start | bytes 196616 | tf_op jit(solution)/shard_map/ppermute | solution.py:30
  35.4 1.1 %collective-permute-start.14 = (bf16[256,128]{1,0:T(8,128)(2,1)S(1)}, bf16[256,128]{1,0:T(8,128)(2,1)S(1)}, u32[]{:S(2)}, u32[]{:S(2)}) collective-permute-start(bf16[256,128]{1,0:T(8,128)(2,1)S(1)} %get-tuple-element.52.rest_0_), channel_id=1, source_target_pairs={{0,2},{1,3},{2,0},{3,1},{4,6},{5,7},{6,4},{7,5},{8,10},{9,11},{10,... | collective-permute-start | bytes 196616 | tf_op jit(solution)/shard_map/ppermute | solution.py:30
  36.7 1.0 %collective-permute-done.17.rest_2_ = bf16[128,256]{1,0:T(8,128)(2,1)S(1)} collective-permute-done((bf16[128,256]{1,0:T(8,128)(2,1)S(1)}, bf16[128,256]{1,0:T(8,128)(2,1)S(1)}, u32[]{:S(2)}, u32[]{:S(2)}) %collective-permute-start.17) | collective-permute-done | bytes 65568 | tf_op jit(solution)/shard_map/ppermute | solution.py:34
  37.8 0.8 %collective-permute-done.18.rest_3_ = bf16[128,256]{1,0:T(8,128)(2,1)S(1)} collective-permute-done((bf16[128,256]{1,0:T(8,128)(2,1)S(1)}, bf16[128,256]{1,0:T(8,128)(2,1)S(1)}, u32[]{:S(2)}, u32[]{:S(2)}) %collective-permute-start.18) | collective-permute-done | bytes 65568 | tf_op jit(solution)/shard_map/ppermute | solution.py:34
  38.6 2.8 %slot_backward.1 = (bf16[9,128,128]{2,1,0:T(8,128)(2,1)S(1)}, bf16[2,128,128]{2,1,0:T(8,128)(2,1)S(1)}, bf16[2,128,128]{2,1,0:T(8,128)(2,1)S(1)}, bf16[2,128,128...) custom-call(s32[1443]{0:T(1024)S(1)} %get-tuple-element.38.plan_ref,, ...), custom_call_target="tpu_custom_call" | custom-call | tf_op jit(solution)/shard_map/slot_backward/pallas_call | solution.py:412
  41.9 1.9 %collective-permute-start.20 = (bf16[2,128,128]{2,1,0:T(8,128)(2,1)S(1)}, bf16[2,128,128]{2,1,0:T(8,128)(2,1)S(1)}, u32[]{:S(2)}, u32[]{:S(2)}) collective-permute-start(bf16[2,128,128]{2,1,0:T(8,128)(2,1)S(1)} %get-tuple-element.60), channel_id=1, source_target_pairs={{8,0},{12,4},{0,8},{4,12},{24,16},{28,20},{16,24},{20,28},{9,1},{1... | collective-permute-start | bytes 196616 | tf_op jit(solution)/shard_map/ppermute | solution.py:34
  43.8 1.2 %collective-permute-start.21 = (bf16[2,128,128]{2,1,0:T(8,128)(2,1)S(1)}, bf16[2,128,128]{2,1,0:T(8,128)(2,1)S(1)}, u32[]{:S(2)}, u32[]{:S(2)}) collective-permute-start(bf16[2,128,128]{2,1,0:T(8,128)(2,1)S(1)} %get-tuple-element.61), channel_id=1, source_target_pairs={{12,0},{8,4},{4,8},{0,12},{28,16},{24,20},{20,24},{16,28},{13,1},{... | collective-permute-start | bytes 196616 | tf_op jit(solution)/shard_map/ppermute | solution.py:34
  45.0 2.5 %collective-permute-start.22 = (bf16[2,128,128]{2,1,0:T(8,128)(2,1)S(1)}, bf16[2,128,128]{2,1,0:T(8,128)(2,1)S(1)}, u32[]{:S(2)}, u32[]{:S(2)}) collective-permute-start(bf16[2,128,128]{2,1,0:T(8,128)(2,1)S(1)} %get-tuple-element.62), channel_id=1, source_target_pairs={{16,0},{20,4},{24,8},{28,12},{0,16},{4,20},{8,24},{12,28},{17,1},{... | collective-permute-start | bytes 196616 | tf_op jit(solution)/shard_map/ppermute | solution.py:34
  47.8 2.7 %collective-permute-start.24 = (bf16[2,128,128]{2,1,0:T(8,128)(2,1)S(1)}, bf16[2,128,128]{2,1,0:T(8,128)(2,1)S(1)}, u32[]{:S(2)}, u32[]{:S(2)}) collective-permute-start(bf16[2,128,128]{2,1,0:T(8,128)(2,1)S(1)} %get-tuple-element.64), channel_id=1, source_target_pairs={{24,0},{28,4},{16,8},{20,12},{8,16},{12,20},{0,24},{4,28},{25,1},{... | collective-permute-start | bytes 196616 | tf_op jit(solution)/shard_map/ppermute | solution.py:34
  50.5 2.2 %collective-permute-start.25 = (bf16[2,128,128]{2,1,0:T(8,128)(2,1)S(1)}, bf16[2,128,128]{2,1,0:T(8,128)(2,1)S(1)}, u32[]{:S(2)}, u32[]{:S(2)}) collective-permute-start(bf16[2,128,128]{2,1,0:T(8,128)(2,1)S(1)} %get-tuple-element.65), channel_id=1, source_target_pairs={{28,0},{24,4},{20,8},{16,12},{12,16},{8,20},{4,24},{0,28},{29,1},{... | collective-permute-start | bytes 196616 | tf_op jit(solution)/shard_map/ppermute | solution.py:34
  52.7 1.7 %local_backward.1.local_ref = f32[17,128,128]{2,1,0:T(8,128)S(1)} custom-call(s32[1443]{0:T(1024)S(1)} %get-tuple-element.38.plan_ref, bf16[128,128,128]{2,1,0:T(8,128)(2,1)S(1)} %get-tuple-element.40.weight_ref, bf16[9,128,128]{2,1,0:T(8,128)(2,1)S(1)} %get-tuple-element.57.rows_grad), custom_call_target="tpu_custom_call" | custom-call | flops 2147483648 | bytes 1024 | tf_op jit(solution)/shard_map/local_backward/pallas_call | solution.py:423
  54.4 0.7 %rows.1 = bf16[1024,128]{1,0:T(8,128)(2,1)} custom-call(bf16[256,128]{1,0:T(8,128)(2,1)S(1)} %get-tuple-element.52.rest_0_, bf16[256,128]{1,0:T(8,128)(2,1)S(1)} %collective-permute-done.13.rest_1_, bf16[256,128]{1,0:T(8,128)(2,1)S(1)} %collective-permute-done.14.rest_2_, bf16[256,128]{1,0:T(8,128)(2,1)S(1)} %collective-permute-done.15.rest_3_), custom_call_target="tpu_custom_call" | custom-call | tf_op jit(solution)/shard_map/rows/pallas_call | solution.py:433
  55.1 2.6 %collective-permute-done.23.rest_5_ = bf16[2,128,128]{2,1,0:T(8,128)(2,1)S(1)} collective-permute-done((bf16[2,128,128]{2,1,0:T(8,128)(2,1)S(1)}, bf16[2,128,128]{2,1,0:T(8,128)(2,1)S(1)}, u32[]{:S(2)}, u32[]{:S(2)}) %collective-permute-start.23) | collective-permute-done | bytes 65568 | tf_op jit(solution)/shard_map/ppermute | solution.py:34
  57.7 1.7 %final.1 = bf16[128,2048]{1,0:T(8,128)(2,1)} custom-call(s32[2,8]{1,0:T(2,128)S(1)} %bitcast.4, s32[8]{0:T(128)S(1)} %copy-done.5, f32[17,128,128]{2,1,0:T(8,128)S(1)} %local_backward.1.local_ref, bf16[2,128,128]{2,1,0:T(8,128)(2,1)S(1)} %get-tuple-element.58.rest_0_, bf16[2,128,128]{2,1,0:T(8,128)(2,1)S(1)} %collective-permute-done.19.rest_1_, ...), custom_call_target="tpu_custom_call" | custom-call | tf_op jit(solution)/shard_map/final/pallas_call | solution.py:442
  (40 shorter events, 2.1 us)
Async XLA Ops:
  0.6 21.4 %copy-start.1 = (bf16[128,2048]{1,0:T(8,128)(2,1)S(1)}, bf16[128,2048]{1,0:T(8,128)(2,1)}, u32[]{:S(2)}) copy-start(bf16[128,2048]{1,0:T(8,128)(2,1)} %rest_4_) | copy-start | bytes 1572868
  2.0 22.8 %collective-permute-start.11 = (bf16[128,2048]{1,0:T(8,128)(2,1)}, bf16[128,2048]{1,0:T(8,128)(2,1)S(1)}, u32[]{:S(2)}, u32[]{:S(2)}) collective-permute-start(bf16[128,2048]{1,0:T(8,128)(2,1)} %rest_4_), channel_id=1, source_target_pairs={{0,2},{1,3},{2,0},{3,1},{4,6},{5,7},{6,4},{7,5},{8,10},{9,11},{10,... | collective-permute-start | bytes 1572872 | tf_op jit(solution)/shard_map/ppermute | solution.py:30
  5.0 6.1 %collective-permute-start = (bf16[2,128,128]{2,1,0:T(8,128)(2,1)S(1)}, bf16[2,128,128]{2,1,0:T(8,128)(2,1)S(1)}, u32[]{:S(2)}, u32[]{:S(2)}) collective-permute-start(bf16[2,128,128]{2,1,0:T(8,128)(2,1)S(1)} %get-tuple-element.35), channel_id=1, source_target_pairs={{0,4},{4,0},{8,12},{12,8},{16,20},{20,16},{24,28},{28,24},{1,5},{5... | collective-permute-start | bytes 196616 | tf_op jit(solution)/shard_map/ppermute | solution.py:30
  6.5 6.3 %collective-permute-start.1 = (bf16[2,128,128]{2,1,0:T(8,128)(2,1)S(1)}, bf16[2,128,128]{2,1,0:T(8,128)(2,1)S(1)}, u32[]{:S(2)}, u32[]{:S(2)}) collective-permute-start(bf16[2,128,128]{2,1,0:T(8,128)(2,1)S(1)} %get-tuple-element.36), channel_id=1, source_target_pairs={{0,8},{4,12},{8,0},{12,4},{16,24},{20,28},{24,16},{28,20},{1,9},{5... | collective-permute-start | bytes 196616 | tf_op jit(solution)/shard_map/ppermute | solution.py:30
  8.1 7.9 %collective-permute-start.2 = (bf16[2,128,128]{2,1,0:T(8,128)(2,1)S(1)}, bf16[2,128,128]{2,1,0:T(8,128)(2,1)S(1)}, u32[]{:S(2)}, u32[]{:S(2)}) collective-permute-start(bf16[2,128,128]{2,1,0:T(8,128)(2,1)S(1)} %get-tuple-element.37), channel_id=1, source_target_pairs={{0,12},{4,8},{8,4},{12,0},{16,28},{20,24},{24,20},{28,16},{1,13},{... | collective-permute-start | bytes 196616 | tf_op jit(solution)/shard_map/ppermute | solution.py:30
  8.5 13.5 %collective-permute-start.3 = (bf16[2,128,128]{2,1,0:T(8,128)(2,1)S(1)}, bf16[2,128,128]{2,1,0:T(8,128)(2,1)S(1)}, u32[]{:S(2)}, u32[]{:S(2)}) collective-permute-start(bf16[2,128,128]{2,1,0:T(8,128)(2,1)S(1)} %get-tuple-element.41), channel_id=1, source_target_pairs={{0,16},{4,20},{8,24},{12,28},{16,0},{20,4},{24,8},{28,12},{1,17},{... | collective-permute-start | bytes 196616 | tf_op jit(solution)/shard_map/ppermute | solution.py:30
  11.1 11.0 %collective-permute-start.4 = (bf16[2,128,128]{2,1,0:T(8,128)(2,1)S(1)}, bf16[2,128,128]{2,1,0:T(8,128)(2,1)S(1)}, u32[]{:S(2)}, u32[]{:S(2)}) collective-permute-start(bf16[2,128,128]{2,1,0:T(8,128)(2,1)S(1)} %get-tuple-element.42), channel_id=1, source_target_pairs={{0,20},{4,16},{8,28},{12,24},{16,4},{20,0},{24,12},{28,8},{1,21},{... | collective-permute-start | bytes 196616 | tf_op jit(solution)/shard_map/ppermute | solution.py:30
  12.8 9.3 %collective-permute-start.5 = (bf16[2,128,128]{2,1,0:T(8,128)(2,1)S(1)}, bf16[2,128,128]{2,1,0:T(8,128)(2,1)S(1)}, u32[]{:S(2)}, u32[]{:S(2)}) collective-permute-start(bf16[2,128,128]{2,1,0:T(8,128)(2,1)S(1)} %get-tuple-element.43), channel_id=1, source_target_pairs={{0,24},{4,28},{8,16},{12,20},{16,8},{20,12},{24,0},{28,4},{1,25},{... | collective-permute-start | bytes 196616 | tf_op jit(solution)/shard_map/ppermute | solution.py:30
  15.9 7.1 %collective-permute-start.6 = (bf16[2,128,128]{2,1,0:T(8,128)(2,1)S(1)}, bf16[2,128,128]{2,1,0:T(8,128)(2,1)S(1)}, u32[]{:S(2)}, u32[]{:S(2)}) collective-permute-start(bf16[2,128,128]{2,1,0:T(8,128)(2,1)S(1)} %get-tuple-element.44), channel_id=1, source_target_pairs={{0,28},{4,24},{8,20},{12,16},{16,12},{20,8},{24,4},{28,0},{1,29},{... | collective-permute-start | bytes 196616 | tf_op jit(solution)/shard_map/ppermute | solution.py:30
  22.0 8.3 %copy-start = (bf16[2048,128]{1,0:T(8,128)(2,1)S(1)}, bf16[2048,128]{1,0:T(8,128)(2,1)}, u32[]{:S(2)}) copy-start(bf16[2048,128]{1,0:T(8,128)(2,1)} %w_out_ref.1) | copy-start | bytes 1572868
  22.0 8.3 %copy-start.2 = (bf16[1024,128]{1,0:T(8,128)(2,1)S(1)}, bf16[1024,128]{1,0:T(8,128)(2,1)}, u32[]{:S(2)}) copy-start(bf16[1024,128]{1,0:T(8,128)(2,1)} %g_ref.1) | copy-start | bytes 786436
  22.0 8.3 %copy-start.3 = (f32[2048]{0:T(1024)S(1)}, f32[2048]{0:T(1024)}, u32[]{:S(2)}) copy-start(f32[2048]{0:T(1024)} %param.17) | copy-start | bytes 24580
  22.0 8.2 %collective-permute-start.10 = (bf16[128,2048]{1,0:T(8,128)(2,1)S(1)}, bf16[128,2048]{1,0:T(8,128)(2,1)S(1)}, u32[]{:S(2)}, u32[]{:S(2)}) collective-permute-start(bf16[128,2048]{1,0:T(8,128)(2,1)S(1)} %copy-done.1), channel_id=1, source_target_pairs={{0,1},{1,0},{2,3},{3,2},{4,5},{5,4},{6,7},{7,6},{8,9},{9,8},{10,11... | collective-permute-start | bytes 1572872 | tf_op jit(solution)/shard_map/ppermute | solution.py:30
  24.8 5.5 %collective-permute-start.12 = (bf16[128,2048]{1,0:T(8,128)(2,1)S(1)}, bf16[128,2048]{1,0:T(8,128)(2,1)S(1)}, u32[]{:S(2)}, u32[]{:S(2)}) collective-permute-start(bf16[128,2048]{1,0:T(8,128)(2,1)S(1)} %collective-permute-done.11.rest_6_), channel_id=1, source_target_pairs={{0,1},{1,0},{2,3},{3,2},{4,5},{5,4},{6,7},{7,6},{8,9},{9,8},{10,11... | collective-permute-start | bytes 1572872 | tf_op jit(solution)/shard_map/ppermute | solution.py:30
  24.9 2.0 %collective-permute-start.7 = (bf16[256,128]{1,0:T(8,128)(2,1)S(1)}, bf16[256,128]{1,0:T(8,128)(2,1)S(1)}, u32[]{:S(2)}, u32[]{:S(2)}) collective-permute-start(bf16[256,128]{1,0:T(8,128)(2,1)S(1)} %get-tuple-element.46), channel_id=1, source_target_pairs={{0,1},{1,0},{2,3},{3,2},{4,5},{5,4},{6,7},{7,6},{8,9},{9,8},{10,11... | collective-permute-start | bytes 196616 | tf_op jit(solution)/shard_map/ppermute | solution.py:30
  25.4 4.9 %collective-permute-start.8 = (bf16[256,128]{1,0:T(8,128)(2,1)S(1)}, bf16[256,128]{1,0:T(8,128)(2,1)S(1)}, u32[]{:S(2)}, u32[]{:S(2)}) collective-permute-start(bf16[256,128]{1,0:T(8,128)(2,1)S(1)} %get-tuple-element.47), channel_id=1, source_target_pairs={{0,2},{1,3},{2,0},{3,1},{4,6},{5,7},{6,4},{7,5},{8,10},{9,11},{10,... | collective-permute-start | bytes 196616 | tf_op jit(solution)/shard_map/ppermute | solution.py:30
  25.9 4.4 %collective-permute-start.9 = (bf16[256,128]{1,0:T(8,128)(2,1)S(1)}, bf16[256,128]{1,0:T(8,128)(2,1)S(1)}, u32[]{:S(2)}, u32[]{:S(2)}) collective-permute-start(bf16[256,128]{1,0:T(8,128)(2,1)S(1)} %get-tuple-element.48), channel_id=1, source_target_pairs={{0,3},{1,2},{2,1},{3,0},{4,7},{5,6},{6,5},{7,4},{8,11},{9,10},{10,... | collective-permute-start | bytes 196616 | tf_op jit(solution)/shard_map/ppermute | solution.py:30
  32.7 3.8 %collective-permute-start.16 = (bf16[128,256]{1,0:T(8,128)(2,1)S(1)}, bf16[128,256]{1,0:T(8,128)(2,1)S(1)}, u32[]{:S(2)}, u32[]{:S(2)}) collective-permute-start(bf16[128,256]{1,0:T(8,128)(2,1)S(1)} %get-tuple-element.54), channel_id=1, source_target_pairs={{1,0},{0,1},{3,2},{2,3},{5,4},{4,5},{7,6},{6,7},{9,8},{8,9},{11,10... | collective-permute-start | bytes 196616 | tf_op jit(solution)/shard_map/ppermute | solution.py:34
  33.2 4.5 %collective-permute-start.17 = (bf16[128,256]{1,0:T(8,128)(2,1)S(1)}, bf16[128,256]{1,0:T(8,128)(2,1)S(1)}, u32[]{:S(2)}, u32[]{:S(2)}) collective-permute-start(bf16[128,256]{1,0:T(8,128)(2,1)S(1)} %get-tuple-element.55), channel_id=1, source_target_pairs={{2,0},{3,1},{0,2},{1,3},{6,4},{7,5},{4,6},{5,7},{10,8},{11,9},{8,1... | collective-permute-start | bytes 196616 | tf_op jit(solution)/shard_map/ppermute | solution.py:34
  34.3 4.3 %collective-permute-start.18 = (bf16[128,256]{1,0:T(8,128)(2,1)S(1)}, bf16[128,256]{1,0:T(8,128)(2,1)S(1)}, u32[]{:S(2)}, u32[]{:S(2)}) collective-permute-start(bf16[128,256]{1,0:T(8,128)(2,1)S(1)} %get-tuple-element.56), channel_id=1, source_target_pairs={{3,0},{2,1},{1,2},{0,3},{7,4},{6,5},{5,6},{4,7},{11,8},{10,9},{9,1... | collective-permute-start | bytes 196616 | tf_op jit(solution)/shard_map/ppermute | solution.py:34
  34.7 9.1 %collective-permute-start.13 = (bf16[256,128]{1,0:T(8,128)(2,1)S(1)}, bf16[256,128]{1,0:T(8,128)(2,1)S(1)}, u32[]{:S(2)}, u32[]{:S(2)}) collective-permute-start(bf16[256,128]{1,0:T(8,128)(2,1)S(1)} %get-tuple-element.52.rest_0_), channel_id=1, source_target_pairs={{0,1},{1,0},{2,3},{3,2},{4,5},{5,4},{6,7},{7,6},{8,9},{9,8},{10,11... | collective-permute-start | bytes 196616 | tf_op jit(solution)/shard_map/ppermute | solution.py:30
  35.4 9.6 %collective-permute-start.14 = (bf16[256,128]{1,0:T(8,128)(2,1)S(1)}, bf16[256,128]{1,0:T(8,128)(2,1)S(1)}, u32[]{:S(2)}, u32[]{:S(2)}) collective-permute-start(bf16[256,128]{1,0:T(8,128)(2,1)S(1)} %get-tuple-element.52.rest_0_), channel_id=1, source_target_pairs={{0,2},{1,3},{2,0},{3,1},{4,6},{5,7},{6,4},{7,5},{8,10},{9,11},{10,... | collective-permute-start | bytes 196616 | tf_op jit(solution)/shard_map/ppermute | solution.py:30
  36.4 11.1 %collective-permute-start.15 = (bf16[256,128]{1,0:T(8,128)(2,1)S(1)}, bf16[256,128]{1,0:T(8,128)(2,1)S(1)}, u32[]{:S(2)}, u32[]{:S(2)}) collective-permute-start(bf16[256,128]{1,0:T(8,128)(2,1)S(1)} %get-tuple-element.52.rest_0_), channel_id=1, source_target_pairs={{0,3},{1,2},{2,1},{3,0},{4,7},{5,6},{6,5},{7,4},{8,11},{9,10},{10,... | collective-permute-start | bytes 196616 | tf_op jit(solution)/shard_map/ppermute | solution.py:30
  41.4 6.4 %collective-permute-start.19 = (bf16[2,128,128]{2,1,0:T(8,128)(2,1)S(1)}, bf16[2,128,128]{2,1,0:T(8,128)(2,1)S(1)}, u32[]{:S(2)}, u32[]{:S(2)}) collective-permute-start(bf16[2,128,128]{2,1,0:T(8,128)(2,1)S(1)} %get-tuple-element.59), channel_id=1, source_target_pairs={{4,0},{0,4},{12,8},{8,12},{20,16},{16,20},{28,24},{24,28},{5,1},{1... | collective-permute-start | bytes 196616 | tf_op jit(solution)/shard_map/ppermute | solution.py:34
  41.9 8.5 %collective-permute-start.20 = (bf16[2,128,128]{2,1,0:T(8,128)(2,1)S(1)}, bf16[2,128,128]{2,1,0:T(8,128)(2,1)S(1)}, u32[]{:S(2)}, u32[]{:S(2)}) collective-permute-start(bf16[2,128,128]{2,1,0:T(8,128)(2,1)S(1)} %get-tuple-element.60), channel_id=1, source_target_pairs={{8,0},{12,4},{0,8},{4,12},{24,16},{28,20},{16,24},{20,28},{9,1},{1... | collective-permute-start | bytes 196616 | tf_op jit(solution)/shard_map/ppermute | solution.py:34
  43.8 11.3 %collective-permute-start.21 = (bf16[2,128,128]{2,1,0:T(8,128)(2,1)S(1)}, bf16[2,128,128]{2,1,0:T(8,128)(2,1)S(1)}, u32[]{:S(2)}, u32[]{:S(2)}) collective-permute-start(bf16[2,128,128]{2,1,0:T(8,128)(2,1)S(1)} %get-tuple-element.61), channel_id=1, source_target_pairs={{12,0},{8,4},{4,8},{0,12},{28,16},{24,20},{20,24},{16,28},{13,1},{... | collective-permute-start | bytes 196616 | tf_op jit(solution)/shard_map/ppermute | solution.py:34
  45.0 10.1 %collective-permute-start.22 = (bf16[2,128,128]{2,1,0:T(8,128)(2,1)S(1)}, bf16[2,128,128]{2,1,0:T(8,128)(2,1)S(1)}, u32[]{:S(2)}, u32[]{:S(2)}) collective-permute-start(bf16[2,128,128]{2,1,0:T(8,128)(2,1)S(1)} %get-tuple-element.62), channel_id=1, source_target_pairs={{16,0},{20,4},{24,8},{28,12},{0,16},{4,20},{8,24},{12,28},{17,1},{... | collective-permute-start | bytes 196616 | tf_op jit(solution)/shard_map/ppermute | solution.py:34
  47.5 10.2 %collective-permute-start.23 = (bf16[2,128,128]{2,1,0:T(8,128)(2,1)S(1)}, bf16[2,128,128]{2,1,0:T(8,128)(2,1)S(1)}, u32[]{:S(2)}, u32[]{:S(2)}) collective-permute-start(bf16[2,128,128]{2,1,0:T(8,128)(2,1)S(1)} %get-tuple-element.63), channel_id=1, source_target_pairs={{20,0},{16,4},{28,8},{24,12},{4,16},{0,20},{12,24},{8,28},{21,1},{... | collective-permute-start | bytes 196616 | tf_op jit(solution)/shard_map/ppermute | solution.py:34
  47.8 9.9 %collective-permute-start.24 = (bf16[2,128,128]{2,1,0:T(8,128)(2,1)S(1)}, bf16[2,128,128]{2,1,0:T(8,128)(2,1)S(1)}, u32[]{:S(2)}, u32[]{:S(2)}) collective-permute-start(bf16[2,128,128]{2,1,0:T(8,128)(2,1)S(1)} %get-tuple-element.64), channel_id=1, source_target_pairs={{24,0},{28,4},{16,8},{20,12},{8,16},{12,20},{0,24},{4,28},{25,1},{... | collective-permute-start | bytes 196616 | tf_op jit(solution)/shard_map/ppermute | solution.py:34
  50.5 7.2 %collective-permute-start.25 = (bf16[2,128,128]{2,1,0:T(8,128)(2,1)S(1)}, bf16[2,128,128]{2,1,0:T(8,128)(2,1)S(1)}, u32[]{:S(2)}, u32[]{:S(2)}) collective-permute-start(bf16[2,128,128]{2,1,0:T(8,128)(2,1)S(1)} %get-tuple-element.65), channel_id=1, source_target_pairs={{28,0},{24,4},{20,8},{16,12},{12,16},{8,20},{4,24},{0,28},{29,1},{... | collective-permute-start | bytes 196616 | tf_op jit(solution)/shard_map/ppermute | solution.py:34
  52.7 5.0 %copy-start.4 = (s32[8,2]{0,1:T(2,128)S(1)}, s32[8,2]{0,1:T(2,128)}, u32[]{:S(2)}) copy-start(s32[8,2]{0,1:T(2,128)} %param.12) | copy-start | bytes 196
  52.7 5.0 %copy-start.5 = (s32[8]{0:T(128)S(1)}, s32[8]{0:T(128)}, u32[]{:S(2)}) copy-start(s32[8]{0:T(128)} %counts_ref.1) | copy-start | bytes 100

commit v5 on v4

--- a/solution.py
+++ b/solution.py
@@ -84,24 +84,30 @@
 
 
 class Plan:
+    LOCAL, NEAR, FAR, SLOTS = range(4)
+
     def __init__(self, edges):
         self.edges = edges
         self.length = edges + UNROLL
 
     def size(self):
-        return 9 * self.length + 3
-
-    def at(self, kind, field):
-        return (kind * 3 + field) * self.length
+        return 6 * self.length + 2
 
     def make(self, ref, src_ref, obs_ref, nodes, obs, dom, cap):
         me = lax.axis_index("dom")
+        length, edges = self.length, self.edges
         mask = None
         if dom * cap <= 31:
             bits = (1 << cap) - 1
             mask = sum(bits << (source(me, d, dom) * cap) for d in range(dom) if is_near(d, dom))
 
+        def put(base, e, src, block):
+            ref[base] = e
+            ref[base + length] = src
+            ref[base + 2 * length] = block
+
         def one(e, counts):
+            n_local, n_near = counts
             src = src_ref[e]
             slot = jnp.maximum(src - nodes, 0)
             if mask is not None:
@@ -111,39 +117,44 @@
                 near = is_near(shift, dom).astype(jnp.int32)
             local = (src < nodes).astype(jnp.int32)
             near = (1 - local) * near
-            far = 1 - local - near
-            kind = near + 2 * far
-            i = local * counts[0] + near * counts[1] + far * counts[2]
-            base = kind * 3 * self.length + i
-            ref[base] = e
-            ref[base + self.length] = jnp.where(local == 1, src, slot)
-            ref[base + 2 * self.length] = obs_ref[e]
-            return counts[0] + local, counts[1] + near, counts[2] + far
-
-        zero = jnp.int32(0)
-        counts = lax.fori_loop(0, self.edges, one, (zero, zero, zero), unroll=4)
-        for kind in range(3):
-            trash = nodes if kind == 0 else dom * cap
-            start = counts[kind]
-
-            def fill(i, carry):
-                base = kind * 3 * self.length + start + i
-                ref[base] = 0
-                ref[base + self.length] = trash
-                ref[base + 2 * self.length] = obs
-                return carry
-
-            lax.fori_loop(0, UNROLL, fill, 0, unroll=4)
-            ref[9 * self.length + kind] = start
+            n_far = e - n_local - n_near
+            at_slot = 3 * length + jnp.where(near == 1, n_near, edges - 1 - n_far)
+            put(jnp.where(local == 1, n_local, at_slot), e, jnp.where(local == 1, src, slot), obs_ref[e])
+            return n_local + local, n_near + near
+
+        n_local, n_near = lax.fori_loop(0, edges, one, (jnp.int32(0), jnp.int32(0)), unroll=4)
+
+        def fill(i, carry):
+            put(n_local + i, 0, nodes, obs)
+            put(3 * length + edges + i, 0, dom * cap, obs)
+            return carry
+
+        lax.fori_loop(0, UNROLL, fill, 0, unroll=4)
+        ref[6 * length] = n_local
+        ref[6 * length + 1] = n_near
 
     def run(self, ref, kind, body):
+        length, edges = self.length, self.edges
+        n_local, n_near = ref[6 * length], ref[6 * length + 1]
+        n_slots = edges - n_local
+        count = (n_local, n_near, n_slots - n_near, n_slots)[kind]
+        base = 0 if kind == self.LOCAL else 3 * length
+
+        def place(i):
+            if kind == self.NEAR:
+                return base + jnp.where(i < n_near, i, edges)
+            if kind == self.FAR:
+                return base + n_local + n_near + i
+            if kind == self.SLOTS:
+                return base + jnp.where(i < n_near, i, i + n_local)
+            return i
+
         def step(t, carry):
             for u in range(UNROLL):
-                i = kind * 3 * self.length + t * UNROLL + u
-                body(ref[i], ref[i + self.length], ref[i + 2 * self.length])
+                at = place(t * UNROLL + u)
+                body(ref[at], ref[at + length], ref[at + 2 * length])
             return carry
 
-        count = ref[9 * self.length + kind]
         lax.fori_loop(0, (count + UNROLL - 1) // UNROLL, step, 0)
 
 
@@ -172,8 +183,8 @@
     def body(e, k, j):
         sum_ref[j] += lax.dot_general(weight_ref[e], pool[k], NN, preferred_element_type=F32)
 
-    plan.run(plan_ref, 0, body)
-    add_slots(plan, 1, shifts, dom, cap, plan_ref, weight_ref, arrived, slots, sum_ref)
+    plan.run(plan_ref, plan.LOCAL, body)
+    add_slots(plan, plan.NEAR, shifts, dom, cap, plan_ref, weight_ref, arrived, slots, sum_ref)
 
 
 def add_slots(plan, kind, shifts, dom, cap, plan_ref, weight_ref, arrived, pool, total):
@@ -193,7 +204,7 @@
     count = len(shifts)
     arrived, outs, (pool, total) = rest[:count], rest[count : count + chan], rest[count + chan :]
     total[...] = sum_ref[...]
-    add_slots(plan, 2, shifts, dom, cap, plan_ref, weight_ref, arrived, pool, total)
+    add_slots(plan, plan.FAR, shifts, dom, cap, plan_ref, weight_ref, arrived, pool, total)
     whole = total.reshape(total.shape[0] * total.shape[1], total.shape[2])
     rows = outs[0].shape[0]
     mine = lax.axis_index("chan")
@@ -258,8 +269,7 @@
     def body(e, k, j):
         total[k] += lax.dot_general(rows_grad[j], weight_ref[e], NN, preferred_element_type=F32)
 
-    plan.run(plan_ref, 1, body)
-    plan.run(plan_ref, 2, body)
+    plan.run(plan_ref, plan.SLOTS, body)
     me = lax.axis_index("dom")
     for d in range(dom):
         outs[d][...] = total[pl.ds(source(me, d, dom) * cap, cap)].astype(BF16)
@@ -271,7 +281,7 @@
     def body(e, k, j):
         total[k] += lax.dot_general(rows_grad[j], weight_ref[e], NN, preferred_element_type=F32)
 
-    plan.run(plan_ref, 0, body)
+    plan.run(plan_ref, plan.LOCAL, body)
 
 
 def rows_kernel(chan, *rest):
@@ -293,10 +303,10 @@
             total[jnp.clip(blocks_ref[s, q], 0, nodes - 1)] += value
 
 
-def final_kernel(dom, cap, blk, nodes, blocks_ref, counts_ref, local_ref, *rest):
+def final_kernel(order, dom, cap, blk, nodes, blocks_ref, counts_ref, local_ref, *rest):
     returned, (grad_ref, total) = rest[:dom], rest[dom:]
     total[...] = local_ref[:nodes]
-    add_returned(range(dom), dom, cap, nodes, blocks_ref, counts_ref, returned, total)
+    add_returned(order, dom, cap, nodes, blocks_ref, counts_ref, returned, total)
     for k in range(nodes):
         grad_ref[:, k * blk : (k + 1) * blk] = total[k].astype(BF16)
 
@@ -393,7 +403,7 @@
     shares = {d: send(shares[d], "chan", d, chan) if d else shares[0] for d in reversed(range(chan))}
 
     mlp = pl.pallas_call(
-        functools.partial(mlp_kernel, chan, min(512, hidden_width)),
+        functools.partial(mlp_kernel, chan, min(1024, hidden_width)),
         out_shape=[shape((rows, out_width), BF16)] + [shape((feat, rows), BF16)] * chan,
         in_specs=vmem(3 + 2 * chan),
         out_specs=vmem(1 + chan),
@@ -439,15 +449,16 @@
         name="rows",
     )(*[obs_parts[d] for d in range(chan)])
 
+    back_order = near[:2] + far[::2] + far[1::2] + near[2:]
     d_latent = pl.pallas_call(
-        functools.partial(final_kernel, dom, cap, blk, nodes),
+        functools.partial(final_kernel, back_order, dom, cap, blk, nodes),
         out_shape=shape((feat, cols), BF16),
         in_specs=smem(2) + vmem(1 + dom),
         out_specs=pl.BlockSpec(memory_space=pltpu.VMEM),
         scratch_shapes=[pltpu.VMEM((nodes, feat, blk), F32)],
         compiler_params=params(),
         name="final",
-    )(*tables, local_grad, *returned)
+    )(*tables, local_grad, *[returned[d] for d in back_order])
     return obs_out, d_latent
 
 

time: 60.1 us -> 58.8 us (0.978)
  waiting for transfers between devices: 8.86 us -> 9.91 us
  Pallas kernels: 17.6 us -> 16.7 us
  starting transfers between devices: 32 us -> 31.1 us
    ppermute x10, starting transfers between devices: 13.2 us -> 12.3 us  [send_back(): lax.ppermute(value, axis, [(target(i, shift, count), i) for i in range(co...]
    ppermute x10, waiting for transfers between devices: 4.47 us -> 5.36 us  [send_back(): lax.ppermute(value, axis, [(target(i, shift, count), i) for i in range(co...]
  transfers between devices with their start and end apart: 26 -> 26, of which waited for: 6 -> 8; matrix products, arithmetic and copies ran while one was open for 0% -> 0% of each run, Pallas kernels for 21% -> 20%
where the time goes in v5:
time: 58.8 us; the launch traced here: 58.6 us
  starting transfers between devices  31.1 us (53%)
  Pallas kernels  16.7 us (28%)
  waiting for transfers between devices  9.91 us (17%)
  between operations  0.81 us (1%)
    ppermute x16, starting transfers between devices, send(): lax.ppermute(value, axis, [(i, target(i, shift, count)) for i in range(co...  18.8 us
    ppermute x10, starting transfers between devices, send_back(): lax.ppermute(value, axis, [(target(i, shift, count), i) for i in range(co...  12.3 us
    ppermute x10, waiting for transfers between devices, send_back(): lax.ppermute(value, axis, [(target(i, shift, count), i) for i in range(co...  5.36 us
    pallas_call x1, Pallas kernels, on_device(): pl.pallas_call(functools.partial(first_forward_kernel, plan, near, dom, c...  5.14 us
    ppermute x16, waiting for transfers between devices, send(): lax.ppermute(value, axis, [(i, target(i, shift, count)) for i in range(co...  4.55 us
    pallas_call x1, Pallas kernels, on_device(): pl.pallas_call(functools.partial(slot_backward_kernel, plan, dom, cap, ch...  2.26 us
    pallas_call x1, Pallas kernels, on_device(): pl.pallas_call(functools.partial(mlp_kernel, chan, min(1024, hidden_width...  2.19 us
    pallas_call x1, Pallas kernels, on_device(): pl.pallas_call(functools.partial(far_forward_kernel, plan, far, dom, cap,...  1.76 us
  transfers between devices with their start and end apart: 26, of which 8 were waited for; matrix products, arithmetic and copies ran while one was open for 0% of the time, Pallas kernels for 20%

profile of v5, /device:TPU:0, one launch (start us, length us, event | category | flops | bytes accessed | tf_op | source)
XLA Modules:
  0.0 58.6 jit_solution(567334024934625814)
XLA Ops:
  0.6 1.3 %pack.1 = (bf16[2,128,128]{2,1,0:T(8,128)(2,1)S(1)}, bf16[2,128,128]{2,1,0:T(8,128)(2,1)S(1)}, bf16[2,128,128]{2,1,0:T(8,128)(2,1)S(1)}, bf16[2,128,128]{2,1,0:T...) custom-call(s32[2,8]{1,0:T(2,128)} %bitcast.3, ...), custom_call_target="tpu_custom_call" | custom-call | tf_op jit(solution)/shard_map/pack/pallas_call | solution.py:338
  2.0 3.0 %collective-permute-start.11 = (bf16[128,2048]{1,0:T(8,128)(2,1)}, bf16[128,2048]{1,0:T(8,128)(2,1)S(1)}, u32[]{:S(2)}, u32[]{:S(2)}) collective-permute-start(bf16[128,2048]{1,0:T(8,128)(2,1)} %rest_4_), channel_id=1, source_target_pairs={{0,2},{1,3},{2,0},{3,1},{4,6},{5,7},{6,4},{7,5},{8,10},{9,11},{10,... | collective-permute-start | bytes 1572872 | tf_op jit(solution)/shard_map/ppermute | solution.py:30
  5.0 1.5 %collective-permute-start = (bf16[2,128,128]{2,1,0:T(8,128)(2,1)S(1)}, bf16[2,128,128]{2,1,0:T(8,128)(2,1)S(1)}, u32[]{:S(2)}, u32[]{:S(2)}) collective-permute-start(bf16[2,128,128]{2,1,0:T(8,128)(2,1)S(1)} %get-tuple-element.35), channel_id=1, source_target_pairs={{0,4},{4,0},{8,12},{12,8},{16,20},{20,16},{24,28},{28,24},{1,5},{5... | collective-permute-start | bytes 196616 | tf_op jit(solution)/shard_map/ppermute | solution.py:30
  6.5 1.6 %collective-permute-start.1 = (bf16[2,128,128]{2,1,0:T(8,128)(2,1)S(1)}, bf16[2,128,128]{2,1,0:T(8,128)(2,1)S(1)}, u32[]{:S(2)}, u32[]{:S(2)}) collective-permute-start(bf16[2,128,128]{2,1,0:T(8,128)(2,1)S(1)} %get-tuple-element.36), channel_id=1, source_target_pairs={{0,8},{4,12},{8,0},{12,4},{16,24},{20,28},{24,16},{28,20},{1,9},{5... | collective-permute-start | bytes 196616 | tf_op jit(solution)/shard_map/ppermute | solution.py:30
  8.5 2.6 %collective-permute-start.3 = (bf16[2,128,128]{2,1,0:T(8,128)(2,1)S(1)}, bf16[2,128,128]{2,1,0:T(8,128)(2,1)S(1)}, u32[]{:S(2)}, u32[]{:S(2)}) collective-permute-start(bf16[2,128,128]{2,1,0:T(8,128)(2,1)S(1)} %get-tuple-element.41), channel_id=1, source_target_pairs={{0,16},{4,20},{8,24},{12,28},{16,0},{20,4},{24,8},{28,12},{1,17},{... | collective-permute-start | bytes 196616 | tf_op jit(solution)/shard_map/ppermute | solution.py:30
  11.1 1.7 %collective-permute-start.4 = (bf16[2,128,128]{2,1,0:T(8,128)(2,1)S(1)}, bf16[2,128,128]{2,1,0:T(8,128)(2,1)S(1)}, u32[]{:S(2)}, u32[]{:S(2)}) collective-permute-start(bf16[2,128,128]{2,1,0:T(8,128)(2,1)S(1)} %get-tuple-element.42), channel_id=1, source_target_pairs={{0,20},{4,16},{8,28},{12,24},{16,4},{20,0},{24,12},{28,8},{1,21},{... | collective-permute-start | bytes 196616 | tf_op jit(solution)/shard_map/ppermute | solution.py:30
  12.8 3.2 %collective-permute-start.5 = (bf16[2,128,128]{2,1,0:T(8,128)(2,1)S(1)}, bf16[2,128,128]{2,1,0:T(8,128)(2,1)S(1)}, u32[]{:S(2)}, u32[]{:S(2)}) collective-permute-start(bf16[2,128,128]{2,1,0:T(8,128)(2,1)S(1)} %get-tuple-element.43), channel_id=1, source_target_pairs={{0,24},{4,28},{8,16},{12,20},{16,8},{20,12},{24,0},{28,4},{1,25},{... | collective-permute-start | bytes 196616 | tf_op jit(solution)/shard_map/ppermute | solution.py:30
  15.9 0.7 %collective-permute-start.6 = (bf16[2,128,128]{2,1,0:T(8,128)(2,1)S(1)}, bf16[2,128,128]{2,1,0:T(8,128)(2,1)S(1)}, u32[]{:S(2)}, u32[]{:S(2)}) collective-permute-start(bf16[2,128,128]{2,1,0:T(8,128)(2,1)S(1)} %get-tuple-element.44), channel_id=1, source_target_pairs={{0,28},{4,24},{8,20},{12,16},{16,12},{20,8},{24,4},{28,0},{1,29},{... | collective-permute-start | bytes 196616 | tf_op jit(solution)/shard_map/ppermute | solution.py:30
  16.7 5.1 %first_forward.1 = (f32[9,128,128]{2,1,0:T(8,128)S(1)}, s32[962]{0:T(1024)S(1)}, bf16[128,128,128]{2,1,0:T(8,128)(2,1)S(1)}) custom-call(s32[128]{0:T(128)} %src_hbm.1, s32[128]{0:T(128)} %obs_hbm.1, bf16[128,2048]{1,0:T(8,128)(2,1)} %latent_hbm.3, bf16[128,128,128]{2,1,0:T(8,128)(2,1)} %weight_hbm.1, bf16[2,128,128]{2,1,0:T(8,128)(2,1)S(1)} %get-tuple-element.34.rest_0_, ...), custom_call_target="tpu_custom_call" | custom-call | flops 2147483648 | bytes 1024 | tf_op jit(solution)/shard_map/first_forward/pallas_call | solution.py:364
  22.0 1.0 %collective-permute-done.6.rest_3_ = bf16[2,128,128]{2,1,0:T(8,128)(2,1)S(1)} collective-permute-done((bf16[2,128,128]{2,1,0:T(8,128)(2,1)S(1)}, bf16[2,128,128]{2,1,0:T(8,128)(2,1)S(1)}, u32[]{:S(2)}, u32[]{:S(2)}) %collective-permute-start.6) | collective-permute-done | bytes 65568 | tf_op jit(solution)/shard_map/ppermute | solution.py:30
  23.0 1.8 %far_forward.1 = (bf16[256,128]{1,0:T(8,128)(2,1)S(1)}, bf16[256,128]{1,0:T(8,128)(2,1)S(1)}, bf16[256,128]{1,0:T(8,128)(2,1)S(1)}, bf16[256,128]{1,0:T(8,128)(2,1)S(1)}) custom-call(s32[962]{0:T(1024)S(1)} %get-tuple-element.38.plan_ref, f32[9,128,128]{2,1,0:T(8,128)S(1)} %get-tuple-element.39.sum_ref, ...), custom_call_target="tpu_custom_call" | custom-call | tf_op jit(solution)/shard_map/far_forward/pallas_call | solution.py:386
  25.9 0.9 %collective-permute-start.9 = (bf16[256,128]{1,0:T(8,128)(2,1)S(1)}, bf16[256,128]{1,0:T(8,128)(2,1)S(1)}, u32[]{:S(2)}, u32[]{:S(2)}) collective-permute-start(bf16[256,128]{1,0:T(8,128)(2,1)S(1)} %get-tuple-element.48), channel_id=1, source_target_pairs={{0,3},{1,2},{2,1},{3,0},{4,7},{5,6},{6,5},{7,4},{8,11},{9,10},{10,... | collective-permute-start | bytes 196616 | tf_op jit(solution)/shard_map/ppermute | solution.py:30
  26.9 3.4 %collective-permute-done.8.rest_2_ = bf16[256,128]{1,0:T(8,128)(2,1)S(1)} collective-permute-done((bf16[256,128]{1,0:T(8,128)(2,1)S(1)}, bf16[256,128]{1,0:T(8,128)(2,1)S(1)}, u32[]{:S(2)}, u32[]{:S(2)}) %collective-permute-start.8) | collective-permute-done | bytes 65568 | tf_op jit(solution)/shard_map/ppermute | solution.py:30
  30.3 2.2 %mlp.1 = (bf16[256,128]{1,0:T(8,128)(2,1)S(1)}, bf16[128,256]{1,0:T(8,128)(2,1)S(1)}, bf16[128,256]{1,0:T(8,128)(2,1)S(1)}, bf16[128,256]{1,0:T(8,128)(2,1)S(1)}, bf16[128,256]{1,0:T(8,128)(2,1)S(1)}) custom-call(f32[1,2048]{1,0:T(1,128)S(1)} %bitcast.2, bf16[2048,128]{1,0:T(8,128)(2,1)S(1)} %copy-done, bf16[1024,128]{1,0:T(8,128)(2,1)S(1)} %copy-done.2, ...), custom_call_target="tpu_custom_call" | custom-call | tf_op jit(solution)/shard_map/mlp/pallas_call | solution.py:405
  33.1 1.1 %collective-permute-start.17 = (bf16[128,256]{1,0:T(8,128)(2,1)S(1)}, bf16[128,256]{1,0:T(8,128)(2,1)S(1)}, u32[]{:S(2)}, u32[]{:S(2)}) collective-permute-start(bf16[128,256]{1,0:T(8,128)(2,1)S(1)} %get-tuple-element.55), channel_id=1, source_target_pairs={{2,0},{3,1},{0,2},{1,3},{6,4},{7,5},{4,6},{5,7},{10,8},{11,9},{8,1... | collective-permute-start | bytes 196616 | tf_op jit(solution)/shard_map/ppermute | solution.py:34
  34.5 0.7 %collective-permute-start.13 = (bf16[256,128]{1,0:T(8,128)(2,1)S(1)}, bf16[256,128]{1,0:T(8,128)(2,1)S(1)}, u32[]{:S(2)}, u32[]{:S(2)}) collective-permute-start(bf16[256,128]{1,0:T(8,128)(2,1)S(1)} %get-tuple-element.52.rest_0_), channel_id=1, source_target_pairs={{0,1},{1,0},{2,3},{3,2},{4,5},{5,4},{6,7},{7,6},{8,9},{9,8},{10,11... | collective-permute-start | bytes 196616 | tf_op jit(solution)/shard_map/ppermute | solution.py:30
  35.2 1.1 %collective-permute-start.14 = (bf16[256,128]{1,0:T(8,128)(2,1)S(1)}, bf16[256,128]{1,0:T(8,128)(2,1)S(1)}, u32[]{:S(2)}, u32[]{:S(2)}) collective-permute-start(bf16[256,128]{1,0:T(8,128)(2,1)S(1)} %get-tuple-element.52.rest_0_), channel_id=1, source_target_pairs={{0,2},{1,3},{2,0},{3,1},{4,6},{5,7},{6,4},{7,5},{8,10},{9,11},{10,... | collective-permute-start | bytes 196616 | tf_op jit(solution)/shard_map/ppermute | solution.py:30
  36.6 1.0 %collective-permute-done.17.rest_2_ = bf16[128,256]{1,0:T(8,128)(2,1)S(1)} collective-permute-done((bf16[128,256]{1,0:T(8,128)(2,1)S(1)}, bf16[128,256]{1,0:T(8,128)(2,1)S(1)}, u32[]{:S(2)}, u32[]{:S(2)}) %collective-permute-start.17) | collective-permute-done | bytes 65568 | tf_op jit(solution)/shard_map/ppermute | solution.py:34
  37.6 0.8 %collective-permute-done.18.rest_3_ = bf16[128,256]{1,0:T(8,128)(2,1)S(1)} collective-permute-done((bf16[128,256]{1,0:T(8,128)(2,1)S(1)}, bf16[128,256]{1,0:T(8,128)(2,1)S(1)}, u32[]{:S(2)}, u32[]{:S(2)}) %collective-permute-start.18) | collective-permute-done | bytes 65568 | tf_op jit(solution)/shard_map/ppermute | solution.py:34
  38.5 2.3 %slot_backward.1 = (bf16[9,128,128]{2,1,0:T(8,128)(2,1)S(1)}, bf16[2,128,128]{2,1,0:T(8,128)(2,1)S(1)}, bf16[2,128,128]{2,1,0:T(8,128)(2,1)S(1)}, bf16[2,128,128...) custom-call(s32[962]{0:T(1024)S(1)} %get-tuple-element.38.plan_ref, ...), custom_call_target="tpu_custom_call" | custom-call | tf_op jit(solution)/shard_map/slot_backward/pallas_call | solution.py:422
  41.3 2.2 %collective-permute-start.20 = (bf16[2,128,128]{2,1,0:T(8,128)(2,1)S(1)}, bf16[2,128,128]{2,1,0:T(8,128)(2,1)S(1)}, u32[]{:S(2)}, u32[]{:S(2)}) collective-permute-start(bf16[2,128,128]{2,1,0:T(8,128)(2,1)S(1)} %get-tuple-element.60), channel_id=1, source_target_pairs={{16,0},{20,4},{24,8},{28,12},{0,16},{4,20},{8,24},{12,28},{17,1},{... | collective-permute-start | bytes 196616 | tf_op jit(solution)/shard_map/ppermute | solution.py:34
  43.5 2.0 %collective-permute-start.21 = (bf16[2,128,128]{2,1,0:T(8,128)(2,1)S(1)}, bf16[2,128,128]{2,1,0:T(8,128)(2,1)S(1)}, u32[]{:S(2)}, u32[]{:S(2)}) collective-permute-start(bf16[2,128,128]{2,1,0:T(8,128)(2,1)S(1)} %get-tuple-element.61), channel_id=1, source_target_pairs={{24,0},{28,4},{16,8},{20,12},{8,16},{12,20},{0,24},{4,28},{25,1},{... | collective-permute-start | bytes 196616 | tf_op jit(solution)/shard_map/ppermute | solution.py:34
  45.5 0.8 %collective-permute-start.22 = (bf16[2,128,128]{2,1,0:T(8,128)(2,1)S(1)}, bf16[2,128,128]{2,1,0:T(8,128)(2,1)S(1)}, u32[]{:S(2)}, u32[]{:S(2)}) collective-permute-start(bf16[2,128,128]{2,1,0:T(8,128)(2,1)S(1)} %get-tuple-element.62), channel_id=1, source_target_pairs={{20,0},{16,4},{28,8},{24,12},{4,16},{0,20},{12,24},{8,28},{21,1},{... | collective-permute-start | bytes 196616 | tf_op jit(solution)/shard_map/ppermute | solution.py:34
  46.2 2.4 %collective-permute-start.23 = (bf16[2,128,128]{2,1,0:T(8,128)(2,1)S(1)}, bf16[2,128,128]{2,1,0:T(8,128)(2,1)S(1)}, u32[]{:S(2)}, u32[]{:S(2)}) collective-permute-start(bf16[2,128,128]{2,1,0:T(8,128)(2,1)S(1)} %get-tuple-element.63), channel_id=1, source_target_pairs={{28,0},{24,4},{20,8},{16,12},{12,16},{8,20},{4,24},{0,28},{29,1},{... | collective-permute-start | bytes 196616 | tf_op jit(solution)/shard_map/ppermute | solution.py:34
  48.6 1.2 %collective-permute-start.24 = (bf16[2,128,128]{2,1,0:T(8,128)(2,1)S(1)}, bf16[2,128,128]{2,1,0:T(8,128)(2,1)S(1)}, u32[]{:S(2)}, u32[]{:S(2)}) collective-permute-start(bf16[2,128,128]{2,1,0:T(8,128)(2,1)S(1)} %get-tuple-element.64), channel_id=1, source_target_pairs={{8,0},{12,4},{0,8},{4,12},{24,16},{28,20},{16,24},{20,28},{9,1},{1... | collective-permute-start | bytes 196616 | tf_op jit(solution)/shard_map/ppermute | solution.py:34
  49.8 1.4 %collective-permute-done.20.rest_2_ = bf16[2,128,128]{2,1,0:T(8,128)(2,1)S(1)} collective-permute-done((bf16[2,128,128]{2,1,0:T(8,128)(2,1)S(1)}, bf16[2,128,128]{2,1,0:T(8,128)(2,1)S(1)}, u32[]{:S(2)}, u32[]{:S(2)}) %collective-permute-start.20) | collective-permute-done | bytes 65568 | tf_op jit(solution)/shard_map/ppermute | solution.py:34
  51.2 1.2 %collective-permute-start.25 = (bf16[2,128,128]{2,1,0:T(8,128)(2,1)S(1)}, bf16[2,128,128]{2,1,0:T(8,128)(2,1)S(1)}, u32[]{:S(2)}, u32[]{:S(2)}) collective-permute-start(bf16[2,128,128]{2,1,0:T(8,128)(2,1)S(1)} %get-tuple-element.65), channel_id=1, source_target_pairs={{12,0},{8,4},{4,8},{0,12},{28,16},{24,20},{20,24},{16,28},{13,1},{... | collective-permute-start | bytes 196616 | tf_op jit(solution)/shard_map/ppermute | solution.py:34
  52.5 1.6 %local_backward.1.local_ref = f32[17,128,128]{2,1,0:T(8,128)S(1)} custom-call(s32[962]{0:T(1024)S(1)} %get-tuple-element.38.plan_ref, bf16[128,128,128]{2,1,0:T(8,128)(2,1)S(1)} %get-tuple-element.40.weight_ref, bf16[9,128,128]{2,1,0:T(8,128)(2,1)S(1)} %get-tuple-element.57.rows_grad), custom_call_target="tpu_custom_call" | custom-call | flops 2147483648 | bytes 1024 | tf_op jit(solution)/shard_map/local_backward/pallas_call | solution.py:433
  54.1 0.7 %rows.1 = bf16[1024,128]{1,0:T(8,128)(2,1)} custom-call(bf16[256,128]{1,0:T(8,128)(2,1)S(1)} %get-tuple-element.52.rest_0_, bf16[256,128]{1,0:T(8,128)(2,1)S(1)} %collective-permute-done.13.rest_1_, bf16[256,128]{1,0:T(8,128)(2,1)S(1)} %collective-permute-done.14.rest_2_, bf16[256,128]{1,0:T(8,128)(2,1)S(1)} %collective-permute-done.15.rest_3_), custom_call_target="tpu_custom_call" | custom-call | tf_op jit(solution)/shard_map/rows/pallas_call | solution.py:443
  54.8 1.5 %collective-permute-done.22.rest_4_ = bf16[2,128,128]{2,1,0:T(8,128)(2,1)S(1)} collective-permute-done((bf16[2,128,128]{2,1,0:T(8,128)(2,1)S(1)}, bf16[2,128,128]{2,1,0:T(8,128)(2,1)S(1)}, u32[]{:S(2)}, u32[]{:S(2)}) %collective-permute-start.22) | collective-permute-done | bytes 65568 | tf_op jit(solution)/shard_map/ppermute | solution.py:34
  56.3 0.6 %collective-permute-done.25.rest_7_ = bf16[2,128,128]{2,1,0:T(8,128)(2,1)S(1)} collective-permute-done((bf16[2,128,128]{2,1,0:T(8,128)(2,1)S(1)}, bf16[2,128,128]{2,1,0:T(8,128)(2,1)S(1)}, u32[]{:S(2)}, u32[]{:S(2)}) %collective-permute-start.25) | collective-permute-done | bytes 65568 | tf_op jit(solution)/shard_map/ppermute | solution.py:34
  56.9 1.7 %final.1 = bf16[128,2048]{1,0:T(8,128)(2,1)} custom-call(s32[2,8]{1,0:T(2,128)S(1)} %bitcast.4, s32[8]{0:T(128)S(1)} %copy-done.5, f32[17,128,128]{2,1,0:T(8,128)S(1)} %local_backward.1.local_ref, bf16[2,128,128]{2,1,0:T(8,128)(2,1)S(1)} %get-tuple-element.58.rest_0_, bf16[2,128,128]{2,1,0:T(8,128)(2,1)S(1)} %collective-permute-done.19.rest_1_, ...), custom_call_target="tpu_custom_call" | custom-call | tf_op jit(solution)/shard_map/final/pallas_call | solution.py:453
  (40 shorter events, 3.5 us)
Async XLA Ops:
  0.6 21.2 %copy-start.1 = (bf16[128,2048]{1,0:T(8,128)(2,1)S(1)}, bf16[128,2048]{1,0:T(8,128)(2,1)}, u32[]{:S(2)}) copy-start(bf16[128,2048]{1,0:T(8,128)(2,1)} %rest_4_) | copy-start | bytes 1572868
  2.0 22.8 %collective-permute-start.11 = (bf16[128,2048]{1,0:T(8,128)(2,1)}, bf16[128,2048]{1,0:T(8,128)(2,1)S(1)}, u32[]{:S(2)}, u32[]{:S(2)}) collective-permute-start(bf16[128,2048]{1,0:T(8,128)(2,1)} %rest_4_), channel_id=1, source_target_pairs={{0,2},{1,3},{2,0},{3,1},{4,6},{5,7},{6,4},{7,5},{8,10},{9,11},{10,... | collective-permute-start | bytes 1572872 | tf_op jit(solution)/shard_map/ppermute | solution.py:30
  5.0 6.1 %collective-permute-start = (bf16[2,128,128]{2,1,0:T(8,128)(2,1)S(1)}, bf16[2,128,128]{2,1,0:T(8,128)(2,1)S(1)}, u32[]{:S(2)}, u32[]{:S(2)}) collective-permute-start(bf16[2,128,128]{2,1,0:T(8,128)(2,1)S(1)} %get-tuple-element.35), channel_id=1, source_target_pairs={{0,4},{4,0},{8,12},{12,8},{16,20},{20,16},{24,28},{28,24},{1,5},{5... | collective-permute-start | bytes 196616 | tf_op jit(solution)/shard_map/ppermute | solution.py:30
  6.5 6.3 %collective-permute-start.1 = (bf16[2,128,128]{2,1,0:T(8,128)(2,1)S(1)}, bf16[2,128,128]{2,1,0:T(8,128)(2,1)S(1)}, u32[]{:S(2)}, u32[]{:S(2)}) collective-permute-start(bf16[2,128,128]{2,1,0:T(8,128)(2,1)S(1)} %get-tuple-element.36), channel_id=1, source_target_pairs={{0,8},{4,12},{8,0},{12,4},{16,24},{20,28},{24,16},{28,20},{1,9},{5... | collective-permute-start | bytes 196616 | tf_op jit(solution)/shard_map/ppermute | solution.py:30
  8.1 7.9 %collective-permute-start.2 = (bf16[2,128,128]{2,1,0:T(8,128)(2,1)S(1)}, bf16[2,128,128]{2,1,0:T(8,128)(2,1)S(1)}, u32[]{:S(2)}, u32[]{:S(2)}) collective-permute-start(bf16[2,128,128]{2,1,0:T(8,128)(2,1)S(1)} %get-tuple-element.37), channel_id=1, source_target_pairs={{0,12},{4,8},{8,4},{12,0},{16,28},{20,24},{24,20},{28,16},{1,13},{... | collective-permute-start | bytes 196616 | tf_op jit(solution)/shard_map/ppermute | solution.py:30
  8.5 13.4 %collective-permute-start.3 = (bf16[2,128,128]{2,1,0:T(8,128)(2,1)S(1)}, bf16[2,128,128]{2,1,0:T(8,128)(2,1)S(1)}, u32[]{:S(2)}, u32[]{:S(2)}) collective-permute-start(bf16[2,128,128]{2,1,0:T(8,128)(2,1)S(1)} %get-tuple-element.41), channel_id=1, source_target_pairs={{0,16},{4,20},{8,24},{12,28},{16,0},{20,4},{24,8},{28,12},{1,17},{... | collective-permute-start | bytes 196616 | tf_op jit(solution)/shard_map/ppermute | solution.py:30
  11.1 10.9 %collective-permute-start.4 = (bf16[2,128,128]{2,1,0:T(8,128)(2,1)S(1)}, bf16[2,128,128]{2,1,0:T(8,128)(2,1)S(1)}, u32[]{:S(2)}, u32[]{:S(2)}) collective-permute-start(bf16[2,128,128]{2,1,0:T(8,128)(2,1)S(1)} %get-tuple-element.42), channel_id=1, source_target_pairs={{0,20},{4,16},{8,28},{12,24},{16,4},{20,0},{24,12},{28,8},{1,21},{... | collective-permute-start | bytes 196616 | tf_op jit(solution)/shard_map/ppermute | solution.py:30
  12.8 9.2 %collective-permute-start.5 = (bf16[2,128,128]{2,1,0:T(8,128)(2,1)S(1)}, bf16[2,128,128]{2,1,0:T(8,128)(2,1)S(1)}, u32[]{:S(2)}, u32[]{:S(2)}) collective-permute-start(bf16[2,128,128]{2,1,0:T(8,128)(2,1)S(1)} %get-tuple-element.43), channel_id=1, source_target_pairs={{0,24},{4,28},{8,16},{12,20},{16,8},{20,12},{24,0},{28,4},{1,25},{... | collective-permute-start | bytes 196616 | tf_op jit(solution)/shard_map/ppermute | solution.py:30
  15.9 7.1 %collective-permute-start.6 = (bf16[2,128,128]{2,1,0:T(8,128)(2,1)S(1)}, bf16[2,128,128]{2,1,0:T(8,128)(2,1)S(1)}, u32[]{:S(2)}, u32[]{:S(2)}) collective-permute-start(bf16[2,128,128]{2,1,0:T(8,128)(2,1)S(1)} %get-tuple-element.44), channel_id=1, source_target_pairs={{0,28},{4,24},{8,20},{12,16},{16,12},{20,8},{24,4},{28,0},{1,29},{... | collective-permute-start | bytes 196616 | tf_op jit(solution)/shard_map/ppermute | solution.py:30
  21.8 8.5 %copy-start = (bf16[2048,128]{1,0:T(8,128)(2,1)S(1)}, bf16[2048,128]{1,0:T(8,128)(2,1)}, u32[]{:S(2)}) copy-start(bf16[2048,128]{1,0:T(8,128)(2,1)} %w_out_ref.1) | copy-start | bytes 1572868
  21.8 8.5 %copy-start.2 = (bf16[1024,128]{1,0:T(8,128)(2,1)S(1)}, bf16[1024,128]{1,0:T(8,128)(2,1)}, u32[]{:S(2)}) copy-start(bf16[1024,128]{1,0:T(8,128)(2,1)} %g_ref.1) | copy-start | bytes 786436
  21.8 8.5 %copy-start.3 = (f32[2048]{0:T(1024)S(1)}, f32[2048]{0:T(1024)}, u32[]{:S(2)}) copy-start(f32[2048]{0:T(1024)} %param.17) | copy-start | bytes 24580
  21.9 8.4 %collective-permute-start.10 = (bf16[128,2048]{1,0:T(8,128)(2,1)S(1)}, bf16[128,2048]{1,0:T(8,128)(2,1)S(1)}, u32[]{:S(2)}, u32[]{:S(2)}) collective-permute-start(bf16[128,2048]{1,0:T(8,128)(2,1)S(1)} %copy-done.1), channel_id=1, source_target_pairs={{0,1},{1,0},{2,3},{3,2},{4,5},{5,4},{6,7},{7,6},{8,9},{9,8},{10,11... | collective-permute-start | bytes 1572872 | tf_op jit(solution)/shard_map/ppermute | solution.py:30
  24.8 5.5 %collective-permute-start.12 = (bf16[128,2048]{1,0:T(8,128)(2,1)S(1)}, bf16[128,2048]{1,0:T(8,128)(2,1)S(1)}, u32[]{:S(2)}, u32[]{:S(2)}) collective-permute-start(bf16[128,2048]{1,0:T(8,128)(2,1)S(1)} %collective-permute-done.11.rest_6_), channel_id=1, source_target_pairs={{0,1},{1,0},{2,3},{3,2},{4,5},{5,4},{6,7},{7,6},{8,9},{9,8},{10,11... | collective-permute-start | bytes 1572872 | tf_op jit(solution)/shard_map/ppermute | solution.py:30
  24.9 2.0 %collective-permute-start.7 = (bf16[256,128]{1,0:T(8,128)(2,1)S(1)}, bf16[256,128]{1,0:T(8,128)(2,1)S(1)}, u32[]{:S(2)}, u32[]{:S(2)}) collective-permute-start(bf16[256,128]{1,0:T(8,128)(2,1)S(1)} %get-tuple-element.46), channel_id=1, source_target_pairs={{0,1},{1,0},{2,3},{3,2},{4,5},{5,4},{6,7},{7,6},{8,9},{9,8},{10,11... | collective-permute-start | bytes 196616 | tf_op jit(solution)/shard_map/ppermute | solution.py:30
  25.4 4.9 %collective-permute-start.8 = (bf16[256,128]{1,0:T(8,128)(2,1)S(1)}, bf16[256,128]{1,0:T(8,128)(2,1)S(1)}, u32[]{:S(2)}, u32[]{:S(2)}) collective-permute-start(bf16[256,128]{1,0:T(8,128)(2,1)S(1)} %get-tuple-element.47), channel_id=1, source_target_pairs={{0,2},{1,3},{2,0},{3,1},{4,6},{5,7},{6,4},{7,5},{8,10},{9,11},{10,... | collective-permute-start | bytes 196616 | tf_op jit(solution)/shard_map/ppermute | solution.py:30
  25.9 4.4 %collective-permute-start.9 = (bf16[256,128]{1,0:T(8,128)(2,1)S(1)}, bf16[256,128]{1,0:T(8,128)(2,1)S(1)}, u32[]{:S(2)}, u32[]{:S(2)}) collective-permute-start(bf16[256,128]{1,0:T(8,128)(2,1)S(1)} %get-tuple-element.48), channel_id=1, source_target_pairs={{0,3},{1,2},{2,1},{3,0},{4,7},{5,6},{6,5},{7,4},{8,11},{9,10},{10,... | collective-permute-start | bytes 196616 | tf_op jit(solution)/shard_map/ppermute | solution.py:30
  32.5 3.8 %collective-permute-start.16 = (bf16[128,256]{1,0:T(8,128)(2,1)S(1)}, bf16[128,256]{1,0:T(8,128)(2,1)S(1)}, u32[]{:S(2)}, u32[]{:S(2)}) collective-permute-start(bf16[128,256]{1,0:T(8,128)(2,1)S(1)} %get-tuple-element.54), channel_id=1, source_target_pairs={{1,0},{0,1},{3,2},{2,3},{5,4},{4,5},{7,6},{6,7},{9,8},{8,9},{11,10... | collective-permute-start | bytes 196616 | tf_op jit(solution)/shard_map/ppermute | solution.py:34
  33.1 4.5 %collective-permute-start.17 = (bf16[128,256]{1,0:T(8,128)(2,1)S(1)}, bf16[128,256]{1,0:T(8,128)(2,1)S(1)}, u32[]{:S(2)}, u32[]{:S(2)}) collective-permute-start(bf16[128,256]{1,0:T(8,128)(2,1)S(1)} %get-tuple-element.55), channel_id=1, source_target_pairs={{2,0},{3,1},{0,2},{1,3},{6,4},{7,5},{4,6},{5,7},{10,8},{11,9},{8,1... | collective-permute-start | bytes 196616 | tf_op jit(solution)/shard_map/ppermute | solution.py:34
  34.1 4.3 %collective-permute-start.18 = (bf16[128,256]{1,0:T(8,128)(2,1)S(1)}, bf16[128,256]{1,0:T(8,128)(2,1)S(1)}, u32[]{:S(2)}, u32[]{:S(2)}) collective-permute-start(bf16[128,256]{1,0:T(8,128)(2,1)S(1)} %get-tuple-element.56), channel_id=1, source_target_pairs={{3,0},{2,1},{1,2},{0,3},{7,4},{6,5},{5,6},{4,7},{11,8},{10,9},{9,1... | collective-permute-start | bytes 196616 | tf_op jit(solution)/shard_map/ppermute | solution.py:34
  34.5 9.0 %collective-permute-start.13 = (bf16[256,128]{1,0:T(8,128)(2,1)S(1)}, bf16[256,128]{1,0:T(8,128)(2,1)S(1)}, u32[]{:S(2)}, u32[]{:S(2)}) collective-permute-start(bf16[256,128]{1,0:T(8,128)(2,1)S(1)} %get-tuple-element.52.rest_0_), channel_id=1, source_target_pairs={{0,1},{1,0},{2,3},{3,2},{4,5},{5,4},{6,7},{7,6},{8,9},{9,8},{10,11... | collective-permute-start | bytes 196616 | tf_op jit(solution)/shard_map/ppermute | solution.py:30
  35.2 10.2 %collective-permute-start.14 = (bf16[256,128]{1,0:T(8,128)(2,1)S(1)}, bf16[256,128]{1,0:T(8,128)(2,1)S(1)}, u32[]{:S(2)}, u32[]{:S(2)}) collective-permute-start(bf16[256,128]{1,0:T(8,128)(2,1)S(1)} %get-tuple-element.52.rest_0_), channel_id=1, source_target_pairs={{0,2},{1,3},{2,0},{3,1},{4,6},{5,7},{6,4},{7,5},{8,10},{9,11},{10,... | collective-permute-start | bytes 196616 | tf_op jit(solution)/shard_map/ppermute | solution.py:30
  36.3 9.9 %collective-permute-start.15 = (bf16[256,128]{1,0:T(8,128)(2,1)S(1)}, bf16[256,128]{1,0:T(8,128)(2,1)S(1)}, u32[]{:S(2)}, u32[]{:S(2)}) collective-permute-start(bf16[256,128]{1,0:T(8,128)(2,1)S(1)} %get-tuple-element.52.rest_0_), channel_id=1, source_target_pairs={{0,3},{1,2},{2,1},{3,0},{4,7},{5,6},{6,5},{7,4},{8,11},{9,10},{10,... | collective-permute-start | bytes 196616 | tf_op jit(solution)/shard_map/ppermute | solution.py:30
  40.7 7.9 %collective-permute-start.19 = (bf16[2,128,128]{2,1,0:T(8,128)(2,1)S(1)}, bf16[2,128,128]{2,1,0:T(8,128)(2,1)S(1)}, u32[]{:S(2)}, u32[]{:S(2)}) collective-permute-start(bf16[2,128,128]{2,1,0:T(8,128)(2,1)S(1)} %get-tuple-element.59), channel_id=1, source_target_pairs={{4,0},{0,4},{12,8},{8,12},{20,16},{16,20},{28,24},{24,28},{5,1},{1... | collective-permute-start | bytes 196616 | tf_op jit(solution)/shard_map/ppermute | solution.py:34
  41.3 10.0 %collective-permute-start.20 = (bf16[2,128,128]{2,1,0:T(8,128)(2,1)S(1)}, bf16[2,128,128]{2,1,0:T(8,128)(2,1)S(1)}, u32[]{:S(2)}, u32[]{:S(2)}) collective-permute-start(bf16[2,128,128]{2,1,0:T(8,128)(2,1)S(1)} %get-tuple-element.60), channel_id=1, source_target_pairs={{16,0},{20,4},{24,8},{28,12},{0,16},{4,20},{8,24},{12,28},{17,1},{... | collective-permute-start | bytes 196616 | tf_op jit(solution)/shard_map/ppermute | solution.py:34
  43.5 11.4 %collective-permute-start.21 = (bf16[2,128,128]{2,1,0:T(8,128)(2,1)S(1)}, bf16[2,128,128]{2,1,0:T(8,128)(2,1)S(1)}, u32[]{:S(2)}, u32[]{:S(2)}) collective-permute-start(bf16[2,128,128]{2,1,0:T(8,128)(2,1)S(1)} %get-tuple-element.61), channel_id=1, source_target_pairs={{24,0},{28,4},{16,8},{20,12},{8,16},{12,20},{0,24},{4,28},{25,1},{... | collective-permute-start | bytes 196616 | tf_op jit(solution)/shard_map/ppermute | solution.py:34
  45.5 10.9 %collective-permute-start.22 = (bf16[2,128,128]{2,1,0:T(8,128)(2,1)S(1)}, bf16[2,128,128]{2,1,0:T(8,128)(2,1)S(1)}, u32[]{:S(2)}, u32[]{:S(2)}) collective-permute-start(bf16[2,128,128]{2,1,0:T(8,128)(2,1)S(1)} %get-tuple-element.62), channel_id=1, source_target_pairs={{20,0},{16,4},{28,8},{24,12},{4,16},{0,20},{12,24},{8,28},{21,1},{... | collective-permute-start | bytes 196616 | tf_op jit(solution)/shard_map/ppermute | solution.py:34
  46.2 10.1 %collective-permute-start.23 = (bf16[2,128,128]{2,1,0:T(8,128)(2,1)S(1)}, bf16[2,128,128]{2,1,0:T(8,128)(2,1)S(1)}, u32[]{:S(2)}, u32[]{:S(2)}) collective-permute-start(bf16[2,128,128]{2,1,0:T(8,128)(2,1)S(1)} %get-tuple-element.63), channel_id=1, source_target_pairs={{28,0},{24,4},{20,8},{16,12},{12,16},{8,20},{4,24},{0,28},{29,1},{... | collective-permute-start | bytes 196616 | tf_op jit(solution)/shard_map/ppermute | solution.py:34
  48.6 7.7 %collective-permute-start.24 = (bf16[2,128,128]{2,1,0:T(8,128)(2,1)S(1)}, bf16[2,128,128]{2,1,0:T(8,128)(2,1)S(1)}, u32[]{:S(2)}, u32[]{:S(2)}) collective-permute-start(bf16[2,128,128]{2,1,0:T(8,128)(2,1)S(1)} %get-tuple-element.64), channel_id=1, source_target_pairs={{8,0},{12,4},{0,8},{4,12},{24,16},{28,20},{16,24},{20,28},{9,1},{1... | collective-permute-start | bytes 196616 | tf_op jit(solution)/shard_map/ppermute | solution.py:34
  51.2 5.7 %collective-permute-start.25 = (bf16[2,128,128]{2,1,0:T(8,128)(2,1)S(1)}, bf16[2,128,128]{2,1,0:T(8,128)(2,1)S(1)}, u32[]{:S(2)}, u32[]{:S(2)}) collective-permute-start(bf16[2,128,128]{2,1,0:T(8,128)(2,1)S(1)} %get-tuple-element.65), channel_id=1, source_target_pairs={{12,0},{8,4},{4,8},{0,12},{28,16},{24,20},{20,24},{16,28},{13,1},{... | collective-permute-start | bytes 196616 | tf_op jit(solution)/shard_map/ppermute | solution.py:34
  52.5 4.5 %copy-start.4 = (s32[8,2]{0,1:T(2,128)S(1)}, s32[8,2]{0,1:T(2,128)}, u32[]{:S(2)}) copy-start(s32[8,2]{0,1:T(2,128)} %param.12) | copy-start | bytes 196
  52.5 4.5 %copy-start.5 = (s32[8]{0:T(128)S(1)}, s32[8]{0:T(128)}, u32[]{:S(2)}) copy-start(s32[8]{0:T(128)} %counts_ref.1) | copy-start | bytes 100

commit v6 on v5

--- a/solution.py
+++ b/solution.py
@@ -9,7 +9,8 @@
 
 F32 = jnp.float32
 BF16 = jnp.bfloat16
-UNROLL = 32
+UNROLL = 48
+TAIL = 16
 NT = (((1,), (1,)), ((), ()))
 NN = (((1,), (0,)), ((), ()))
 
@@ -149,13 +150,17 @@
                 return base + jnp.where(i < n_near, i, i + n_local)
             return i
 
-        def step(t, carry):
-            for u in range(UNROLL):
-                at = place(t * UNROLL + u)
+        def step(start, width, t, carry):
+            for u in range(width):
+                at = place(start + t * width + u)
                 body(ref[at], ref[at + length], ref[at + 2 * length])
             return carry
 
-        lax.fori_loop(0, (count + UNROLL - 1) // UNROLL, step, 0)
+        full = lax.div(count + UNROLL - 1 - TAIL, UNROLL)
+        done = full * UNROLL
+        left = jnp.maximum(count - done, 0)
+        lax.fori_loop(0, full, functools.partial(step, 0, UNROLL), 0)
+        lax.fori_loop(0, lax.div(left + TAIL - 1, TAIL), functools.partial(step, done, TAIL), 0)
 
 
 def first_forward_kernel(

time: 58.8 us -> 58.2 us (0.990)
  Pallas kernels: 16.7 us -> 15.4 us
  starting transfers between devices: 31.1 us -> 32.1 us
    ppermute x10, starting transfers between devices: 12.3 us -> 13.3 us  [send_back(): lax.ppermute(value, axis, [(target(i, shift, count), i) for i in range(co...]
    ppermute x10, waiting for transfers between devices: 5.36 us -> 4.61 us  [send_back(): lax.ppermute(value, axis, [(target(i, shift, count), i) for i in range(co...]
  transfers between devices with their start and end apart: 26 -> 26, of which waited for: 8 -> 7; matrix products, arithmetic and copies ran while one was open for 0% -> 0% of each run, Pallas kernels for 20% -> 18%
where the time goes in v6:
time: 58.2 us; the launch traced here: 58.1 us
  starting transfers between devices  32.1 us (55%)
  Pallas kernels  15.4 us (26%)
  waiting for transfers between devices  9.74 us (17%)
  between operations  0.81 us (1%)
    ppermute x16, starting transfers between devices, send(): lax.ppermute(value, axis, [(i, target(i, shift, count)) for i in range(co...  18.8 us
    ppermute x10, starting transfers between devices, send_back(): lax.ppermute(value, axis, [(target(i, shift, count), i) for i in range(co...  13.3 us
    ppermute x16, waiting for transfers between devices, send(): lax.ppermute(value, axis, [(i, target(i, shift, count)) for i in range(co...  5.13 us
    ppermute x10, waiting for transfers between devices, send_back(): lax.ppermute(value, axis, [(target(i, shift, count), i) for i in range(co...  4.61 us
    pallas_call x1, Pallas kernels, on_device(): pl.pallas_call(functools.partial(first_forward_kernel, plan, near, dom, c...  4.57 us
    pallas_call x1, Pallas kernels, on_device(): pl.pallas_call(functools.partial(mlp_kernel, chan, min(1024, hidden_width...  2.17 us
    pallas_call x1, Pallas kernels, on_device(): pl.pallas_call(functools.partial(slot_backward_kernel, plan, dom, cap, ch...  2.16 us
    pallas_call x1, Pallas kernels, on_device(): pl.pallas_call(functools.partial(final_kernel, back_order, dom, cap, blk,...  1.67 us
  transfers between devices with their start and end apart: 26, of which 7 were waited for; matrix products, arithmetic and copies ran while one was open for 0% of the time, Pallas kernels for 18%

profile of v6, /device:TPU:0, one launch (start us, length us, event | category | flops | bytes accessed | tf_op | source)
XLA Modules:
  0.0 58.1 jit_solution(9710616373690294966)
XLA Ops:
  0.6 1.3 %pack.1 = (bf16[2,128,128]{2,1,0:T(8,128)(2,1)S(1)}, bf16[2,128,128]{2,1,0:T(8,128)(2,1)S(1)}, bf16[2,128,128]{2,1,0:T(8,128)(2,1)S(1)}, bf16[2,128,128]{2,1,0:T...) custom-call(s32[2,8]{1,0:T(2,128)} %bitcast.3, ...), custom_call_target="tpu_custom_call" | custom-call | tf_op jit(solution)/shard_map/pack/pallas_call | solution.py:343
  2.0 3.0 %collective-permute-start.11 = (bf16[128,2048]{1,0:T(8,128)(2,1)}, bf16[128,2048]{1,0:T(8,128)(2,1)S(1)}, u32[]{:S(2)}, u32[]{:S(2)}) collective-permute-start(bf16[128,2048]{1,0:T(8,128)(2,1)} %rest_4_), channel_id=1, source_target_pairs={{0,2},{1,3},{2,0},{3,1},{4,6},{5,7},{6,4},{7,5},{8,10},{9,11},{10,... | collective-permute-start | bytes 1572872 | tf_op jit(solution)/shard_map/ppermute | solution.py:31
  5.0 1.5 %collective-permute-start = (bf16[2,128,128]{2,1,0:T(8,128)(2,1)S(1)}, bf16[2,128,128]{2,1,0:T(8,128)(2,1)S(1)}, u32[]{:S(2)}, u32[]{:S(2)}) collective-permute-start(bf16[2,128,128]{2,1,0:T(8,128)(2,1)S(1)} %get-tuple-element.35), channel_id=1, source_target_pairs={{0,4},{4,0},{8,12},{12,8},{16,20},{20,16},{24,28},{28,24},{1,5},{5... | collective-permute-start | bytes 196616 | tf_op jit(solution)/shard_map/ppermute | solution.py:31
  6.5 1.6 %collective-permute-start.1 = (bf16[2,128,128]{2,1,0:T(8,128)(2,1)S(1)}, bf16[2,128,128]{2,1,0:T(8,128)(2,1)S(1)}, u32[]{:S(2)}, u32[]{:S(2)}) collective-permute-start(bf16[2,128,128]{2,1,0:T(8,128)(2,1)S(1)} %get-tuple-element.36), channel_id=1, source_target_pairs={{0,8},{4,12},{8,0},{12,4},{16,24},{20,28},{24,16},{28,20},{1,9},{5... | collective-permute-start | bytes 196616 | tf_op jit(solution)/shard_map/ppermute | solution.py:31
  8.5 2.6 %collective-permute-start.3 = (bf16[2,128,128]{2,1,0:T(8,128)(2,1)S(1)}, bf16[2,128,128]{2,1,0:T(8,128)(2,1)S(1)}, u32[]{:S(2)}, u32[]{:S(2)}) collective-permute-start(bf16[2,128,128]{2,1,0:T(8,128)(2,1)S(1)} %get-tuple-element.41), channel_id=1, source_target_pairs={{0,16},{4,20},{8,24},{12,28},{16,0},{20,4},{24,8},{28,12},{1,17},{... | collective-permute-start | bytes 196616 | tf_op jit(solution)/shard_map/ppermute | solution.py:31
  11.1 1.7 %collective-permute-start.4 = (bf16[2,128,128]{2,1,0:T(8,128)(2,1)S(1)}, bf16[2,128,128]{2,1,0:T(8,128)(2,1)S(1)}, u32[]{:S(2)}, u32[]{:S(2)}) collective-permute-start(bf16[2,128,128]{2,1,0:T(8,128)(2,1)S(1)} %get-tuple-element.42), channel_id=1, source_target_pairs={{0,20},{4,16},{8,28},{12,24},{16,4},{20,0},{24,12},{28,8},{1,21},{... | collective-permute-start | bytes 196616 | tf_op jit(solution)/shard_map/ppermute | solution.py:31
  12.8 3.2 %collective-permute-start.5 = (bf16[2,128,128]{2,1,0:T(8,128)(2,1)S(1)}, bf16[2,128,128]{2,1,0:T(8,128)(2,1)S(1)}, u32[]{:S(2)}, u32[]{:S(2)}) collective-permute-start(bf16[2,128,128]{2,1,0:T(8,128)(2,1)S(1)} %get-tuple-element.43), channel_id=1, source_target_pairs={{0,24},{4,28},{8,16},{12,20},{16,8},{20,12},{24,0},{28,4},{1,25},{... | collective-permute-start | bytes 196616 | tf_op jit(solution)/shard_map/ppermute | solution.py:31
  15.9 0.7 %collective-permute-start.6 = (bf16[2,128,128]{2,1,0:T(8,128)(2,1)S(1)}, bf16[2,128,128]{2,1,0:T(8,128)(2,1)S(1)}, u32[]{:S(2)}, u32[]{:S(2)}) collective-permute-start(bf16[2,128,128]{2,1,0:T(8,128)(2,1)S(1)} %get-tuple-element.44), channel_id=1, source_target_pairs={{0,28},{4,24},{8,20},{12,16},{16,12},{20,8},{24,4},{28,0},{1,29},{... | collective-permute-start | bytes 196616 | tf_op jit(solution)/shard_map/ppermute | solution.py:31
  16.7 4.6 %first_forward.1 = (f32[9,128,128]{2,1,0:T(8,128)S(1)}, s32[1058]{0:T(1024)S(1)}, bf16[128,128,128]{2,1,0:T(8,128)(2,1)S(1)}) custom-call(s32[128]{0:T(128)} %src_hbm.1, s32[128]{0:T(128)} %obs_hbm.1, bf16[128,2048]{1,0:T(8,128)(2,1)} %latent_hbm.3, bf16[128,128,128]{2,1,0:T(8,128)(2,1)} %weight_hbm.1, bf16[2,128,128]{2,1,0:T(8,128)(2,1)S(1)} %get-tuple-element.34.rest_0_, ...), custom_call_target="tpu_custom_call" | custom-call | flops 2147483648 | bytes 1024 | tf_op jit(solution)/shard_map/first_forward/pallas_call | solution.py:369
  21.4 1.6 %collective-permute-done.6.rest_3_ = bf16[2,128,128]{2,1,0:T(8,128)(2,1)S(1)} collective-permute-done((bf16[2,128,128]{2,1,0:T(8,128)(2,1)S(1)}, bf16[2,128,128]{2,1,0:T(8,128)(2,1)S(1)}, u32[]{:S(2)}, u32[]{:S(2)}) %collective-permute-start.6) | collective-permute-done | bytes 65568 | tf_op jit(solution)/shard_map/ppermute | solution.py:31
  23.0 1.4 %far_forward.1 = (bf16[256,128]{1,0:T(8,128)(2,1)S(1)}, bf16[256,128]{1,0:T(8,128)(2,1)S(1)}, bf16[256,128]{1,0:T(8,128)(2,1)S(1)}, bf16[256,128]{1,0:T(8,128)(2,1)S(1)}) custom-call(s32[1058]{0:T(1024)S(1)} %get-tuple-element.38.plan_ref, f32[9,128,128]{2,1,0:T(8,128)S(1)} %get-tuple-element.39.sum_ref, ...), custom_call_target="tpu_custom_call" | custom-call | tf_op jit(solution)/shard_map/far_forward/pallas_call | solution.py:391
  25.6 0.9 %collective-permute-start.9 = (bf16[256,128]{1,0:T(8,128)(2,1)S(1)}, bf16[256,128]{1,0:T(8,128)(2,1)S(1)}, u32[]{:S(2)}, u32[]{:S(2)}) collective-permute-start(bf16[256,128]{1,0:T(8,128)(2,1)S(1)} %get-tuple-element.48), channel_id=1, source_target_pairs={{0,3},{1,2},{2,1},{3,0},{4,7},{5,6},{6,5},{7,4},{8,11},{9,10},{10,... | collective-permute-start | bytes 196616 | tf_op jit(solution)/shard_map/ppermute | solution.py:31
  26.5 3.4 %collective-permute-done.8.rest_2_ = bf16[256,128]{1,0:T(8,128)(2,1)S(1)} collective-permute-done((bf16[256,128]{1,0:T(8,128)(2,1)S(1)}, bf16[256,128]{1,0:T(8,128)(2,1)S(1)}, u32[]{:S(2)}, u32[]{:S(2)}) %collective-permute-start.8) | collective-permute-done | bytes 65568 | tf_op jit(solution)/shard_map/ppermute | solution.py:31
  30.0 2.2 %mlp.1 = (bf16[256,128]{1,0:T(8,128)(2,1)S(1)}, bf16[128,256]{1,0:T(8,128)(2,1)S(1)}, bf16[128,256]{1,0:T(8,128)(2,1)S(1)}, bf16[128,256]{1,0:T(8,128)(2,1)S(1)}, bf16[128,256]{1,0:T(8,128)(2,1)S(1)}) custom-call(f32[1,2048]{1,0:T(1,128)S(1)} %bitcast.2, bf16[2048,128]{1,0:T(8,128)(2,1)S(1)} %copy-done, bf16[1024,128]{1,0:T(8,128)(2,1)S(1)} %copy-done.2, ...), custom_call_target="tpu_custom_call" | custom-call | tf_op jit(solution)/shard_map/mlp/pallas_call | solution.py:410
  32.2 0.6 collective-permute-start.16
  32.7 1.1 %collective-permute-start.17 = (bf16[128,256]{1,0:T(8,128)(2,1)S(1)}, bf16[128,256]{1,0:T(8,128)(2,1)S(1)}, u32[]{:S(2)}, u32[]{:S(2)}) collective-permute-start(bf16[128,256]{1,0:T(8,128)(2,1)S(1)} %get-tuple-element.55), channel_id=1, source_target_pairs={{2,0},{3,1},{0,2},{1,3},{6,4},{7,5},{4,6},{5,7},{10,8},{11,9},{8,1... | collective-permute-start | bytes 196616 | tf_op jit(solution)/shard_map/ppermute | solution.py:35
  34.2 0.7 %collective-permute-start.13 = (bf16[256,128]{1,0:T(8,128)(2,1)S(1)}, bf16[256,128]{1,0:T(8,128)(2,1)S(1)}, u32[]{:S(2)}, u32[]{:S(2)}) collective-permute-start(bf16[256,128]{1,0:T(8,128)(2,1)S(1)} %get-tuple-element.52.rest_0_), channel_id=1, source_target_pairs={{0,1},{1,0},{2,3},{3,2},{4,5},{5,4},{6,7},{7,6},{8,9},{9,8},{10,11... | collective-permute-start | bytes 196616 | tf_op jit(solution)/shard_map/ppermute | solution.py:31
  34.9 1.1 %collective-permute-start.14 = (bf16[256,128]{1,0:T(8,128)(2,1)S(1)}, bf16[256,128]{1,0:T(8,128)(2,1)S(1)}, u32[]{:S(2)}, u32[]{:S(2)}) collective-permute-start(bf16[256,128]{1,0:T(8,128)(2,1)S(1)} %get-tuple-element.52.rest_0_), channel_id=1, source_target_pairs={{0,2},{1,3},{2,0},{3,1},{4,6},{5,7},{6,4},{7,5},{8,10},{9,11},{10,... | collective-permute-start | bytes 196616 | tf_op jit(solution)/shard_map/ppermute | solution.py:31
  36.2 1.0 %collective-permute-done.17.rest_2_ = bf16[128,256]{1,0:T(8,128)(2,1)S(1)} collective-permute-done((bf16[128,256]{1,0:T(8,128)(2,1)S(1)}, bf16[128,256]{1,0:T(8,128)(2,1)S(1)}, u32[]{:S(2)}, u32[]{:S(2)}) %collective-permute-start.17) | collective-permute-done | bytes 65568 | tf_op jit(solution)/shard_map/ppermute | solution.py:35
  37.3 0.8 %collective-permute-done.18.rest_3_ = bf16[128,256]{1,0:T(8,128)(2,1)S(1)} collective-permute-done((bf16[128,256]{1,0:T(8,128)(2,1)S(1)}, bf16[128,256]{1,0:T(8,128)(2,1)S(1)}, u32[]{:S(2)}, u32[]{:S(2)}) %collective-permute-start.18) | collective-permute-done | bytes 65568 | tf_op jit(solution)/shard_map/ppermute | solution.py:35
  38.1 2.2 %slot_backward.1 = (bf16[9,128,128]{2,1,0:T(8,128)(2,1)S(1)}, bf16[2,128,128]{2,1,0:T(8,128)(2,1)S(1)}, bf16[2,128,128]{2,1,0:T(8,128)(2,1)S(1)}, bf16[2,128,128...) custom-call(s32[1058]{0:T(1024)S(1)} %get-tuple-element.38.plan_ref,, ...), custom_call_target="tpu_custom_call" | custom-call | tf_op jit(solution)/shard_map/slot_backward/pallas_call | solution.py:427
  40.3 0.6 %collective-permute-start.19 = (bf16[2,128,128]{2,1,0:T(8,128)(2,1)S(1)}, bf16[2,128,128]{2,1,0:T(8,128)(2,1)S(1)}, u32[]{:S(2)}, u32[]{:S(2)}) collective-permute-start(bf16[2,128,128]{2,1,0:T(8,128)(2,1)S(1)} %get-tuple-element.59), channel_id=1, source_target_pairs={{4,0},{0,4},{12,8},{8,12},{20,16},{16,20},{28,24},{24,28},{5,1},{1... | collective-permute-start | bytes 196616 | tf_op jit(solution)/shard_map/ppermute | solution.py:35
  40.9 2.6 %collective-permute-start.20 = (bf16[2,128,128]{2,1,0:T(8,128)(2,1)S(1)}, bf16[2,128,128]{2,1,0:T(8,128)(2,1)S(1)}, u32[]{:S(2)}, u32[]{:S(2)}) collective-permute-start(bf16[2,128,128]{2,1,0:T(8,128)(2,1)S(1)} %get-tuple-element.60), channel_id=1, source_target_pairs={{16,0},{20,4},{24,8},{28,12},{0,16},{4,20},{8,24},{12,28},{17,1},{... | collective-permute-start | bytes 196616 | tf_op jit(solution)/shard_map/ppermute | solution.py:35
  43.5 1.8 %collective-permute-start.21 = (bf16[2,128,128]{2,1,0:T(8,128)(2,1)S(1)}, bf16[2,128,128]{2,1,0:T(8,128)(2,1)S(1)}, u32[]{:S(2)}, u32[]{:S(2)}) collective-permute-start(bf16[2,128,128]{2,1,0:T(8,128)(2,1)S(1)} %get-tuple-element.61), channel_id=1, source_target_pairs={{24,0},{28,4},{16,8},{20,12},{8,16},{12,20},{0,24},{4,28},{25,1},{... | collective-permute-start | bytes 196616 | tf_op jit(solution)/shard_map/ppermute | solution.py:35
  45.6 2.7 %collective-permute-start.23 = (bf16[2,128,128]{2,1,0:T(8,128)(2,1)S(1)}, bf16[2,128,128]{2,1,0:T(8,128)(2,1)S(1)}, u32[]{:S(2)}, u32[]{:S(2)}) collective-permute-start(bf16[2,128,128]{2,1,0:T(8,128)(2,1)S(1)} %get-tuple-element.63), channel_id=1, source_target_pairs={{28,0},{24,4},{20,8},{16,12},{12,16},{8,20},{4,24},{0,28},{29,1},{... | collective-permute-start | bytes 196616 | tf_op jit(solution)/shard_map/ppermute | solution.py:35
  48.2 1.5 %collective-permute-start.24 = (bf16[2,128,128]{2,1,0:T(8,128)(2,1)S(1)}, bf16[2,128,128]{2,1,0:T(8,128)(2,1)S(1)}, u32[]{:S(2)}, u32[]{:S(2)}) collective-permute-start(bf16[2,128,128]{2,1,0:T(8,128)(2,1)S(1)} %get-tuple-element.64), channel_id=1, source_target_pairs={{8,0},{12,4},{0,8},{4,12},{24,16},{28,20},{16,24},{20,28},{9,1},{1... | collective-permute-start | bytes 196616 | tf_op jit(solution)/shard_map/ppermute | solution.py:35
  49.8 1.8 %collective-permute-start.25 = (bf16[2,128,128]{2,1,0:T(8,128)(2,1)S(1)}, bf16[2,128,128]{2,1,0:T(8,128)(2,1)S(1)}, u32[]{:S(2)}, u32[]{:S(2)}) collective-permute-start(bf16[2,128,128]{2,1,0:T(8,128)(2,1)S(1)} %get-tuple-element.65), channel_id=1, source_target_pairs={{12,0},{8,4},{4,8},{0,12},{28,16},{24,20},{20,24},{16,28},{13,1},{... | collective-permute-start | bytes 196616 | tf_op jit(solution)/shard_map/ppermute | solution.py:35
  51.6 1.4 %local_backward.1.local_ref = f32[17,128,128]{2,1,0:T(8,128)S(1)} custom-call(s32[1058]{0:T(1024)S(1)} %get-tuple-element.38.plan_ref, bf16[128,128,128]{2,1,0:T(8,128)(2,1)S(1)} %get-tuple-element.40.weight_ref, bf16[9,128,128]{2,1,0:T(8,128)(2,1)S(1)} %get-tuple-element.57.rows_grad), custom_call_target="tpu_custom_call" | custom-call | flops 2147483648 | bytes 1024 | tf_op jit(solution)/shard_map/local_backward/pallas_call | solution.py:438
  52.9 0.7 %rows.1 = bf16[1024,128]{1,0:T(8,128)(2,1)} custom-call(bf16[256,128]{1,0:T(8,128)(2,1)S(1)} %get-tuple-element.52.rest_0_, bf16[256,128]{1,0:T(8,128)(2,1)S(1)} %collective-permute-done.13.rest_1_, bf16[256,128]{1,0:T(8,128)(2,1)S(1)} %collective-permute-done.14.rest_2_, bf16[256,128]{1,0:T(8,128)(2,1)S(1)} %collective-permute-done.15.rest_3_), custom_call_target="tpu_custom_call" | custom-call | tf_op jit(solution)/shard_map/rows/pallas_call | solution.py:448
  53.7 2.1 %collective-permute-done.22.rest_4_ = bf16[2,128,128]{2,1,0:T(8,128)(2,1)S(1)} collective-permute-done((bf16[2,128,128]{2,1,0:T(8,128)(2,1)S(1)}, bf16[2,128,128]{2,1,0:T(8,128)(2,1)S(1)}, u32[]{:S(2)}, u32[]{:S(2)}) %collective-permute-start.22) | collective-permute-done | bytes 65568 | tf_op jit(solution)/shard_map/ppermute | solution.py:35
  55.8 0.6 %collective-permute-done.25.rest_7_ = bf16[2,128,128]{2,1,0:T(8,128)(2,1)S(1)} collective-permute-done((bf16[2,128,128]{2,1,0:T(8,128)(2,1)S(1)}, bf16[2,128,128]{2,1,0:T(8,128)(2,1)S(1)}, u32[]{:S(2)}, u32[]{:S(2)}) %collective-permute-start.25) | collective-permute-done | bytes 65568 | tf_op jit(solution)/shard_map/ppermute | solution.py:35
  56.4 1.7 %final.1 = bf16[128,2048]{1,0:T(8,128)(2,1)} custom-call(s32[2,8]{1,0:T(2,128)S(1)} %bitcast.4, s32[8]{0:T(128)S(1)} %copy-done.5, f32[17,128,128]{2,1,0:T(8,128)S(1)} %local_backward.1.local_ref, bf16[2,128,128]{2,1,0:T(8,128)(2,1)S(1)} %get-tuple-element.58.rest_0_, bf16[2,128,128]{2,1,0:T(8,128)(2,1)S(1)} %collective-permute-done.19.rest_1_, ...), custom_call_target="tpu_custom_call" | custom-call | tf_op jit(solution)/shard_map/final/pallas_call | solution.py:458
  (40 shorter events, 2.6 us)
Async XLA Ops:
  0.6 20.6 %copy-start.1 = (bf16[128,2048]{1,0:T(8,128)(2,1)S(1)}, bf16[128,2048]{1,0:T(8,128)(2,1)}, u32[]{:S(2)}) copy-start(bf16[128,2048]{1,0:T(8,128)(2,1)} %rest_4_) | copy-start | bytes 1572868
  2.0 22.5 %collective-permute-start.11 = (bf16[128,2048]{1,0:T(8,128)(2,1)}, bf16[128,2048]{1,0:T(8,128)(2,1)S(1)}, u32[]{:S(2)}, u32[]{:S(2)}) collective-permute-start(bf16[128,2048]{1,0:T(8,128)(2,1)} %rest_4_), channel_id=1, source_target_pairs={{0,2},{1,3},{2,0},{3,1},{4,6},{5,7},{6,4},{7,5},{8,10},{9,11},{10,... | collective-permute-start | bytes 1572872 | tf_op jit(solution)/shard_map/ppermute | solution.py:31
  5.0 6.1 %collective-permute-start = (bf16[2,128,128]{2,1,0:T(8,128)(2,1)S(1)}, bf16[2,128,128]{2,1,0:T(8,128)(2,1)S(1)}, u32[]{:S(2)}, u32[]{:S(2)}) collective-permute-start(bf16[2,128,128]{2,1,0:T(8,128)(2,1)S(1)} %get-tuple-element.35), channel_id=1, source_target_pairs={{0,4},{4,0},{8,12},{12,8},{16,20},{20,16},{24,28},{28,24},{1,5},{5... | collective-permute-start | bytes 196616 | tf_op jit(solution)/shard_map/ppermute | solution.py:31
  6.5 6.3 %collective-permute-start.1 = (bf16[2,128,128]{2,1,0:T(8,128)(2,1)S(1)}, bf16[2,128,128]{2,1,0:T(8,128)(2,1)S(1)}, u32[]{:S(2)}, u32[]{:S(2)}) collective-permute-start(bf16[2,128,128]{2,1,0:T(8,128)(2,1)S(1)} %get-tuple-element.36), channel_id=1, source_target_pairs={{0,8},{4,12},{8,0},{12,4},{16,24},{20,28},{24,16},{28,20},{1,9},{5... | collective-permute-start | bytes 196616 | tf_op jit(solution)/shard_map/ppermute | solution.py:31
  8.1 7.9 %collective-permute-start.2 = (bf16[2,128,128]{2,1,0:T(8,128)(2,1)S(1)}, bf16[2,128,128]{2,1,0:T(8,128)(2,1)S(1)}, u32[]{:S(2)}, u32[]{:S(2)}) collective-permute-start(bf16[2,128,128]{2,1,0:T(8,128)(2,1)S(1)} %get-tuple-element.37), channel_id=1, source_target_pairs={{0,12},{4,8},{8,4},{12,0},{16,28},{20,24},{24,20},{28,16},{1,13},{... | collective-permute-start | bytes 196616 | tf_op jit(solution)/shard_map/ppermute | solution.py:31
  8.5 12.8 %collective-permute-start.3 = (bf16[2,128,128]{2,1,0:T(8,128)(2,1)S(1)}, bf16[2,128,128]{2,1,0:T(8,128)(2,1)S(1)}, u32[]{:S(2)}, u32[]{:S(2)}) collective-permute-start(bf16[2,128,128]{2,1,0:T(8,128)(2,1)S(1)} %get-tuple-element.41), channel_id=1, source_target_pairs={{0,16},{4,20},{8,24},{12,28},{16,0},{20,4},{24,8},{28,12},{1,17},{... | collective-permute-start | bytes 196616 | tf_op jit(solution)/shard_map/ppermute | solution.py:31
  11.1 10.3 %collective-permute-start.4 = (bf16[2,128,128]{2,1,0:T(8,128)(2,1)S(1)}, bf16[2,128,128]{2,1,0:T(8,128)(2,1)S(1)}, u32[]{:S(2)}, u32[]{:S(2)}) collective-permute-start(bf16[2,128,128]{2,1,0:T(8,128)(2,1)S(1)} %get-tuple-element.42), channel_id=1, source_target_pairs={{0,20},{4,16},{8,28},{12,24},{16,4},{20,0},{24,12},{28,8},{1,21},{... | collective-permute-start | bytes 196616 | tf_op jit(solution)/shard_map/ppermute | solution.py:31
  12.8 8.6 %collective-permute-start.5 = (bf16[2,128,128]{2,1,0:T(8,128)(2,1)S(1)}, bf16[2,128,128]{2,1,0:T(8,128)(2,1)S(1)}, u32[]{:S(2)}, u32[]{:S(2)}) collective-permute-start(bf16[2,128,128]{2,1,0:T(8,128)(2,1)S(1)} %get-tuple-element.43), channel_id=1, source_target_pairs={{0,24},{4,28},{8,16},{12,20},{16,8},{20,12},{24,0},{28,4},{1,25},{... | collective-permute-start | bytes 196616 | tf_op jit(solution)/shard_map/ppermute | solution.py:31
  15.9 7.1 %collective-permute-start.6 = (bf16[2,128,128]{2,1,0:T(8,128)(2,1)S(1)}, bf16[2,128,128]{2,1,0:T(8,128)(2,1)S(1)}, u32[]{:S(2)}, u32[]{:S(2)}) collective-permute-start(bf16[2,128,128]{2,1,0:T(8,128)(2,1)S(1)} %get-tuple-element.44), channel_id=1, source_target_pairs={{0,28},{4,24},{8,20},{12,16},{16,12},{20,8},{24,4},{28,0},{1,29},{... | collective-permute-start | bytes 196616 | tf_op jit(solution)/shard_map/ppermute | solution.py:31
  21.2 8.7 %copy-start = (bf16[2048,128]{1,0:T(8,128)(2,1)S(1)}, bf16[2048,128]{1,0:T(8,128)(2,1)}, u32[]{:S(2)}) copy-start(bf16[2048,128]{1,0:T(8,128)(2,1)} %w_out_ref.1) | copy-start | bytes 1572868
  21.2 8.7 %copy-start.2 = (bf16[1024,128]{1,0:T(8,128)(2,1)S(1)}, bf16[1024,128]{1,0:T(8,128)(2,1)}, u32[]{:S(2)}) copy-start(bf16[1024,128]{1,0:T(8,128)(2,1)} %g_ref.1) | copy-start | bytes 786436
  21.2 8.7 %copy-start.3 = (f32[2048]{0:T(1024)S(1)}, f32[2048]{0:T(1024)}, u32[]{:S(2)}) copy-start(f32[2048]{0:T(1024)} %param.17) | copy-start | bytes 24580
  21.3 8.7 %collective-permute-start.10 = (bf16[128,2048]{1,0:T(8,128)(2,1)S(1)}, bf16[128,2048]{1,0:T(8,128)(2,1)S(1)}, u32[]{:S(2)}, u32[]{:S(2)}) collective-permute-start(bf16[128,2048]{1,0:T(8,128)(2,1)S(1)} %copy-done.1), channel_id=1, source_target_pairs={{0,1},{1,0},{2,3},{3,2},{4,5},{5,4},{6,7},{7,6},{8,9},{9,8},{10,11... | collective-permute-start | bytes 1572872 | tf_op jit(solution)/shard_map/ppermute | solution.py:31
  24.5 5.5 %collective-permute-start.12 = (bf16[128,2048]{1,0:T(8,128)(2,1)S(1)}, bf16[128,2048]{1,0:T(8,128)(2,1)S(1)}, u32[]{:S(2)}, u32[]{:S(2)}) collective-permute-start(bf16[128,2048]{1,0:T(8,128)(2,1)S(1)} %collective-permute-done.11.rest_6_), channel_id=1, source_target_pairs={{0,1},{1,0},{2,3},{3,2},{4,5},{5,4},{6,7},{7,6},{8,9},{9,8},{10,11... | collective-permute-start | bytes 1572872 | tf_op jit(solution)/shard_map/ppermute | solution.py:31
  24.6 2.0 %collective-permute-start.7 = (bf16[256,128]{1,0:T(8,128)(2,1)S(1)}, bf16[256,128]{1,0:T(8,128)(2,1)S(1)}, u32[]{:S(2)}, u32[]{:S(2)}) collective-permute-start(bf16[256,128]{1,0:T(8,128)(2,1)S(1)} %get-tuple-element.46), channel_id=1, source_target_pairs={{0,1},{1,0},{2,3},{3,2},{4,5},{5,4},{6,7},{7,6},{8,9},{9,8},{10,11... | collective-permute-start | bytes 196616 | tf_op jit(solution)/shard_map/ppermute | solution.py:31
  25.0 4.9 %collective-permute-start.8 = (bf16[256,128]{1,0:T(8,128)(2,1)S(1)}, bf16[256,128]{1,0:T(8,128)(2,1)S(1)}, u32[]{:S(2)}, u32[]{:S(2)}) collective-permute-start(bf16[256,128]{1,0:T(8,128)(2,1)S(1)} %get-tuple-element.47), channel_id=1, source_target_pairs={{0,2},{1,3},{2,0},{3,1},{4,6},{5,7},{6,4},{7,5},{8,10},{9,11},{10,... | collective-permute-start | bytes 196616 | tf_op jit(solution)/shard_map/ppermute | solution.py:31
  25.6 4.4 %collective-permute-start.9 = (bf16[256,128]{1,0:T(8,128)(2,1)S(1)}, bf16[256,128]{1,0:T(8,128)(2,1)S(1)}, u32[]{:S(2)}, u32[]{:S(2)}) collective-permute-start(bf16[256,128]{1,0:T(8,128)(2,1)S(1)} %get-tuple-element.48), channel_id=1, source_target_pairs={{0,3},{1,2},{2,1},{3,0},{4,7},{5,6},{6,5},{7,4},{8,11},{9,10},{10,... | collective-permute-start | bytes 196616 | tf_op jit(solution)/shard_map/ppermute | solution.py:31
  32.2 3.8 %collective-permute-start.16 = (bf16[128,256]{1,0:T(8,128)(2,1)S(1)}, bf16[128,256]{1,0:T(8,128)(2,1)S(1)}, u32[]{:S(2)}, u32[]{:S(2)}) collective-permute-start(bf16[128,256]{1,0:T(8,128)(2,1)S(1)} %get-tuple-element.54), channel_id=1, source_target_pairs={{1,0},{0,1},{3,2},{2,3},{5,4},{4,5},{7,6},{6,7},{9,8},{8,9},{11,10... | collective-permute-start | bytes 196616 | tf_op jit(solution)/shard_map/ppermute | solution.py:35
  32.7 4.5 %collective-permute-start.17 = (bf16[128,256]{1,0:T(8,128)(2,1)S(1)}, bf16[128,256]{1,0:T(8,128)(2,1)S(1)}, u32[]{:S(2)}, u32[]{:S(2)}) collective-permute-start(bf16[128,256]{1,0:T(8,128)(2,1)S(1)} %get-tuple-element.55), channel_id=1, source_target_pairs={{2,0},{3,1},{0,2},{1,3},{6,4},{7,5},{4,6},{5,7},{10,8},{11,9},{8,1... | collective-permute-start | bytes 196616 | tf_op jit(solution)/shard_map/ppermute | solution.py:35
  33.8 4.3 %collective-permute-start.18 = (bf16[128,256]{1,0:T(8,128)(2,1)S(1)}, bf16[128,256]{1,0:T(8,128)(2,1)S(1)}, u32[]{:S(2)}, u32[]{:S(2)}) collective-permute-start(bf16[128,256]{1,0:T(8,128)(2,1)S(1)} %get-tuple-element.56), channel_id=1, source_target_pairs={{3,0},{2,1},{1,2},{0,3},{7,4},{6,5},{5,6},{4,7},{11,8},{10,9},{9,1... | collective-permute-start | bytes 196616 | tf_op jit(solution)/shard_map/ppermute | solution.py:35
  34.2 9.4 %collective-permute-start.13 = (bf16[256,128]{1,0:T(8,128)(2,1)S(1)}, bf16[256,128]{1,0:T(8,128)(2,1)S(1)}, u32[]{:S(2)}, u32[]{:S(2)}) collective-permute-start(bf16[256,128]{1,0:T(8,128)(2,1)S(1)} %get-tuple-element.52.rest_0_), channel_id=1, source_target_pairs={{0,1},{1,0},{2,3},{3,2},{4,5},{5,4},{6,7},{7,6},{8,9},{9,8},{10,11... | collective-permute-start | bytes 196616 | tf_op jit(solution)/shard_map/ppermute | solution.py:31
  34.9 10.5 %collective-permute-start.14 = (bf16[256,128]{1,0:T(8,128)(2,1)S(1)}, bf16[256,128]{1,0:T(8,128)(2,1)S(1)}, u32[]{:S(2)}, u32[]{:S(2)}) collective-permute-start(bf16[256,128]{1,0:T(8,128)(2,1)S(1)} %get-tuple-element.52.rest_0_), channel_id=1, source_target_pairs={{0,2},{1,3},{2,0},{3,1},{4,6},{5,7},{6,4},{7,5},{8,10},{9,11},{10,... | collective-permute-start | bytes 196616 | tf_op jit(solution)/shard_map/ppermute | solution.py:31
  36.0 9.6 %collective-permute-start.15 = (bf16[256,128]{1,0:T(8,128)(2,1)S(1)}, bf16[256,128]{1,0:T(8,128)(2,1)S(1)}, u32[]{:S(2)}, u32[]{:S(2)}) collective-permute-start(bf16[256,128]{1,0:T(8,128)(2,1)S(1)} %get-tuple-element.52.rest_0_), channel_id=1, source_target_pairs={{0,3},{1,2},{2,1},{3,0},{4,7},{5,6},{6,5},{7,4},{8,11},{9,10},{10,... | collective-permute-start | bytes 196616 | tf_op jit(solution)/shard_map/ppermute | solution.py:31
  40.3 7.9 %collective-permute-start.19 = (bf16[2,128,128]{2,1,0:T(8,128)(2,1)S(1)}, bf16[2,128,128]{2,1,0:T(8,128)(2,1)S(1)}, u32[]{:S(2)}, u32[]{:S(2)}) collective-permute-start(bf16[2,128,128]{2,1,0:T(8,128)(2,1)S(1)} %get-tuple-element.59), channel_id=1, source_target_pairs={{4,0},{0,4},{12,8},{8,12},{20,16},{16,20},{28,24},{24,28},{5,1},{1... | collective-permute-start | bytes 196616 | tf_op jit(solution)/shard_map/ppermute | solution.py:35
  40.9 8.8 %collective-permute-start.20 = (bf16[2,128,128]{2,1,0:T(8,128)(2,1)S(1)}, bf16[2,128,128]{2,1,0:T(8,128)(2,1)S(1)}, u32[]{:S(2)}, u32[]{:S(2)}) collective-permute-start(bf16[2,128,128]{2,1,0:T(8,128)(2,1)S(1)} %get-tuple-element.60), channel_id=1, source_target_pairs={{16,0},{20,4},{24,8},{28,12},{0,16},{4,20},{8,24},{12,28},{17,1},{... | collective-permute-start | bytes 196616 | tf_op jit(solution)/shard_map/ppermute | solution.py:35
  43.5 10.1 %collective-permute-start.21 = (bf16[2,128,128]{2,1,0:T(8,128)(2,1)S(1)}, bf16[2,128,128]{2,1,0:T(8,128)(2,1)S(1)}, u32[]{:S(2)}, u32[]{:S(2)}) collective-permute-start(bf16[2,128,128]{2,1,0:T(8,128)(2,1)S(1)} %get-tuple-element.61), channel_id=1, source_target_pairs={{24,0},{28,4},{16,8},{20,12},{8,16},{12,20},{0,24},{4,28},{25,1},{... | collective-permute-start | bytes 196616 | tf_op jit(solution)/shard_map/ppermute | solution.py:35
  45.4 10.4 %collective-permute-start.22 = (bf16[2,128,128]{2,1,0:T(8,128)(2,1)S(1)}, bf16[2,128,128]{2,1,0:T(8,128)(2,1)S(1)}, u32[]{:S(2)}, u32[]{:S(2)}) collective-permute-start(bf16[2,128,128]{2,1,0:T(8,128)(2,1)S(1)} %get-tuple-element.62), channel_id=1, source_target_pairs={{20,0},{16,4},{28,8},{24,12},{4,16},{0,20},{12,24},{8,28},{21,1},{... | collective-permute-start | bytes 196616 | tf_op jit(solution)/shard_map/ppermute | solution.py:35
  45.6 10.2 %collective-permute-start.23 = (bf16[2,128,128]{2,1,0:T(8,128)(2,1)S(1)}, bf16[2,128,128]{2,1,0:T(8,128)(2,1)S(1)}, u32[]{:S(2)}, u32[]{:S(2)}) collective-permute-start(bf16[2,128,128]{2,1,0:T(8,128)(2,1)S(1)} %get-tuple-element.63), channel_id=1, source_target_pairs={{28,0},{24,4},{20,8},{16,12},{12,16},{8,20},{4,24},{0,28},{29,1},{... | collective-permute-start | bytes 196616 | tf_op jit(solution)/shard_map/ppermute | solution.py:35
  48.2 7.6 %collective-permute-start.24 = (bf16[2,128,128]{2,1,0:T(8,128)(2,1)S(1)}, bf16[2,128,128]{2,1,0:T(8,128)(2,1)S(1)}, u32[]{:S(2)}, u32[]{:S(2)}) collective-permute-start(bf16[2,128,128]{2,1,0:T(8,128)(2,1)S(1)} %get-tuple-element.64), channel_id=1, source_target_pairs={{8,0},{12,4},{0,8},{4,12},{24,16},{28,20},{16,24},{20,28},{9,1},{1... | collective-permute-start | bytes 196616 | tf_op jit(solution)/shard_map/ppermute | solution.py:35
  49.8 6.6 %collective-permute-start.25 = (bf16[2,128,128]{2,1,0:T(8,128)(2,1)S(1)}, bf16[2,128,128]{2,1,0:T(8,128)(2,1)S(1)}, u32[]{:S(2)}, u32[]{:S(2)}) collective-permute-start(bf16[2,128,128]{2,1,0:T(8,128)(2,1)S(1)} %get-tuple-element.65), channel_id=1, source_target_pairs={{12,0},{8,4},{4,8},{0,12},{28,16},{24,20},{20,24},{16,28},{13,1},{... | collective-permute-start | bytes 196616 | tf_op jit(solution)/shard_map/ppermute | solution.py:35
  51.6 4.8 %copy-start.4 = (s32[8,2]{0,1:T(2,128)S(1)}, s32[8,2]{0,1:T(2,128)}, u32[]{:S(2)}) copy-start(s32[8,2]{0,1:T(2,128)} %param.12) | copy-start | bytes 196
  51.6 4.8 %copy-start.5 = (s32[8]{0:T(128)S(1)}, s32[8]{0:T(128)}, u32[]{:S(2)}) copy-start(s32[8]{0:T(128)} %counts_ref.1) | copy-start | bytes 100
